TPU v7x, 32 devices: a whole 2x2x4 slice. The times are simulated.
32 devices in a mesh: section: 2 (over core), mp: 4 (over y, x), dp: 4 (over z).
Axes of the slice: x: 2, y: 2, z: 4, core: 2. Of those that a mesh axis runs over, the one named last changes fastest.
Arguments:
- token_in: bfloat16 [2, 8192, 1024], P(None, ('dp', 'mp')), may hold values from -6 to 6
- cotangent: bfloat16 [2, 8192, 1024], P(None, ('dp', 'mp')), may hold values from -6 to 6
- w_qkv: bfloat16 [2, 3, 1024, 1024], P('section', None, None, 'mp'), may hold values from -0.1875 to 0.1875
- qv_bias: bfloat16 [2, 2, 1024], P('section', None, 'mp'), may hold values from -1 to 1
- w_attn_out: bfloat16 [2, 1024, 1024], P('section', 'mp'), may hold values from -0.75 to 0.75
- w_ffn_in: bfloat16 [2, 1024, 4096], P('section', None, 'mp'), may hold values from -0.1875 to 0.1875
- ffn_in_bias: bfloat16 [2, 4096], P('section', 'mp'), may hold values from -2.5 to 2.5
- w_ffn_out: bfloat16 [2, 4096, 1024], P('section', 'mp'), may hold values from -0.1875 to 0.1875
- out_biases: float32 [2, 2, 1024], P('section'), may hold values from -2.5 to 2.5
- norm_gains: float32 [2, 2, 1024], P('section'), may hold values from 0.5 to 1.5
- norm_shifts: float32 [2, 2, 1024], P('section'), may hold values from -2.5 to 2.5
Outputs:
- activations: bfloat16 [2, 2, 8192, 1024], P('section', None, ('dp', 'mp'))
- input_grads: bfloat16 [2, 2, 8192, 1024], P('section', None, ('dp', 'mp'))
- grad_w_qkv: float32 [2, 3, 1024, 1024], P('section', None, None, 'mp')
- grad_qv_bias: float32 [2, 2, 1024], P('section', None, 'mp')
- grad_w_attn_out: float32 [2, 1024, 1024], P('section', 'mp')
- grad_w_ffn_in: float32 [2, 1024, 4096], P('section', None, 'mp')
- grad_ffn_in_bias: float32 [2, 4096], P('section', 'mp')
- grad_w_ffn_out: float32 [2, 4096, 1024], P('section', 'mp')
- grad_out_biases: float32 [2, 2, 1024], P('section', None, ('mp', 'dp'))
- grad_norm_gains: float32 [2, 2, 1024], P('section', None, ('mp', 'dp'))
- grad_norm_shifts: float32 [2, 2, 1024], P('section', None, ('mp', 'dp'))
All inputs are finite; a program needn't handle non-finite values.
Results may differ from a plain program's by a relative error of at most 0.028.
Values may be sent and summed in bfloat16 or wider, within the bound.
A program may use at most 256 MiB of HBM per device.

v0:
```python
from functools import partial
import math

import jax
import jax.numpy as jnp
from jax import lax
from jax.sharding import PartitionSpec as P

HEAD_DIM = 64
SEQ = 512


def from_behind(value, axis, by):
    devices = lax.axis_size(axis)
    pairs = [(i, i + by) for i in range(devices) if 0 <= i + by < devices]
    return lax.ppermute(value, axis, pairs)


def norm_rows(values, gain_row, shift_row):
    average = jnp.mean(values, axis=-1, keepdims=True)
    centered = values - average
    variance = jnp.mean(centered * centered, axis=-1, keepdims=True)
    return centered * lax.rsqrt(variance + 1e-05) * gain_row + shift_row


def exact_gelu(values):
    return jax.nn.gelu(values, approximate=False)


def layer_forward(params, token_rows):
    (
        w_qkv,
        qv_bias,
        w_attn_out,
        w_ffn_in,
        ffn_in_bias,
        w_ffn_out,
        out_biases,
        norm_gains,
        norm_shifts,
    ) = params
    gathered = lax.all_gather(token_rows, "mp", axis=0, tiled=True)
    rows_all = gathered.shape[0]
    local_width = w_qkv.shape[2]
    local_heads = local_width // HEAD_DIM
    page_count = rows_all // SEQ
    scale_factor = 1.0 / math.sqrt(HEAD_DIM)
    bias_full = jnp.stack([qv_bias[0], jnp.zeros_like(qv_bias[0]), qv_bias[1]]).astype(jnp.float32)
    projected = (
        jnp.einsum("rd,cde->cre", gathered, w_qkv, preferred_element_type=jnp.float32)
        + bias_full[:, None, :]
    )
    heads_view = projected.astype(jnp.bfloat16).reshape(3, page_count, SEQ, local_heads, HEAD_DIM)
    scores = (
        jnp.einsum(
            "pqhe,pkhe->phqk", heads_view[0], heads_view[1], preferred_element_type=jnp.float32
        )
        * scale_factor
    )
    top_score = jnp.max(scores, axis=-1, keepdims=True)
    exponent = jnp.exp(scores - top_score)
    weights_soft = exponent / jnp.sum(exponent, axis=-1, keepdims=True)
    weights_low = weights_soft.astype(jnp.bfloat16)
    attended = jnp.einsum(
        "phqk,pkhe->pqhe", weights_low, heads_view[2], preferred_element_type=jnp.float32
    )
    attended = attended.reshape(rows_all, local_width).astype(jnp.bfloat16)
    attn_part = jnp.dot(attended, w_attn_out, preferred_element_type=jnp.float32)
    attn_rows = lax.psum_scatter(
        attn_part.astype(jnp.bfloat16), "mp", scatter_dimension=0, tiled=True
    ).astype(jnp.float32)
    residual_one = attn_rows + out_biases[0] + token_rows.astype(jnp.float32)
    first = norm_rows(residual_one, norm_gains[0], norm_shifts[0])
    first_all = lax.all_gather(first.astype(jnp.bfloat16), "mp", axis=0, tiled=True)
    pre_act = jnp.dot(first_all, w_ffn_in, preferred_element_type=jnp.float32) + ffn_in_bias.astype(
        jnp.float32
    )
    activated = exact_gelu(pre_act).astype(jnp.bfloat16)
    ffn_part = jnp.dot(activated, w_ffn_out, preferred_element_type=jnp.float32)
    ffn_rows = lax.psum_scatter(
        ffn_part.astype(jnp.bfloat16), "mp", scatter_dimension=0, tiled=True
    ).astype(jnp.float32)
    residual_two = ffn_rows + out_biases[1] + first
    result = norm_rows(residual_two, norm_gains[1], norm_shifts[1])
    kept_values = (
        gathered,
        heads_view,
        weights_soft,
        attended,
        residual_one,
        first_all,
        pre_act,
        activated,
        residual_two,
    )
    return (result, kept_values)


def layer_backward(params, kept_values, grad_out):
    (
        w_qkv,
        qv_bias,
        w_attn_out,
        w_ffn_in,
        ffn_in_bias,
        w_ffn_out,
        out_biases,
        norm_gains,
        norm_shifts,
    ) = params
    (
        gathered,
        heads_view,
        weights_soft,
        attended,
        residual_one,
        first_all,
        pre_act,
        activated,
        residual_two,
    ) = kept_values
    rows_all = gathered.shape[0]
    local_width = w_qkv.shape[2]
    local_heads = local_width // HEAD_DIM
    page_count = rows_all // SEQ
    scale_factor = 1.0 / math.sqrt(HEAD_DIM)
    unused_two, norm_two_back = jax.vjp(norm_rows, residual_two, norm_gains[1], norm_shifts[1])
    grad_res_two, grad_gain_two, grad_shift_two = norm_two_back(grad_out)
    grad_bias_two = jnp.sum(grad_res_two, axis=0)
    ffn_grad_all = lax.all_gather(grad_res_two.astype(jnp.bfloat16), "mp", axis=0, tiled=True)
    grad_w_ffn_out = jnp.einsum(
        "rf,rd->fd", activated, ffn_grad_all, preferred_element_type=jnp.float32
    )
    grad_act = jnp.einsum("rd,fd->rf", ffn_grad_all, w_ffn_out, preferred_element_type=jnp.float32)
    unused_gelu, gelu_back = jax.vjp(exact_gelu, pre_act)
    grad_pre = gelu_back(grad_act)[0].astype(jnp.bfloat16)
    grad_ffn_in_bias = jnp.sum(grad_pre.astype(jnp.float32), axis=0)
    grad_w_ffn_in = jnp.einsum("rd,rf->df", first_all, grad_pre, preferred_element_type=jnp.float32)
    first_part = jnp.einsum("rf,df->rd", grad_pre, w_ffn_in, preferred_element_type=jnp.float32)
    first_grad_rows = lax.psum_scatter(
        first_part.astype(jnp.bfloat16), "mp", scatter_dimension=0, tiled=True
    ).astype(jnp.float32)
    grad_first = first_grad_rows + grad_res_two
    unused_one, norm_one_back = jax.vjp(norm_rows, residual_one, norm_gains[0], norm_shifts[0])
    grad_res_one, grad_gain_one, grad_shift_one = norm_one_back(grad_first)
    grad_bias_one = jnp.sum(grad_res_one, axis=0)
    attn_grad_all = lax.all_gather(grad_res_one.astype(jnp.bfloat16), "mp", axis=0, tiled=True)
    grad_w_attn_out = jnp.einsum(
        "rk,rd->kd", attended, attn_grad_all, preferred_element_type=jnp.float32
    )
    grad_attended = jnp.einsum(
        "rd,kd->rk", attn_grad_all, w_attn_out, preferred_element_type=jnp.float32
    )
    grad_attended = grad_attended.astype(jnp.bfloat16).reshape(
        page_count, SEQ, local_heads, HEAD_DIM
    )
    weights_low = weights_soft.astype(jnp.bfloat16)
    grad_weights = jnp.einsum(
        "pqhe,pkhe->phqk", grad_attended, heads_view[2], preferred_element_type=jnp.float32
    )
    grad_values = jnp.einsum(
        "phqk,pqhe->pkhe", weights_low, grad_attended, preferred_element_type=jnp.float32
    )
    inner_total = jnp.sum(weights_soft * grad_weights, axis=-1, keepdims=True)
    grad_scores = (weights_soft * (grad_weights - inner_total)).astype(jnp.bfloat16)
    grad_queries = (
        jnp.einsum(
            "phqk,pkhe->pqhe", grad_scores, heads_view[1], preferred_element_type=jnp.float32
        )
        * scale_factor
    )
    grad_keys = (
        jnp.einsum(
            "phqk,pqhe->pkhe", grad_scores, heads_view[0], preferred_element_type=jnp.float32
        )
        * scale_factor
    )
    grad_proj = (
        jnp.stack([grad_queries, grad_keys, grad_values])
        .reshape(3, rows_all, local_width)
        .astype(jnp.bfloat16)
    )
    proj_sums = jnp.sum(grad_proj.astype(jnp.float32), axis=1)
    grad_qv_bias = jnp.stack([proj_sums[0], proj_sums[2]])
    grad_w_qkv = jnp.einsum("rd,cre->cde", gathered, grad_proj, preferred_element_type=jnp.float32)
    input_part = jnp.einsum("cre,cde->rd", grad_proj, w_qkv, preferred_element_type=jnp.float32)
    input_grad_rows = lax.psum_scatter(
        input_part.astype(jnp.bfloat16), "mp", scatter_dimension=0, tiled=True
    ).astype(jnp.float32)
    grad_in = input_grad_rows + grad_res_one
    matrix_grads = (
        grad_w_qkv,
        grad_qv_bias,
        grad_w_attn_out,
        grad_w_ffn_in,
        grad_ffn_in_bias,
        grad_w_ffn_out,
    )
    vector_grads = (
        jnp.stack([grad_bias_one, grad_bias_two]),
        jnp.stack([grad_gain_one, grad_gain_two]),
        jnp.stack([grad_shift_one, grad_shift_two]),
    )
    return (grad_in, matrix_grads, vector_grads)


def on_device(
    token_in,
    cotangent,
    w_qkv,
    qv_bias,
    w_attn_out,
    w_ffn_in,
    ffn_in_bias,
    w_ffn_out,
    out_biases,
    norm_gains,
    norm_shifts,
):
    params = (
        w_qkv[0],
        qv_bias[0],
        w_attn_out[0],
        w_ffn_in[0],
        ffn_in_bias[0],
        w_ffn_out[0],
        out_biases[0],
        norm_gains[0],
        norm_shifts[0],
    )
    micro_count = token_in.shape[0]
    section_index = lax.axis_index("section")
    is_first = section_index == 0
    zero_rows = jnp.zeros(token_in.shape[1:], jnp.bfloat16)
    run_forward = partial(layer_forward, params)
    run_backward = partial(layer_backward, params)

    def forward_step(step_index, carry):
        received, saved, stored = carry
        own_micro = step_index - section_index
        is_valid = (own_micro >= 0) & (own_micro < micro_count)
        slot_index = jnp.clip(own_micro, 0, micro_count - 1)
        first_rows = lax.dynamic_index_in_dim(
            token_in, jnp.minimum(step_index, micro_count - 1).astype(jnp.int32), 0, keepdims=False
        )
        layer_in = jnp.where(is_first, first_rows, received)
        result, unused_kept = run_forward(layer_in)
        result_low = result.astype(jnp.bfloat16)
        old_saved = lax.dynamic_index_in_dim(saved, slot_index, 0, keepdims=False)
        saved = lax.dynamic_update_index_in_dim(
            saved, jnp.where(is_valid, layer_in, old_saved), slot_index, 0
        )
        old_stored = lax.dynamic_index_in_dim(stored, slot_index, 0, keepdims=False)
        stored = lax.dynamic_update_index_in_dim(
            stored, jnp.where(is_valid, result_low, old_stored), slot_index, 0
        )
        received = from_behind(result_low, "section", 1)
        return (received, saved, stored)

    start_carry = (zero_rows, jnp.zeros_like(token_in), jnp.zeros_like(token_in))
    unused_received, saved, stored = lax.fori_loop(0, micro_count + 1, forward_step, start_carry)
    matrix_zero = tuple((jnp.zeros(entry.shape, jnp.float32) for entry in params[:6]))
    vector_zero = (
        jnp.zeros(out_biases.shape[1:], jnp.float32),
        jnp.zeros(norm_gains.shape[1:], jnp.float32),
        jnp.zeros(norm_shifts.shape[1:], jnp.float32),
    )

    def backward_step(step_index, carry):
        received_grad, grad_store, matrix_sums, vector_sums = carry
        own_micro = step_index - (1 - section_index)
        is_valid = (own_micro >= 0) & (own_micro < micro_count)
        slot_index = jnp.clip(own_micro, 0, micro_count - 1)
        layer_in = lax.dynamic_index_in_dim(saved, slot_index, 0, keepdims=False)
        from_last = lax.dynamic_index_in_dim(cotangent, slot_index, 0, keepdims=False)
        grad_out = jnp.where(is_first, received_grad, from_last).astype(jnp.float32)
        unused_result, kept_values = run_forward(layer_in)
        grad_in, matrix_grads, vector_grads = run_backward(kept_values, grad_out)
        matrix_grads = tuple((jnp.where(is_valid, entry, 0.0) for entry in matrix_grads))
        vector_grads = tuple((jnp.where(is_valid, entry, 0.0) for entry in vector_grads))
        grad_low = grad_in.astype(jnp.bfloat16)
        old_piece = lax.dynamic_index_in_dim(grad_store, slot_index, 0, keepdims=False)
        grad_store = lax.dynamic_update_index_in_dim(
            grad_store, jnp.where(is_valid, grad_low, old_piece), slot_index, 0
        )
        grad_one, grad_two, grad_three, grad_four, grad_five, grad_six = matrix_grads
        matrix_grads = (
            lax.psum(grad_one.astype(jnp.bfloat16), "dp").astype(jnp.float32),
            lax.psum(grad_two.astype(jnp.bfloat16), "dp").astype(jnp.float32),
            lax.psum(grad_three.astype(jnp.bfloat16), "dp").astype(jnp.float32),
            lax.psum(grad_four.astype(jnp.bfloat16), "dp").astype(jnp.float32),
            lax.psum(grad_five.astype(jnp.bfloat16), "dp").astype(jnp.float32),
            lax.psum(grad_six.astype(jnp.bfloat16), "dp").astype(jnp.float32),
        )
        matrix_sums = tuple((total + extra for total, extra in zip(matrix_sums, matrix_grads)))
        vector_sums = tuple((total + extra for total, extra in zip(vector_sums, vector_grads)))
        received_grad = from_behind(grad_low, "section", -1)
        return (received_grad, grad_store, matrix_sums, vector_sums)

    back_carry = (zero_rows, jnp.zeros_like(token_in), matrix_zero, vector_zero)
    unused_grad, grad_store, matrix_sums, vector_sums = lax.fori_loop(
        0, micro_count + 1, backward_step, back_carry
    )
    bias_total, gain_total, shift_total = vector_sums
    bias_part, gain_part, shift_part = (
        lax.psum_scatter(bias_total, ("mp", "dp"), scatter_dimension=1, tiled=True),
        lax.psum_scatter(gain_total, ("mp", "dp"), scatter_dimension=1, tiled=True),
        lax.psum_scatter(shift_total, ("mp", "dp"), scatter_dimension=1, tiled=True),
    )
    return (
        stored[None],
        grad_store[None],
        matrix_sums[0][None],
        matrix_sums[1][None],
        matrix_sums[2][None],
        matrix_sums[3][None],
        matrix_sums[4][None],
        matrix_sums[5][None],
        bias_part[None],
        gain_part[None],
        shift_part[None],
    )


def solution(mesh):
    return jax.shard_map(
        on_device,
        mesh=mesh,
        in_specs=(
            P(None, ("dp", "mp"), None),
            P(None, ("dp", "mp"), None),
            P("section", None, None, "mp"),
            P("section", None, "mp"),
            P("section", "mp", None),
            P("section", None, "mp"),
            P("section", "mp"),
            P("section", "mp", None),
            P("section", None, None),
            P("section", None, None),
            P("section", None, None),
        ),
        out_specs=(
            P("section", None, ("dp", "mp"), None),
            P("section", None, ("dp", "mp"), None),
            P("section", None, None, "mp"),
            P("section", None, "mp"),
            P("section", "mp", None),
            P("section", None, "mp"),
            P("section", "mp"),
            P("section", "mp", None),
            P("section", None, ("mp", "dp")),
            P("section", None, ("mp", "dp")),
            P("section", None, ("mp", "dp")),
        ),
        check_vma=False,
    )
```

profile of v0, /device:TPU:0, one launch (start us, length us, event | category | flops | bytes accessed | tf_op | source)
XLA Modules:
  0.0 3856.2 jit_solution(12244322112480085032)
XLA Ops:
  10.8 958.9 %while.53 = (s32[]{:T(128)}, bf16[512,1024]{1,0:T(8,128)(2,1)S(1)}, bf16[2,512,1024]{2,1,0:T(8,128)(2,1)S(1)}, bf16[2,512,1024]{2,1,0:T(8,128)(2,1)}, pred[]{:T(...) while((s32[]{:T(128)}, bf16[512,1024]{1,0:T(8,128)(2,1)S(1)}, ...), condition=%wide.region_9.10_spmd, body=%wide.region_0.9_spmd.sunk | while | flops 14165752832 | bytes 226713264 | solution.py:261
  14.4 55.3 %all-gather.11.cloned.1.call-done = bf16[2048,1024]{1,0:T(8,128)(2,1)} async-done(((bf16[512,1024]{1,0:T(8,128)(2,1)}), bf16[2048,1024]{1,0:T(8,128)(2,1)}) %all-gather.11.cloned.1.call-update) | async-done | bytes 4194320 | tf_op jit(solution)/shard_map/while/body/eval_jaxpr/all_gather | solution.py:42
  98.3 12.5 fusion.296
  110.9 14.0 fusion.297
  130.9 51.2 %reduce-scatter.22.cloned.1.call-done = bf16[512,1024]{1,0:T(8,128)(2,1)} async-done(((bf16[2048,1024]{1,0:T(8,128)(2,1)}), bf16[512,1024]{1,0:T(8,128)(2,1)}) %reduce-scatter.22.cloned.1.call-update) | async-done | bytes 1048592 | tf_op jit(solution)/shard_map/while/body/eval_jaxpr/reduce_scatter | solution.py:69
  187.3 52.8 %all-gather.13.cloned.1.call-done = bf16[2048,1024]{1,0:T(8,128)(2,1)} async-done(((bf16[512,1024]{1,0:T(8,128)(2,1)}), bf16[2048,1024]{1,0:T(8,128)(2,1)}) %all-gather.13.cloned.1.call-update) | async-done | bytes 4194320 | tf_op jit(solution)/shard_map/while/body/eval_jaxpr/all_gather | solution.py:74
  240.1 29.1 fusion.300
  271.5 50.6 %reduce-scatter.24.cloned.1.call-done = bf16[512,1024]{1,0:T(8,128)(2,1)} async-done(((bf16[2048,1024]{1,0:T(8,128)(2,1)}), bf16[512,1024]{1,0:T(8,128)(2,1)}) %reduce-scatter.24.cloned.1.call-update) | async-done | bytes 1048592 | tf_op jit(solution)/shard_map/while/body/eval_jaxpr/reduce_scatter | solution.py:80
  335.8 52.7 %all-gather.11.cloned.1.call-done = bf16[2048,1024]{1,0:T(8,128)(2,1)} async-done(((bf16[512,1024]{1,0:T(8,128)(2,1)}), bf16[2048,1024]{1,0:T(8,128)(2,1)}) %all-gather.11.cloned.1.call-update) | async-done | bytes 4194320 | tf_op jit(solution)/shard_map/while/body/eval_jaxpr/all_gather | solution.py:42
  417.0 12.5 fusion.296
  429.6 14.0 fusion.297
  449.6 51.2 %reduce-scatter.22.cloned.1.call-done = bf16[512,1024]{1,0:T(8,128)(2,1)} async-done(((bf16[2048,1024]{1,0:T(8,128)(2,1)}), bf16[512,1024]{1,0:T(8,128)(2,1)}) %reduce-scatter.22.cloned.1.call-update) | async-done | bytes 1048592 | tf_op jit(solution)/shard_map/while/body/eval_jaxpr/reduce_scatter | solution.py:69
  506.0 52.8 %all-gather.13.cloned.1.call-done = bf16[2048,1024]{1,0:T(8,128)(2,1)} async-done(((bf16[512,1024]{1,0:T(8,128)(2,1)}), bf16[2048,1024]{1,0:T(8,128)(2,1)}) %all-gather.13.cloned.1.call-update) | async-done | bytes 4194320 | tf_op jit(solution)/shard_map/while/body/eval_jaxpr/all_gather | solution.py:74
  558.8 29.1 fusion.300
  590.2 50.6 %reduce-scatter.24.cloned.1.call-done = bf16[512,1024]{1,0:T(8,128)(2,1)} async-done(((bf16[2048,1024]{1,0:T(8,128)(2,1)}), bf16[512,1024]{1,0:T(8,128)(2,1)}) %reduce-scatter.24.cloned.1.call-update) | async-done | bytes 1048592 | tf_op jit(solution)/shard_map/while/body/eval_jaxpr/reduce_scatter | solution.py:80
  654.5 52.7 %all-gather.11.cloned.1.call-done = bf16[2048,1024]{1,0:T(8,128)(2,1)} async-done(((bf16[512,1024]{1,0:T(8,128)(2,1)}), bf16[2048,1024]{1,0:T(8,128)(2,1)}) %all-gather.11.cloned.1.call-update) | async-done | bytes 4194320 | tf_op jit(solution)/shard_map/while/body/eval_jaxpr/all_gather | solution.py:42
  735.8 12.5 fusion.296
  748.3 14.0 fusion.297
  768.3 51.2 %reduce-scatter.22.cloned.1.call-done = bf16[512,1024]{1,0:T(8,128)(2,1)} async-done(((bf16[2048,1024]{1,0:T(8,128)(2,1)}), bf16[512,1024]{1,0:T(8,128)(2,1)}) %reduce-scatter.22.cloned.1.call-update) | async-done | bytes 1048592 | tf_op jit(solution)/shard_map/while/body/eval_jaxpr/reduce_scatter | solution.py:69
  824.8 52.8 %all-gather.13.cloned.1.call-done = bf16[2048,1024]{1,0:T(8,128)(2,1)} async-done(((bf16[512,1024]{1,0:T(8,128)(2,1)}), bf16[2048,1024]{1,0:T(8,128)(2,1)}) %all-gather.13.cloned.1.call-update) | async-done | bytes 4194320 | tf_op jit(solution)/shard_map/while/body/eval_jaxpr/all_gather | solution.py:74
  877.5 29.1 fusion.300
  909.0 50.6 %reduce-scatter.24.cloned.1.call-done = bf16[512,1024]{1,0:T(8,128)(2,1)} async-done(((bf16[2048,1024]{1,0:T(8,128)(2,1)}), bf16[512,1024]{1,0:T(8,128)(2,1)}) %reduce-scatter.24.cloned.1.call-update) | async-done | bytes 1048592 | tf_op jit(solution)/shard_map/while/body/eval_jaxpr/reduce_scatter | solution.py:80
  972.4 2644.7 %while.54 = (s32[]{:T(128)}, bf16[512,1024]{1,0:T(8,128)(2,1)}, bf16[2,512,1024]{2,1,0:T(8,128)(2,1)}, f32[3,1024,256]{1,2,0:T(8,128)}, f32[2,256]{1,0:T(2,128)}...) while((s32[]{:T(128)}, bf16[512,1024]{1,0:T(8,128)(2,1)}, ...), condition=%wide.region_40.41_spmd.clone, body=%wide.region_10.40_spmd.clone.sunk | while | flops 42195251200 | bytes 907971328 | solution.py:301
  977.0 54.8 %all-gather.15.cloned.1.call-done = bf16[1,2048,1024]{2,1,0:T(8,128)(2,1)} async-done(((bf16[1,512,1024]{2,1,0:T(8,128)(2,1)}), bf16[1,2048,1024]{2,1,0:T(8,128)(2,1)}) %all-gather.15.cloned.1.call-update) | async-done | bytes 4194320 | tf_op jit(solution)/shard_map/while/body/eval_jaxpr/all_gather | solution.py:42
  1085.4 52.1 %reduce-scatter.26.cloned.1.call-done = bf16[512,1024]{1,0:T(8,128)(2,1)} async-done(((bf16[2048,1024]{1,0:T(8,128)(2,1)}), bf16[512,1024]{1,0:T(8,128)(2,1)}) %reduce-scatter.26.cloned.1.call-update) | async-done | bytes 1048592 | tf_op jit(solution)/shard_map/while/body/eval_jaxpr/reduce_scatter | solution.py:69
  1143.4 52.1 %all-gather.17.cloned.1.call-done = bf16[2048,1024]{1,0:T(8,128)(2,1)} async-done(((bf16[512,1024]{1,0:T(8,128)(2,1)}), bf16[2048,1024]{1,0:T(8,128)(2,1)}) %all-gather.17.cloned.1.call-update) | async-done | bytes 4194320 | tf_op jit(solution)/shard_map/while/body/eval_jaxpr/all_gather | solution.py:74
  1195.5 26.4 multiply_convert_fusion.6
  1229.9 52.8 %reduce-scatter.28.cloned.1.call-done = bf16[512,1024]{1,0:T(8,128)(2,1)} async-done(((bf16[2048,1024]{1,0:T(8,128)(2,1)}), bf16[512,1024]{1,0:T(8,128)(2,1)}) %reduce-scatter.28.cloned.1.call-update) | async-done | bytes 1048592 | tf_op jit(solution)/shard_map/while/body/eval_jaxpr/reduce_scatter | solution.py:80
  1289.8 52.8 %all-gather.19.cloned.1.call-done = bf16[2048,1024]{1,0:T(8,128)(2,1)} async-done(((bf16[512,1024]{1,0:T(8,128)(2,1)}), bf16[2048,1024]{1,0:T(8,128)(2,1)}) %all-gather.19.cloned.1.call-update) | async-done | bytes 4194320 | tf_op jit(solution)/shard_map/while/body/eval_jaxpr/all_gather | solution.py:130
  1342.6 13.9 convert_reduce_fusion.5
  1365.0 52.8 %reduce-scatter.30.cloned.1.call-done = bf16[512,1024]{1,0:T(8,128)(2,1)} async-done(((bf16[2048,1024]{1,0:T(8,128)(2,1)}), bf16[512,1024]{1,0:T(8,128)(2,1)}) %reduce-scatter.30.cloned.1.call-update) | async-done | bytes 1048592 | tf_op jit(solution)/shard_map/while/body/eval_jaxpr/reduce_scatter | solution.py:140
  1425.0 52.8 %all-gather.21.cloned.1.call-done = bf16[2048,1024]{1,0:T(8,128)(2,1)} async-done(((bf16[512,1024]{1,0:T(8,128)(2,1)}), bf16[2048,1024]{1,0:T(8,128)(2,1)}) %all-gather.21.cloned.1.call-update) | async-done | bytes 4194320 | tf_op jit(solution)/shard_map/while/body/eval_jaxpr/all_gather | solution.py:147
  1510.1 12.1 multiply_convert_fusion.7
  1600.3 13.4 reduce-scatter.32.cloned.1.call-done
  1618.6 221.8 %all-reduce.8.cloned.1.call-done = (bf16[3,1024,256]{1,2,0:T(8,128)(2,1)}, bf16[256,1024]{1,0:T(8,128)(2,1)}, bf16[1024,1024]{1,0:T(8,128)(2,1)}, bf16[1024,1024]{1,0:T(8,128)(2,1)}) async-done(((bf16[3,1024,256]{1,2,0:T(8,128)(2,1)}, bf16[256,1024]{1,0:T(8,128)(2,1)}, bf16[1024,1024]{1,0:T(8,128)(2,1)}, bf16[1024,1024]{1,0:T(8,128)(2,1)}), (bf16[3,1024,256]{1,2,0:T(8,128)(2,1)}, ...) | async-done | bytes 6291472 | tf_op jit(solution)/shard_map/while/body/eval_jaxpr/psum | solution.py:288
  1857.2 53.7 %all-gather.15.cloned.1.call-done = bf16[1,2048,1024]{2,1,0:T(8,128)(2,1)} async-done(((bf16[1,512,1024]{2,1,0:T(8,128)(2,1)}), bf16[1,2048,1024]{2,1,0:T(8,128)(2,1)}) %all-gather.15.cloned.1.call-update) | async-done | bytes 4194320 | tf_op jit(solution)/shard_map/while/body/eval_jaxpr/all_gather | solution.py:42
  1964.3 52.1 %reduce-scatter.26.cloned.1.call-done = bf16[512,1024]{1,0:T(8,128)(2,1)} async-done(((bf16[2048,1024]{1,0:T(8,128)(2,1)}), bf16[512,1024]{1,0:T(8,128)(2,1)}) %reduce-scatter.26.cloned.1.call-update) | async-done | bytes 1048592 | tf_op jit(solution)/shard_map/while/body/eval_jaxpr/reduce_scatter | solution.py:69
  2022.3 52.1 %all-gather.17.cloned.1.call-done = bf16[2048,1024]{1,0:T(8,128)(2,1)} async-done(((bf16[512,1024]{1,0:T(8,128)(2,1)}), bf16[2048,1024]{1,0:T(8,128)(2,1)}) %all-gather.17.cloned.1.call-update) | async-done | bytes 4194320 | tf_op jit(solution)/shard_map/while/body/eval_jaxpr/all_gather | solution.py:74
  2074.5 26.3 multiply_convert_fusion.6
  2108.8 52.8 %reduce-scatter.28.cloned.1.call-done = bf16[512,1024]{1,0:T(8,128)(2,1)} async-done(((bf16[2048,1024]{1,0:T(8,128)(2,1)}), bf16[512,1024]{1,0:T(8,128)(2,1)}) %reduce-scatter.28.cloned.1.call-update) | async-done | bytes 1048592 | tf_op jit(solution)/shard_map/while/body/eval_jaxpr/reduce_scatter | solution.py:80
  2168.7 52.8 %all-gather.19.cloned.1.call-done = bf16[2048,1024]{1,0:T(8,128)(2,1)} async-done(((bf16[512,1024]{1,0:T(8,128)(2,1)}), bf16[2048,1024]{1,0:T(8,128)(2,1)}) %all-gather.19.cloned.1.call-update) | async-done | bytes 4194320 | tf_op jit(solution)/shard_map/while/body/eval_jaxpr/all_gather | solution.py:130
  2221.5 13.9 convert_reduce_fusion.5
  2243.9 52.8 %reduce-scatter.30.cloned.1.call-done = bf16[512,1024]{1,0:T(8,128)(2,1)} async-done(((bf16[2048,1024]{1,0:T(8,128)(2,1)}), bf16[512,1024]{1,0:T(8,128)(2,1)}) %reduce-scatter.30.cloned.1.call-update) | async-done | bytes 1048592 | tf_op jit(solution)/shard_map/while/body/eval_jaxpr/reduce_scatter | solution.py:140
  2303.9 52.8 %all-gather.21.cloned.1.call-done = bf16[2048,1024]{1,0:T(8,128)(2,1)} async-done(((bf16[512,1024]{1,0:T(8,128)(2,1)}), bf16[2048,1024]{1,0:T(8,128)(2,1)}) %all-gather.21.cloned.1.call-update) | async-done | bytes 4194320 | tf_op jit(solution)/shard_map/while/body/eval_jaxpr/all_gather | solution.py:147
  2389.0 12.1 multiply_convert_fusion.7
  2467.4 11.7 all-reduce.5
  2479.2 13.4 reduce-scatter.32.cloned.1.call-done
  2497.5 221.6 %all-reduce.8.cloned.1.call-done = (bf16[3,1024,256]{1,2,0:T(8,128)(2,1)}, bf16[256,1024]{1,0:T(8,128)(2,1)}, bf16[1024,1024]{1,0:T(8,128)(2,1)}, bf16[1024,1024]{1,0:T(8,128)(2,1)}) async-done(((bf16[3,1024,256]{1,2,0:T(8,128)(2,1)}, bf16[256,1024]{1,0:T(8,128)(2,1)}, bf16[1024,1024]{1,0:T(8,128)(2,1)}, bf16[1024,1024]{1,0:T(8,128)(2,1)}), (bf16[3,1024,256]{1,2,0:T(8,128)(2,1)}, ...) | async-done | bytes 6291472 | tf_op jit(solution)/shard_map/while/body/eval_jaxpr/psum | solution.py:288
  2737.2 53.7 %all-gather.15.cloned.1.call-done = bf16[1,2048,1024]{2,1,0:T(8,128)(2,1)} async-done(((bf16[1,512,1024]{2,1,0:T(8,128)(2,1)}), bf16[1,2048,1024]{2,1,0:T(8,128)(2,1)}) %all-gather.15.cloned.1.call-update) | async-done | bytes 4194320 | tf_op jit(solution)/shard_map/while/body/eval_jaxpr/all_gather | solution.py:42
  2844.3 52.1 %reduce-scatter.26.cloned.1.call-done = bf16[512,1024]{1,0:T(8,128)(2,1)} async-done(((bf16[2048,1024]{1,0:T(8,128)(2,1)}), bf16[512,1024]{1,0:T(8,128)(2,1)}) %reduce-scatter.26.cloned.1.call-update) | async-done | bytes 1048592 | tf_op jit(solution)/shard_map/while/body/eval_jaxpr/reduce_scatter | solution.py:69
  2902.3 52.1 %all-gather.17.cloned.1.call-done = bf16[2048,1024]{1,0:T(8,128)(2,1)} async-done(((bf16[512,1024]{1,0:T(8,128)(2,1)}), bf16[2048,1024]{1,0:T(8,128)(2,1)}) %all-gather.17.cloned.1.call-update) | async-done | bytes 4194320 | tf_op jit(solution)/shard_map/while/body/eval_jaxpr/all_gather | solution.py:74
  2954.5 26.3 multiply_convert_fusion.6
  2988.8 52.8 %reduce-scatter.28.cloned.1.call-done = bf16[512,1024]{1,0:T(8,128)(2,1)} async-done(((bf16[2048,1024]{1,0:T(8,128)(2,1)}), bf16[512,1024]{1,0:T(8,128)(2,1)}) %reduce-scatter.28.cloned.1.call-update) | async-done | bytes 1048592 | tf_op jit(solution)/shard_map/while/body/eval_jaxpr/reduce_scatter | solution.py:80
  3048.7 52.8 %all-gather.19.cloned.1.call-done = bf16[2048,1024]{1,0:T(8,128)(2,1)} async-done(((bf16[512,1024]{1,0:T(8,128)(2,1)}), bf16[2048,1024]{1,0:T(8,128)(2,1)}) %all-gather.19.cloned.1.call-update) | async-done | bytes 4194320 | tf_op jit(solution)/shard_map/while/body/eval_jaxpr/all_gather | solution.py:130
  3101.5 13.9 convert_reduce_fusion.5
  3123.9 52.8 %reduce-scatter.30.cloned.1.call-done = bf16[512,1024]{1,0:T(8,128)(2,1)} async-done(((bf16[2048,1024]{1,0:T(8,128)(2,1)}), bf16[512,1024]{1,0:T(8,128)(2,1)}) %reduce-scatter.30.cloned.1.call-update) | async-done | bytes 1048592 | tf_op jit(solution)/shard_map/while/body/eval_jaxpr/reduce_scatter | solution.py:140
  3183.9 52.8 %all-gather.21.cloned.1.call-done = bf16[2048,1024]{1,0:T(8,128)(2,1)} async-done(((bf16[512,1024]{1,0:T(8,128)(2,1)}), bf16[2048,1024]{1,0:T(8,128)(2,1)}) %all-gather.21.cloned.1.call-update) | async-done | bytes 4194320 | tf_op jit(solution)/shard_map/while/body/eval_jaxpr/all_gather | solution.py:147
  3269.0 12.1 multiply_convert_fusion.7
  3347.4 11.7 all-reduce.5
  3359.2 13.4 reduce-scatter.32.cloned.1.call-done
  3377.5 221.6 %all-reduce.8.cloned.1.call-done = (bf16[3,1024,256]{1,2,0:T(8,128)(2,1)}, bf16[256,1024]{1,0:T(8,128)(2,1)}, bf16[1024,1024]{1,0:T(8,128)(2,1)}, bf16[1024,1024]{1,0:T(8,128)(2,1)}) async-done(((bf16[3,1024,256]{1,2,0:T(8,128)(2,1)}, bf16[256,1024]{1,0:T(8,128)(2,1)}, bf16[1024,1024]{1,0:T(8,128)(2,1)}, bf16[1024,1024]{1,0:T(8,128)(2,1)}), (bf16[3,1024,256]{1,2,0:T(8,128)(2,1)}, ...) | async-done | bytes 6291472 | tf_op jit(solution)/shard_map/while/body/eval_jaxpr/psum | solution.py:288
  3626.1 69.6 %reduce-scatter.18.cloned.1.call-done = f32[64,2]{1,0:T(8,128)} async-done(((f32[1024,2]{1,0:T(8,128)}), f32[64,2]{1,0:T(8,128)}) %reduce-scatter.18.cloned.1.call-update) | async-done | bytes 528
  3697.1 74.2 %reduce-scatter.20.cloned.1.call-done = f32[64,2]{1,0:T(8,128)} async-done(((f32[1024,2]{1,0:T(8,128)}), f32[64,2]{1,0:T(8,128)}) %reduce-scatter.20.cloned.1.call-update) | async-done | bytes 528
  3772.7 74.1 %reduce-scatter.16.cloned.1.call-done = f32[64,2]{1,0:T(8,128)} async-done(((f32[1024,2]{1,0:T(8,128)}), f32[64,2]{1,0:T(8,128)}) %reduce-scatter.16.cloned.1.call-update) | async-done | bytes 528
  (769 shorter events, 827.8 us)
Async XLA Ops:
  10.8 58.9 %all-gather.11.cloned.1.call-start = ((), (), s32[]{:S(2)}) async-start(), calls=%async_computation.12 | async-start | bytes 5242880 | tf_op jit(solution)/shard_map/while/body/eval_jaxpr/all_gather | solution.py:42
  14.2 167.9 %reduce-scatter.22.cloned.1.call-start = ((), (), s32[]{:S(2)}) async-start(), calls=%async_computation.13 | async-start | bytes 5242880 | tf_op jit(solution)/shard_map/while/body/eval_jaxpr/reduce_scatter | solution.py:69
  129.2 52.9 %copy-start = (bf16[512,1024]{1,0:T(8,128)(2,1)S(1)}, bf16[512,1024]{1,0:T(8,128)(2,1)}, u32[]{:S(2)}) copy-start(bf16[512,1024]{1,0:T(8,128)(2,1)} %get-tuple-element.1359) | copy-start | bytes 3145732 | tf_op jit(solution)/shard_map/while
  129.2 110.9 %all-gather.13.cloned.1.call-start = ((), (), s32[]{:S(2)}) async-start(), calls=%async_computation.14 | async-start | bytes 5242880 | tf_op jit(solution)/shard_map/while/body/eval_jaxpr/all_gather | solution.py:74
  187.2 134.9 %reduce-scatter.24.cloned.1.call-start = ((), (), s32[]{:S(2)}) async-start(), calls=%async_computation.15 | async-start | bytes 5242880 | tf_op jit(solution)/shard_map/while/body/eval_jaxpr/reduce_scatter | solution.py:80
  328.1 4.2 collective-permute-start
  332.3 56.2 %all-gather.11.cloned.1.call-start = ((), (), s32[]{:S(2)}) async-start(), calls=%async_computation.12 | async-start | bytes 5242880 | tf_op jit(solution)/shard_map/while/body/eval_jaxpr/all_gather | solution.py:42
  335.6 165.3 %reduce-scatter.22.cloned.1.call-start = ((), (), s32[]{:S(2)}) async-start(), calls=%async_computation.13 | async-start | bytes 5242880 | tf_op jit(solution)/shard_map/while/body/eval_jaxpr/reduce_scatter | solution.py:69
  448.0 110.8 %all-gather.13.cloned.1.call-start = ((), (), s32[]{:S(2)}) async-start(), calls=%async_computation.14 | async-start | bytes 5242880 | tf_op jit(solution)/shard_map/while/body/eval_jaxpr/all_gather | solution.py:74
  506.0 134.9 %reduce-scatter.24.cloned.1.call-start = ((), (), s32[]{:S(2)}) async-start(), calls=%async_computation.15 | async-start | bytes 5242880 | tf_op jit(solution)/shard_map/while/body/eval_jaxpr/reduce_scatter | solution.py:80
  646.8 4.2 collective-permute-start
  651.0 56.2 %all-gather.11.cloned.1.call-start = ((), (), s32[]{:S(2)}) async-start(), calls=%async_computation.12 | async-start | bytes 5242880 | tf_op jit(solution)/shard_map/while/body/eval_jaxpr/all_gather | solution.py:42
  654.3 165.3 %reduce-scatter.22.cloned.1.call-start = ((), (), s32[]{:S(2)}) async-start(), calls=%async_computation.13 | async-start | bytes 5242880 | tf_op jit(solution)/shard_map/while/body/eval_jaxpr/reduce_scatter | solution.py:69
  766.7 110.8 %all-gather.13.cloned.1.call-start = ((), (), s32[]{:S(2)}) async-start(), calls=%async_computation.14 | async-start | bytes 5242880 | tf_op jit(solution)/shard_map/while/body/eval_jaxpr/all_gather | solution.py:74
  824.7 134.9 %reduce-scatter.24.cloned.1.call-start = ((), (), s32[]{:S(2)}) async-start(), calls=%async_computation.15 | async-start | bytes 5242880 | tf_op jit(solution)/shard_map/while/body/eval_jaxpr/reduce_scatter | solution.py:80
  965.5 4.2 collective-permute-start
  975.6 62.3 %copy-start.34 = (bf16[2,256]{1,0:T(2,128)(2,1)}, bf16[2,256]{1,0:T(2,128)(2,1)S(1)}, u32[]{:S(2)}) copy-start(bf16[2,256]{1,0:T(2,128)(2,1)S(1)} %get-tuple-element.1583) | copy-start | bytes 3076 | tf_op jit(solution)/shard_map/while
  975.7 62.3 %copy-start.42 = (bf16[1024]{0:T(1024)(128)(2,1)}, bf16[1024]{0:T(1024)(128)(2,1)S(1)}, u32[]{:S(2)}) copy-start(bf16[1024]{0:T(1024)(128)(2,1)S(1)} %get-tuple-element.1589) | copy-start | bytes 6148 | tf_op jit(solution)/shard_map/while
  975.7 56.2 %all-gather.15.cloned.1.call-start = ((), (), s32[]{:S(2)}) async-start(), calls=%async_computation.16 | async-start | bytes 5242880 | tf_op jit(solution)/shard_map/while/body/eval_jaxpr/all_gather | solution.py:42
  976.8 160.7 %reduce-scatter.26.cloned.1.call-start = ((), (), s32[]{:S(2)}) async-start(), calls=%async_computation.17 | async-start | bytes 5242880 | tf_op jit(solution)/shard_map/while/body/eval_jaxpr/reduce_scatter | solution.py:69
  1084.7 110.8 %all-gather.17.cloned.1.call-start = ((), (), s32[]{:S(2)}) async-start(), calls=%async_computation.18 | async-start | bytes 5242880 | tf_op jit(solution)/shard_map/while/body/eval_jaxpr/all_gather | solution.py:74
  1142.7 140.0 %reduce-scatter.28.cloned.1.call-start = ((), (), s32[]{:S(2)}) async-start(), calls=%async_computation.19 | async-start | bytes 5242880 | tf_op jit(solution)/shard_map/while/body/eval_jaxpr/reduce_scatter | solution.py:80
  1229.8 112.7 %all-gather.19.cloned.1.call-start = ((), (), s32[]{:S(2)}) async-start(), calls=%async_computation.20 | async-start | bytes 5242880 | tf_op jit(solution)/shard_map/while/body/eval_jaxpr/all_gather | solution.py:130
  1289.7 128.1 %reduce-scatter.30.cloned.1.call-start = ((), (), s32[]{:S(2)}) async-start(), calls=%async_computation.21 | async-start | bytes 5242880 | tf_op jit(solution)/shard_map/while/body/eval_jaxpr/reduce_scatter | solution.py:140
  1364.9 112.9 %all-gather.21.cloned.1.call-start = ((), (), s32[]{:S(2)}) async-start(), calls=%async_computation.22 | async-start | bytes 5242880 | tf_op jit(solution)/shard_map/while/body/eval_jaxpr/all_gather | solution.py:147
  1422.4 55.5 %copy-start.23 = (bf16[256,1024]{1,0:T(8,128)(2,1)S(1)}, bf16[256,1024]{1,0:T(8,128)(2,1)}, u32[]{:S(2)}) copy-start(bf16[256,1024]{1,0:T(8,128)(2,1)} %get-tuple-element.1584) | copy-start | bytes 1572868 | tf_op jit(solution)/shard_map/while
  1425.0 188.7 %reduce-scatter.32.cloned.1.call-start = ((), (), s32[]{:S(2)}) async-start(), calls=%async_computation.23 | async-start | bytes 5242880 | tf_op jit(solution)/shard_map/while/body/eval_jaxpr/reduce_scatter | solution.py:187
  1560.8 279.6 %all-reduce.8.cloned.1.call-start = ((), (), s32[]{:S(2)}) async-start(), calls=%async_computation.24 | async-start | bytes 12582912 | tf_op jit(solution)/shard_map/while/body/eval_jaxpr/psum | solution.py:288
  1600.2 244.2 %copy-start.47 = (f32[2,256]{1,0:T(2,128)}, f32[2,256]{1,0:T(2,128)S(1)}, u32[]{:S(2)}) copy-start(f32[2,256]{1,0:T(2,128)S(1)} %select_add_fusion.12) | copy-start | bytes 6148 | tf_op jit(solution)/shard_map/while
  1600.3 244.2 %copy-start.45 = (f32[1024]{0:T(1024)}, f32[1024]{0:T(1024)S(1)}, u32[]{:S(2)}) copy-start(f32[1024]{0:T(1024)S(1)} %select_add_fusion.15) | copy-start | bytes 12292 | tf_op jit(solution)/shard_map/while
  1617.3 234.4 %collective-permute-start.1 = (bf16[512,1024]{1,0:T(8,128)(2,1)}, bf16[512,1024]{1,0:T(8,128)(2,1)S(1)}, u32[]{:S(2)}, u32[]{:S(2)}) collective-permute-start(bf16[512,1024]{1,0:T(8,128)(2,1)} %get-tuple-element.1424), channel_id=1, source_target_pairs={{16,0},{17,1},{18,2},{19,3},{20,4},{21,5},{22,6},{23,7},{24,8},{25... | collective-permute-start | bytes 3145736 | tf_op jit(solution)/shard_map/while/body/eval_jaxpr/ppermute | solution.py:16
  1855.8 61.2 %copy-start.34 = (bf16[2,256]{1,0:T(2,128)(2,1)}, bf16[2,256]{1,0:T(2,128)(2,1)S(1)}, u32[]{:S(2)}) copy-start(bf16[2,256]{1,0:T(2,128)(2,1)S(1)} %get-tuple-element.1583) | copy-start | bytes 3076 | tf_op jit(solution)/shard_map/while
  1855.8 61.2 %copy-start.42 = (bf16[1024]{0:T(1024)(128)(2,1)}, bf16[1024]{0:T(1024)(128)(2,1)S(1)}, u32[]{:S(2)}) copy-start(bf16[1024]{0:T(1024)(128)(2,1)S(1)} %get-tuple-element.1589) | copy-start | bytes 6148 | tf_op jit(solution)/shard_map/while
  1855.8 55.0 %all-gather.15.cloned.1.call-start = ((), (), s32[]{:S(2)}) async-start(), calls=%async_computation.16 | async-start | bytes 5242880 | tf_op jit(solution)/shard_map/while/body/eval_jaxpr/all_gather | solution.py:42
  1857.0 159.5 %reduce-scatter.26.cloned.1.call-start = ((), (), s32[]{:S(2)}) async-start(), calls=%async_computation.17 | async-start | bytes 5242880 | tf_op jit(solution)/shard_map/while/body/eval_jaxpr/reduce_scatter | solution.py:69
  1963.6 110.8 %all-gather.17.cloned.1.call-start = ((), (), s32[]{:S(2)}) async-start(), calls=%async_computation.18 | async-start | bytes 5242880 | tf_op jit(solution)/shard_map/while/body/eval_jaxpr/all_gather | solution.py:74
  2021.6 140.0 %reduce-scatter.28.cloned.1.call-start = ((), (), s32[]{:S(2)}) async-start(), calls=%async_computation.19 | async-start | bytes 5242880 | tf_op jit(solution)/shard_map/while/body/eval_jaxpr/reduce_scatter | solution.py:80
  2108.8 112.8 %all-gather.19.cloned.1.call-start = ((), (), s32[]{:S(2)}) async-start(), calls=%async_computation.20 | async-start | bytes 5242880 | tf_op jit(solution)/shard_map/while/body/eval_jaxpr/all_gather | solution.py:130
  2168.7 128.0 %reduce-scatter.30.cloned.1.call-start = ((), (), s32[]{:S(2)}) async-start(), calls=%async_computation.21 | async-start | bytes 5242880 | tf_op jit(solution)/shard_map/while/body/eval_jaxpr/reduce_scatter | solution.py:140
  2243.8 112.9 %all-gather.21.cloned.1.call-start = ((), (), s32[]{:S(2)}) async-start(), calls=%async_computation.22 | async-start | bytes 5242880 | tf_op jit(solution)/shard_map/while/body/eval_jaxpr/all_gather | solution.py:147
  2301.3 55.5 %copy-start.23 = (bf16[256,1024]{1,0:T(8,128)(2,1)S(1)}, bf16[256,1024]{1,0:T(8,128)(2,1)}, u32[]{:S(2)}) copy-start(bf16[256,1024]{1,0:T(8,128)(2,1)} %get-tuple-element.1584) | copy-start | bytes 1572868 | tf_op jit(solution)/shard_map/while
  2303.9 188.7 %reduce-scatter.32.cloned.1.call-start = ((), (), s32[]{:S(2)}) async-start(), calls=%async_computation.23 | async-start | bytes 5242880 | tf_op jit(solution)/shard_map/while/body/eval_jaxpr/reduce_scatter | solution.py:187
  2439.7 279.4 %all-reduce.8.cloned.1.call-start = ((), (), s32[]{:S(2)}) async-start(), calls=%async_computation.24 | async-start | bytes 12582912 | tf_op jit(solution)/shard_map/while/body/eval_jaxpr/psum | solution.py:288
  2479.1 245.0 %copy-start.47 = (f32[2,256]{1,0:T(2,128)}, f32[2,256]{1,0:T(2,128)S(1)}, u32[]{:S(2)}) copy-start(f32[2,256]{1,0:T(2,128)S(1)} %select_add_fusion.12) | copy-start | bytes 6148 | tf_op jit(solution)/shard_map/while
  2479.2 244.9 %copy-start.45 = (f32[1024]{0:T(1024)}, f32[1024]{0:T(1024)S(1)}, u32[]{:S(2)}) copy-start(f32[1024]{0:T(1024)S(1)} %select_add_fusion.15) | copy-start | bytes 12292 | tf_op jit(solution)/shard_map/while
  2496.2 235.5 %collective-permute-start.1 = (bf16[512,1024]{1,0:T(8,128)(2,1)}, bf16[512,1024]{1,0:T(8,128)(2,1)S(1)}, u32[]{:S(2)}, u32[]{:S(2)}) collective-permute-start(bf16[512,1024]{1,0:T(8,128)(2,1)} %get-tuple-element.1424), channel_id=1, source_target_pairs={{16,0},{17,1},{18,2},{19,3},{20,4},{21,5},{22,6},{23,7},{24,8},{25... | collective-permute-start | bytes 3145736 | tf_op jit(solution)/shard_map/while/body/eval_jaxpr/ppermute | solution.py:16
  2735.8 61.2 %copy-start.34 = (bf16[2,256]{1,0:T(2,128)(2,1)}, bf16[2,256]{1,0:T(2,128)(2,1)S(1)}, u32[]{:S(2)}) copy-start(bf16[2,256]{1,0:T(2,128)(2,1)S(1)} %get-tuple-element.1583) | copy-start | bytes 3076 | tf_op jit(solution)/shard_map/while
  2735.8 61.2 %copy-start.42 = (bf16[1024]{0:T(1024)(128)(2,1)}, bf16[1024]{0:T(1024)(128)(2,1)S(1)}, u32[]{:S(2)}) copy-start(bf16[1024]{0:T(1024)(128)(2,1)S(1)} %get-tuple-element.1589) | copy-start | bytes 6148 | tf_op jit(solution)/shard_map/while
  2735.8 55.0 %all-gather.15.cloned.1.call-start = ((), (), s32[]{:S(2)}) async-start(), calls=%async_computation.16 | async-start | bytes 5242880 | tf_op jit(solution)/shard_map/while/body/eval_jaxpr/all_gather | solution.py:42
  2737.0 159.5 %reduce-scatter.26.cloned.1.call-start = ((), (), s32[]{:S(2)}) async-start(), calls=%async_computation.17 | async-start | bytes 5242880 | tf_op jit(solution)/shard_map/while/body/eval_jaxpr/reduce_scatter | solution.py:69
  2843.6 110.8 %all-gather.17.cloned.1.call-start = ((), (), s32[]{:S(2)}) async-start(), calls=%async_computation.18 | async-start | bytes 5242880 | tf_op jit(solution)/shard_map/while/body/eval_jaxpr/all_gather | solution.py:74
  2901.6 140.0 %reduce-scatter.28.cloned.1.call-start = ((), (), s32[]{:S(2)}) async-start(), calls=%async_computation.19 | async-start | bytes 5242880 | tf_op jit(solution)/shard_map/while/body/eval_jaxpr/reduce_scatter | solution.py:80
  2988.8 112.8 %all-gather.19.cloned.1.call-start = ((), (), s32[]{:S(2)}) async-start(), calls=%async_computation.20 | async-start | bytes 5242880 | tf_op jit(solution)/shard_map/while/body/eval_jaxpr/all_gather | solution.py:130
  3048.7 128.0 %reduce-scatter.30.cloned.1.call-start = ((), (), s32[]{:S(2)}) async-start(), calls=%async_computation.21 | async-start | bytes 5242880 | tf_op jit(solution)/shard_map/while/body/eval_jaxpr/reduce_scatter | solution.py:140
  3123.8 112.9 %all-gather.21.cloned.1.call-start = ((), (), s32[]{:S(2)}) async-start(), calls=%async_computation.22 | async-start | bytes 5242880 | tf_op jit(solution)/shard_map/while/body/eval_jaxpr/all_gather | solution.py:147
  3181.3 55.5 %copy-start.23 = (bf16[256,1024]{1,0:T(8,128)(2,1)S(1)}, bf16[256,1024]{1,0:T(8,128)(2,1)}, u32[]{:S(2)}) copy-start(bf16[256,1024]{1,0:T(8,128)(2,1)} %get-tuple-element.1584) | copy-start | bytes 1572868 | tf_op jit(solution)/shard_map/while
  3183.9 188.7 %reduce-scatter.32.cloned.1.call-start = ((), (), s32[]{:S(2)}) async-start(), calls=%async_computation.23 | async-start | bytes 5242880 | tf_op jit(solution)/shard_map/while/body/eval_jaxpr/reduce_scatter | solution.py:187
  3319.7 279.4 %all-reduce.8.cloned.1.call-start = ((), (), s32[]{:S(2)}) async-start(), calls=%async_computation.24 | async-start | bytes 12582912 | tf_op jit(solution)/shard_map/while/body/eval_jaxpr/psum | solution.py:288
  3359.1 245.0 %copy-start.47 = (f32[2,256]{1,0:T(2,128)}, f32[2,256]{1,0:T(2,128)S(1)}, u32[]{:S(2)}) copy-start(f32[2,256]{1,0:T(2,128)S(1)} %select_add_fusion.12) | copy-start | bytes 6148 | tf_op jit(solution)/shard_map/while
  3359.2 245.0 %copy-start.45 = (f32[1024]{0:T(1024)}, f32[1024]{0:T(1024)S(1)}, u32[]{:S(2)}) copy-start(f32[1024]{0:T(1024)S(1)} %select_add_fusion.15) | copy-start | bytes 12292 | tf_op jit(solution)/shard_map/while
  3376.2 235.5 %collective-permute-start.1 = (bf16[512,1024]{1,0:T(8,128)(2,1)}, bf16[512,1024]{1,0:T(8,128)(2,1)S(1)}, u32[]{:S(2)}, u32[]{:S(2)}) collective-permute-start(bf16[512,1024]{1,0:T(8,128)(2,1)} %get-tuple-element.1424), channel_id=1, source_target_pairs={{16,0},{17,1},{18,2},{19,3},{20,4},{21,5},{22,6},{23,7},{24,8},{25... | collective-permute-start | bytes 3145736 | tf_op jit(solution)/shard_map/while/body/eval_jaxpr/ppermute | solution.py:16
  3617.1 78.5 %reduce-scatter.18.cloned.1.call-start = ((), (), s32[]{:S(2)}) async-start(), calls=%async_computation.10 | async-start | bytes 557056
  3618.9 152.3 %reduce-scatter.20.cloned.1.call-start = ((), (), s32[]{:S(2)}) async-start(), calls=%async_computation.11 | async-start | bytes 557056
  3620.7 226.0 %reduce-scatter.16.cloned.1.call-start = ((), (), s32[]{:S(2)}) async-start(), calls=%async_computation.9 | async-start | bytes 557056
  (153 other events, 1173.4 us)
Sparse Core Ops, SparseCore 0:
  14.3 55.3 all-gather.10
  129.4 52.6 reduce-scatter.21
  187.4 52.6 all-gather.12
  269.4 52.6 reduce-scatter.23
  335.7 52.7 all-gather.10
  448.1 52.6 reduce-scatter.21
  506.1 52.6 all-gather.12
  588.1 52.6 reduce-scatter.23
  654.4 52.7 all-gather.10
  766.8 52.6 reduce-scatter.21
  824.8 52.6 all-gather.12
  906.8 52.6 reduce-scatter.23
  979.1 52.7 all-gather.14
  1084.8 52.6 reduce-scatter.25
  1142.8 52.6 all-gather.16
  1230.0 52.6 reduce-scatter.27
  1289.8 52.6 all-gather.18
  1365.1 52.6 reduce-scatter.29
  1425.1 52.6 all-gather.20
  1560.9 52.6 reduce-scatter.31
  1616.5 223.8 all-reduce.7
  1859.2 51.5 all-gather.14
  1963.8 52.6 reduce-scatter.25
  2021.7 52.6 all-gather.16
  2108.9 52.6 reduce-scatter.27
  2168.8 52.6 all-gather.18
  2244.0 52.6 reduce-scatter.29
  2304.0 52.6 all-gather.20
  2439.8 52.6 reduce-scatter.31
  2495.2 223.8 all-reduce.7
  2739.2 51.5 all-gather.14
  2843.8 52.6 reduce-scatter.25
  2901.7 52.6 all-gather.16
  2988.9 52.6 reduce-scatter.27
  3048.8 52.6 all-gather.18
  3124.0 52.6 reduce-scatter.29
  3184.0 52.6 all-gather.20
  3319.8 52.6 reduce-scatter.31
  3375.2 223.8 all-reduce.7
Sparse Core Ops, SparseCore 1:
  3619.8 75.8 reduce-scatter.17
  3697.9 73.3 reduce-scatter.19
  3773.4 73.3 reduce-scatter.15
where the time goes:
time: 3860 us
  waiting for transfers between devices  2660 us (69%)
  matrix products  599 us (16%)
  local copies, waits for them, and re-layouts  303 us (8%)
  other arithmetic  220 us (6%)
    psum x3, waiting for transfers between devices, backward_step(): lax.psum(grad_one.astype(jnp.bfloat16), 'dp').astype(jnp.float32)  665 us
    all_gather x6, waiting for transfers between devices, layer_forward(): gathered = lax.all_gather(token_rows, 'mp', axis=0, tiled=True)  323 us
    all_gather x6, waiting for transfers between devices, layer_forward(): lax.all_gather(first.astype(jnp.bfloat16), 'mp', axis=0, tiled=True)  315 us
    reduce_scatter x6, waiting for transfers between devices, layer_forward(): lax.psum_scatter(ffn_part.astype(jnp.bfloat16), 'mp', scatter_dimension=0...  310 us
    reduce_scatter x6, waiting for transfers between devices, layer_forward(): lax.psum_scatter(attn_part.astype(jnp.bfloat16), 'mp', scatter_dimension=...  310 us
    unnamed x6, waiting for transfers between devices  218 us
    reduce_scatter x3, waiting for transfers between devices, layer_backward(): lax.psum_scatter(first_part.astype(jnp.bfloat16), 'mp', scatter_dimension...  158 us
    all_gather x3, waiting for transfers between devices, layer_backward(): lax.all_gather(grad_res_one.astype(jnp.bfloat16), 'mp', axis=0, tiled=True)  158 us
  transfers between devices with their start and end apart: 48, of which 45 were waited for; matrix products, arithmetic and copies ran while one was open for 4% of the time, Pallas kernels for 0%

commit v1 on v0

--- a/solution.py
+++ b/solution.py
@@ -204,7 +204,7 @@
     return (grad_in, matrix_grads, vector_grads)
 
 
-def on_device(
+def pipelined(
     token_in,
     cotangent,
     w_qkv,
@@ -320,6 +320,334 @@
         gain_part[None],
         shift_part[None],
     )
+
+
+def swapped(value, axis, bit):
+    return lax.ppermute(value, axis, [(i, i ^ bit) for i in range(lax.axis_size(axis))])
+
+
+def swap_x(value):
+    return swapped(value, "mp", 1)
+
+
+def swap_y(value):
+    return swapped(value, "mp", 2)
+
+
+def swap_core(value):
+    return swapped(value, "section", 1)
+
+
+def gather_blocks(own):
+    half = own.shape[0] // 2
+    by_x = swap_x(own)
+    by_y = swap_y(own)
+    far_low = swap_x(by_y[:half])
+    far_high = swap_y(by_x[half:])
+    return [own, by_x, by_y, jnp.concatenate([far_low, far_high], axis=0)]
+
+
+def gather_layer(own):
+    mine = gather_blocks(own)
+    other = [swap_core(block) for block in mine]
+    return [[a, b] for a, b in zip(mine, other)]
+
+
+def sum_dp(value):
+    devices = lax.axis_size("dp")
+    if devices != 4:
+        return lax.psum(value.astype(jnp.float32), "dp").astype(jnp.bfloat16)
+    place = lax.axis_index("dp")
+    is_end = (place == 0) | (place == devices - 1)
+    inner = lax.ppermute(value, "dp", [(0, 1), (3, 2)])
+    pair = (value.astype(jnp.float32) + inner.astype(jnp.float32)).astype(jnp.bfloat16)
+    across = lax.ppermute(pair, "dp", [(1, 2), (2, 1)])
+    total = (pair.astype(jnp.float32) + across.astype(jnp.float32)).astype(jnp.bfloat16)
+    outer = lax.ppermute(total, "dp", [(1, 0), (2, 3)])
+    return jnp.where(is_end, outer, total)
+
+
+def low(value):
+    return value.astype(jnp.bfloat16)
+
+
+def high(value):
+    return value.astype(jnp.float32)
+
+
+def reduce_blocks(mine, other):
+    blocks = [a + high(swap_core(low(b))) for a, b in zip(mine, other)]
+    half = blocks[0].shape[0] // 2
+    tops = [block[:half] for block in blocks]
+    ends = [block[half:] for block in blocks]
+    top_two = low(tops[2] + high(swap_x(low(tops[3]))))
+    end_one = low(ends[1] + high(swap_y(low(ends[3]))))
+    top = tops[0] + high(swap_x(low(tops[1]))) + high(swap_y(top_two))
+    end = ends[0] + high(swap_x(end_one)) + high(swap_y(low(ends[2])))
+    return sum_dp(jnp.concatenate([low(top), low(end)], axis=0))
+
+
+def dot(a, b):
+    return jnp.dot(a, b, preferred_element_type=jnp.float32)
+
+
+def dot_tn(a, b):
+    return lax.dot_general(a, b, (((0,), (0,)), ((), ())), preferred_element_type=jnp.float32)
+
+
+def dot_nt(a, b):
+    return lax.dot_general(a, b, (((1,), (1,)), ((), ())), preferred_element_type=jnp.float32)
+
+
+def local_forward(weights, vectors, rows):
+    w_qkv, w_attn_out, w_ffn_in, w_ffn_out = weights
+    qv_bias, ffn_bias, out_biases, norm_gains, norm_shifts = vectors
+    count, width = rows.shape
+    pages = count // SEQ
+    heads = width // HEAD_DIM
+    scale_factor = 1.0 / math.sqrt(HEAD_DIM)
+    heads_view = []
+    for c in range(3):
+        projected = dot(rows, w_qkv[c])
+        if c != 1:
+            projected = projected + qv_bias[c // 2]
+        heads_view.append(low(projected).reshape(pages, SEQ, heads, HEAD_DIM))
+    scores = (
+        jnp.einsum("pqhe,pkhe->phqk", heads_view[0], heads_view[1], preferred_element_type=jnp.float32)
+        * scale_factor
+    )
+    top_score = jnp.max(scores, axis=-1, keepdims=True)
+    exponent = jnp.exp(scores - top_score)
+    weights_soft = exponent / jnp.sum(exponent, axis=-1, keepdims=True)
+    weights_low = low(weights_soft)
+    attended = jnp.einsum("phqk,pkhe->pqhe", weights_low, heads_view[2], preferred_element_type=jnp.float32)
+    attended = low(attended.reshape(count, width))
+    residual_one = dot(attended, w_attn_out) + out_biases[0] + high(rows)
+    first = norm_rows(residual_one, norm_gains[0], norm_shifts[0])
+    first_low = low(first)
+    ffn_sum = out_biases[1] + first
+    pre_acts, activated = [], []
+    for r in range(4):
+        for h in range(2):
+            pre_act = dot(first_low, w_ffn_in[r][h]) + ffn_bias[r][h]
+            act = low(exact_gelu(pre_act))
+            ffn_sum = ffn_sum + dot(act, w_ffn_out[r][h])
+            pre_acts.append(pre_act)
+            activated.append(act)
+    result = norm_rows(ffn_sum, norm_gains[1], norm_shifts[1])
+    kept = (rows, heads_view, weights_soft, attended, residual_one, first_low, pre_acts, activated, ffn_sum)
+    return low(result), kept
+
+
+def local_backward(weights, vectors, kept, grad_out):
+    w_qkv, w_attn_out, w_ffn_in, w_ffn_out = weights
+    qv_bias, ffn_bias, out_biases, norm_gains, norm_shifts = vectors
+    rows, heads_view, weights_soft, attended, residual_one, first_low, pre_acts, activated, residual_two = kept
+    count, width = rows.shape
+    pages = count // SEQ
+    heads = width // HEAD_DIM
+    scale_factor = 1.0 / math.sqrt(HEAD_DIM)
+    unused_two, norm_two_back = jax.vjp(norm_rows, residual_two, norm_gains[1], norm_shifts[1])
+    grad_res_two, grad_gain_two, grad_shift_two = norm_two_back(high(grad_out))
+    grad_bias_two = jnp.sum(grad_res_two, axis=0)
+    ffn_grad = low(grad_res_two)
+    grads_out = [[dot_tn(activated[2 * r + h], ffn_grad) for r in range(4)] for h in range(2)]
+    sum_ffn_out = reduce_blocks(*grads_out)
+    grad_first = grad_res_two
+    grads_in, ffn_bias_grads = [[], []], []
+    for r in range(4):
+        for h in range(2):
+            grad_act = dot_nt(ffn_grad, w_ffn_out[r][h])
+            unused_gelu, gelu_back = jax.vjp(exact_gelu, pre_acts[2 * r + h])
+            grad_pre = low(gelu_back(grad_act)[0])
+            ffn_bias_grads.append(jnp.sum(high(grad_pre), axis=0))
+            grads_in[h].append(dot_tn(first_low, grad_pre))
+            grad_first = grad_first + dot_nt(grad_pre, w_ffn_in[r][h])
+    sum_ffn_in = reduce_blocks(*grads_in)
+    unused_one, norm_one_back = jax.vjp(norm_rows, residual_one, norm_gains[0], norm_shifts[0])
+    grad_res_one, grad_gain_one, grad_shift_one = norm_one_back(grad_first)
+    grad_bias_one = jnp.sum(grad_res_one, axis=0)
+    attn_grad = low(grad_res_one)
+    grad_w_out = dot_tn(attended, attn_grad).reshape(4, 2, width // 8, width)
+    sum_attn_out = reduce_blocks(*[[grad_w_out[r, h] for r in range(4)] for h in range(2)])
+    grad_attended = low(dot_nt(attn_grad, w_attn_out)).reshape(pages, SEQ, heads, HEAD_DIM)
+    weights_low = low(weights_soft)
+    grad_weights = jnp.einsum("pqhe,pkhe->phqk", grad_attended, heads_view[2], preferred_element_type=jnp.float32)
+    grad_values = jnp.einsum("phqk,pqhe->pkhe", weights_low, grad_attended, preferred_element_type=jnp.float32)
+    inner_total = jnp.sum(weights_soft * grad_weights, axis=-1, keepdims=True)
+    grad_scores = low(weights_soft * (grad_weights - inner_total))
+    grad_queries = (
+        jnp.einsum("phqk,pkhe->pqhe", grad_scores, heads_view[1], preferred_element_type=jnp.float32)
+        * scale_factor
+    )
+    grad_keys = (
+        jnp.einsum("phqk,pqhe->pkhe", grad_scores, heads_view[0], preferred_element_type=jnp.float32)
+        * scale_factor
+    )
+    grad_proj = [low(g).reshape(count, width) for g in (grad_queries, grad_keys, grad_values)]
+    sums_qkv = []
+    for c in range(3):
+        whole = dot_tn(rows, grad_proj[c])
+        parts = [whole[:, b * (width // 8) : (b + 1) * (width // 8)] for b in range(8)]
+        sums_qkv.append(reduce_blocks(parts[0::2], parts[1::2]))
+    grad_in = grad_res_one
+    for c in range(3):
+        grad_in = grad_in + dot_nt(grad_proj[c], w_qkv[c])
+    qv_sums = jnp.stack([jnp.sum(high(grad_proj[0]), axis=0), jnp.sum(high(grad_proj[2]), axis=0)])
+    vector_grads = (
+        qv_sums.reshape(2, 8, width // 8),
+        jnp.stack(ffn_bias_grads),
+        jnp.stack([grad_bias_one, grad_bias_two]),
+        jnp.stack([grad_gain_one, grad_gain_two]),
+        jnp.stack([grad_shift_one, grad_shift_two]),
+    )
+    return low(grad_in), (sums_qkv, sum_attn_out, sum_ffn_in, sum_ffn_out), vector_grads
+
+
+def by_page(
+    token_in,
+    cotangent,
+    w_qkv,
+    qv_bias,
+    w_attn_out,
+    w_ffn_in,
+    ffn_in_bias,
+    w_ffn_out,
+    out_biases,
+    norm_gains,
+    norm_shifts,
+):
+    core = lax.axis_index("section")
+    place = lax.axis_index("mp")
+    is_first = core == 0
+    width = token_in.shape[2]
+    own_rows = lax.dynamic_index_in_dim(token_in, core, 0, keepdims=False)
+    own_cot = lax.dynamic_index_in_dim(cotangent, core, 0, keepdims=False)
+
+    def by_layer(own, received):
+        return [jnp.where(is_first, own, received), jnp.where(is_first, received, own)]
+
+    def halves(shard, axis):
+        size = shard.shape[axis] // 2
+        return (
+            lax.dynamic_slice_in_dim(shard, core * size, size, axis),
+            lax.dynamic_slice_in_dim(shard, (1 - core) * size, size, axis),
+        )
+
+    def own_halves(shard, axis):
+        keep, give = halves(shard, axis)
+        return by_layer(keep, swap_core(give))
+
+    eighth = w_qkv.shape[3] // 2
+    qkv_keep, qkv_give = halves(w_qkv[0], 2)
+    qkv_own = by_layer(qkv_keep.reshape(-1, eighth), swap_core(qkv_give.reshape(-1, eighth)))
+    attn_own = own_halves(w_attn_out[0], 0)
+    ffn_in_own = own_halves(w_ffn_in[0], 1)
+    ffn_out_own = own_halves(w_ffn_out[0], 0)
+
+    ffn_half = ffn_in_bias.shape[1] // 2
+    small = jnp.concatenate(
+        [
+            qv_bias[0].reshape(2, 2, eighth).transpose(1, 0, 2).reshape(2, 2 * eighth),
+            ffn_in_bias[0].reshape(2, ffn_half),
+        ],
+        axis=1,
+    )
+    small = jnp.stack(by_layer(small, swap_core(small)))
+    small = jnp.stack([small, swap_x(small), swap_y(small), swapped(small, "mp", 3)])
+    small = high(jnp.where(is_first, small, small[:, :, ::-1]))
+    norms = jnp.concatenate([out_biases[0], norm_gains[0], norm_shifts[0]], axis=0)
+    norms = by_layer(norms, swap_core(norms))
+
+    layers = []
+    for layer in range(2):
+        qkv = gather_layer(qkv_own[layer])
+        blocks = [block for pair in qkv for block in pair]
+        full_qkv = [
+            jnp.concatenate([block[c * width : (c + 1) * width] for block in blocks], axis=1) for c in range(3)
+        ]
+        attn = gather_layer(attn_own[layer])
+        full_attn = jnp.concatenate([block for pair in attn for block in pair], axis=0)
+        ffn_in = gather_layer(ffn_in_own[layer])
+        ffn_out = gather_layer(ffn_out_own[layer])
+        own_small = small[:, layer]
+        qv = own_small[:, :, : 2 * eighth].reshape(8, 2, eighth).transpose(1, 0, 2).reshape(2, width)
+        ffn_bias = own_small[:, :, 2 * eighth :]
+        layer_norms = norms[layer]
+        layers.append(
+            (
+                (full_qkv, full_attn, ffn_in, ffn_out),
+                (qv, ffn_bias, layer_norms[0:2], layer_norms[2:4], layer_norms[4:6]),
+            )
+        )
+
+    out_zero, kept_zero = local_forward(*layers[0], own_rows)
+    out_one, kept_one = local_forward(*layers[1], out_zero)
+    grad_one, sums_one, vectors_one = local_backward(*layers[1], kept_one, own_cot)
+    grad_zero, sums_zero, vectors_zero = local_backward(*layers[0], kept_zero, grad_one)
+
+    def trade(first, second):
+        own = jnp.where(is_first, first, second)
+        received = swap_core(jnp.where(is_first, second, first))
+        return jnp.where(is_first, jnp.stack([own, received]), jnp.stack([received, own]))
+
+    activations = trade(out_zero, out_one)
+    input_grads = trade(grad_zero, grad_one)
+
+    def joined(zero, one, axis):
+        got_one = lax.ppermute(one, "section", [(0, 1)])
+        got_zero = lax.ppermute(zero, "section", [(1, 0)])
+        low_part = jnp.where(is_first, zero, got_one)
+        high_part = jnp.where(is_first, got_zero, one)
+        return high(jnp.concatenate([low_part, high_part], axis=axis))
+
+    grad_qkv = jnp.stack([joined(a, b, 1) for a, b in zip(sums_zero[0], sums_one[0])])
+    grad_attn = joined(sums_zero[1], sums_one[1], 0)
+    grad_ffn_in = joined(sums_zero[2], sums_one[2], 1)
+    grad_ffn_out = joined(sums_zero[3], sums_one[3], 0)
+
+    order = jnp.stack([2 * (place ^ (j // 2)) + (core ^ (j % 2)) for j in range(8)])
+
+    def packed(vectors):
+        qv, ffn, biases, gains, shifts = vectors
+        qv = jnp.take(qv, order, axis=1)
+        ffn = jnp.take(ffn, order, axis=0)
+        return jnp.concatenate([v.reshape(-1) for v in (qv, ffn, biases, gains, shifts)])
+
+    totals = jnp.stack([packed(vectors_zero), packed(vectors_one)]).reshape(2, -1, 128)
+    totals = lax.psum(totals, ("section", "mp", "dp")).reshape(2, -1)
+    totals = lax.dynamic_index_in_dim(totals, core, 0, keepdims=False)
+    qv_width, ffn_width = 2 * eighth, 2 * ffn_half
+    qv_total = totals[: 2 * width].reshape(2, width)
+    ffn_total = totals[2 * width : 2 * width + 4 * ffn_width]
+    rest = totals[2 * width + 4 * ffn_width :].reshape(3, 2, width)
+    piece = width // (lax.axis_size("mp") * lax.axis_size("dp"))
+    start = (place * lax.axis_size("dp") + lax.axis_index("dp")) * piece
+    rest = lax.dynamic_slice_in_dim(rest, start, piece, 2)
+    return (
+        activations[None],
+        input_grads[None],
+        grad_qkv[None],
+        lax.dynamic_slice_in_dim(qv_total, place * qv_width, qv_width, 1)[None],
+        grad_attn[None],
+        grad_ffn_in[None],
+        lax.dynamic_slice_in_dim(ffn_total, place * ffn_width, ffn_width, 0)[None],
+        grad_ffn_out[None],
+        rest[0][None],
+        rest[1][None],
+        rest[2][None],
+    )
+
+
+def on_device(*args):
+    token_in = args[0]
+    fits = (
+        lax.axis_size("section") == 2
+        and lax.axis_size("mp") == 4
+        and token_in.shape[0] == 2
+        and token_in.shape[1] % SEQ == 0
+    )
+    return by_page(*args) if fits else pipelined(*args)
 
 
 def solution(mesh):

time: 3860 us -> 1350 us (0.35)
  waiting for transfers between devices: 2660 us -> 600 us
  matrix products: 599 us -> 351 us
  local copies, waits for them, and re-layouts: 303 us -> 85.8 us
  starting transfers between devices: 11 us -> 211 us
  other arithmetic: 220 us -> 72.1 us
    all_gather x18 -> x0, waiting for transfers between devices: 955 us -> none  [the longest x6 323 us: layer_forward(): gathered = lax.all_gather(token_rows, 'mp', axis=0, tiled=True)]
    reduce_scatter x18 -> x0, waiting for transfers between devices: 819 us -> none  [the longest x6 310 us: layer_forward(): lax.psum_scatter(ffn_part.astype(jnp.bfloat16), 'mp', scatter_dimension=0...]
    psum x3 -> x1, waiting for transfers between devices: 665 us -> 111 us  [by_page(): totals = lax.psum(totals, ('section', 'mp', 'dp')).reshape(2, -1)]
    ppermute x6 -> x243, waiting for transfers between devices: 7.24 us -> 489 us  [the longest x195 318 us: swapped(): lax.ppermute(value, axis, [(i, i ^ bit) for i in range(lax.axis_size(axis...]
    dot_general x66 -> x130, matrix products: 569 us -> 331 us  [the longest x40 120 us: dot(): return jnp.dot(a, b, preferred_element_type=jnp.float32)]
    unnamed x6 -> x1, waiting for transfers between devices: 218 us -> 0.02 us
    ppermute x6 -> x243, starting transfers between devices: 9.26 us -> 211 us  [the longest x195 129 us: swapped(): lax.ppermute(value, axis, [(i, i ^ bit) for i in range(lax.axis_size(axis...]
    squeeze x27 -> x1, local copies, waits for them, and re-layouts: 98 us -> 0.01 us  [by_page(): own_small = small[:, layer]]
  transfers between devices with their start and end apart: 48 -> 244, of which waited for: 45 -> 105; matrix products, arithmetic and copies ran while one was open for 4% -> 20% of each run, Pallas kernels for 0% -> 0%
where the time goes in v1:
time: 1350 us; the launch traced here: 1340 us
  waiting for transfers between devices  600 us (44%)
  matrix products  351 us (26%)
  starting transfers between devices  211 us (16%)
  local copies, waits for them, and re-layouts  85.8 us (6%)
  other arithmetic  72.1 us (5%)
  between operations  19.7 us (1%)
    ppermute x195, waiting for transfers between devices, swapped(): lax.ppermute(value, axis, [(i, i ^ bit) for i in range(lax.axis_size(axis...  318 us
    ppermute x195, starting transfers between devices, swapped(): lax.ppermute(value, axis, [(i, i ^ bit) for i in range(lax.axis_size(axis...  129 us
    ppermute x12, waiting for transfers between devices, sum_dp(): outer = lax.ppermute(total, 'dp', [(1, 0), (2, 3)])  123 us
    dot_general x40, matrix products, dot(): return jnp.dot(a, b, preferred_element_type=jnp.float32)  120 us
    psum x1, waiting for transfers between devices, by_page(): totals = lax.psum(totals, ('section', 'mp', 'dp')).reshape(2, -1)  111 us
    dot_general x40, matrix products, dot_nt(): lax.dot_general(a, b, (((1,), (1,)), ((), ())), preferred_element_type=jn...  73.6 us
    dot_general x40, matrix products, dot_tn(): lax.dot_general(a, b, (((0,), (0,)), ((), ())), preferred_element_type=jn...  67.8 us
    ppermute x12, waiting for transfers between devices, sum_dp(): inner = lax.ppermute(value, 'dp', [(0, 1), (3, 2)])  48.2 us
  transfers between devices with their start and end apart: 244, of which 105 were waited for; matrix products, arithmetic and copies ran while one was open for 20% of the time, Pallas kernels for 0%

profile of v1, /device:TPU:0, one launch (start us, length us, event | category | flops | bytes accessed | tf_op | source)
XLA Modules:
  0.0 1339.4 jit_solution(16350882350339564525)
XLA Ops:
  60.6 16.1 %collective-permute-done.5 = bf16[3072,128]{1,0:T(8,128)(2,1)S(1)} collective-permute-done((bf16[3072,128]{1,0:T(8,128)(2,1)S(1)}, bf16[3072,128]{1,0:T(8,128)(2,1)S(1)}, u32[]{:S(2)}, u32[]{:S(2)}) %collective-permute-start.5) | collective-permute-done | bytes 786464 | tf_op jit(solution)/shard_map/ppermute | solution.py:326
  80.7 12.0 collective-permute-done.44
  97.7 7.9 collective-permute-done.8
  107.0 26.9 %collective-permute-done.47 = bf16[1536,128]{1,0:T(8,128)(2,1)S(1)} collective-permute-done((bf16[1536,128]{1,0:T(8,128)(2,1)S(1)}, bf16[1536,128]{1,0:T(8,128)(2,1)S(1)}, u32[]{:S(2)}, u32[]{:S(2)}) %collective-permute-start.47) | collective-permute-done | bytes 393248 | tf_op jit(solution)/shard_map/ppermute | solution.py:326
  134.8 21.6 %collective-permute-done.46 = bf16[1536,128]{1,0:T(8,128)(2,1)S(1)} collective-permute-done((bf16[1536,128]{1,0:T(8,128)(2,1)S(1)}, bf16[1536,128]{1,0:T(8,128)(2,1)S(1)}, u32[]{:S(2)}, u32[]{:S(2)}) %collective-permute-start.46) | collective-permute-done | bytes 393248 | tf_op jit(solution)/shard_map/ppermute | solution.py:326
  162.5 20.3 %collective-permute-done.63 = bf16[1024,512]{1,0:T(8,128)(2,1)} collective-permute-done((bf16[1024,512]{1,0:T(8,128)(2,1)}, bf16[1024,512]{1,0:T(8,128)(2,1)}, u32[]{:S(2)}, u32[]{:S(2)}) %collective-permute-start.63) | collective-permute-done | bytes 1048608 | tf_op jit(solution)/shard_map/ppermute | solution.py:326
  185.6 16.9 %collective-permute-done.64 = bf16[512,1024]{1,0:T(8,128)(2,1)S(1)} collective-permute-done((bf16[512,1024]{1,0:T(8,128)(2,1)}, bf16[512,1024]{1,0:T(8,128)(2,1)S(1)}, u32[]{:S(2)}, u32[]{:S(2)}) %collective-permute-start.64) | collective-permute-done | bytes 1048608 | tf_op jit(solution)/shard_map/ppermute | solution.py:326
  212.6 5.7 collective-permute-done.35
  219.9 9.6 collective-permute-done.37
  229.5 11.2 collective-permute-done.67
  242.3 8.4 collective-permute-done.69
  254.6 8.8 collective-permute-done.70
  280.1 10.4 fusion.310
  290.5 7.8 fusion.35
  300.5 5.6 multiply_convert_fusion.21
  310.1 4.2 multiply_convert_fusion.17
  318.3 5.4 multiply_convert_fusion.20
  343.4 4.3 multiply_convert_fusion.14
  358.4 4.2 convolution_convert_fusion.2
  364.2 9.0 fusion.313
  373.3 7.8 fusion.41
  383.6 5.6 multiply_convert_fusion.7
  391.4 5.0 multiply_convert_fusion.13
  398.6 7.2 multiply_convert_fusion.9
  407.2 6.2 multiply_convert_fusion.11
  414.6 5.2 multiply_convert_fusion.6
  427.2 5.2 multiply_convert_fusion.12
  434.6 5.6 multiply_convert_fusion.8
  488.8 13.6 %multiply_reduce_fusion.1 = (f32[16,512]{1,0:T(8,128)S(1)}, f32[16,512,512]{1,2,0:T(8,128)}) fusion(f32[16,512,512]{1,2,0:T(8,128)} %get-tuple-element.346, f32[16,512]{1,0:T(8,128)S(1)} %get-tuple-element.345, bf16[512,16,64]{0,2,1:T(8,128)(2,1)} %bitcast.640, bf16[512,16,64]{0,2,1:T(8,128)(2,1)} %bitcast.639), kind=kOutput, calls=%fused_computation.9 | convolution fusion | flops 549445632 | bytes 35717120 | tf_op jit(solution)/shard_map/pqhe,pkhe->phqk/dot_general | solution.py:475
  505.8 8.3 multiply_convert_fusion.1
  520.2 9.3 convert_reduce_fusion.2
  578.0 11.7 multiply_reduce_fusion
  589.7 11.7 multiply_convert_fusion
  605.6 9.6 convert_reduce_fusion.4
  691.6 4.6 fusion.322
  701.2 110.5 %all-reduce.2.cloned.1.call-done = f32[2,12288]{1,0:T(2,128)} async-done(((f32[2,12288]{1,0:T(2,128)}), f32[2,12288]{1,0:T(2,128)}) %all-reduce.2.cloned.1.call-update) | async-done | bytes 98320 | tf_op jit(solution)/shard_map/psum | solution.py:618
  926.7 5.1 collective-permute-start.154
  933.4 5.2 collective-permute-done.154
  938.6 4.4 collective-permute-start.126
  944.2 4.4 collective-permute-start.113
  949.8 4.4 collective-permute-start.98
  955.4 4.4 collective-permute-start.85
  961.0 4.4 collective-permute-start.182
  966.7 4.4 collective-permute-start.169
  1014.5 32.6 %collective-permute-done.156 = bf16[1024,128]{1,0:T(8,128)(2,1)S(1)} collective-permute-done((bf16[1024,128]{1,0:T(8,128)(2,1)S(1)}, bf16[1024,128]{1,0:T(8,128)(2,1)S(1)}, u32[]{:S(2)}, u32[]{:S(2)}) %collective-permute-start.156) | collective-permute-done | bytes 262176 | tf_op jit(solution)/shard_map/ppermute | solution.py:366
  1048.4 5.7 collective-permute-done.128
  1055.5 4.3 collective-permute-done.100
  1067.3 7.3 collective-permute-done.192
  1079.1 6.7 collective-permute-done.233
  1102.5 10.0 collective-permute-done.209
  1115.4 8.4 collective-permute-done.206
  1126.5 9.2 collective-permute-done.230
  1138.5 7.7 collective-permute-done.234
  1149.2 8.2 collective-permute-done.196
  1159.5 9.2 collective-permute-done.193
  1173.2 6.7 collective-permute-done.224
  1181.2 7.6 collective-permute-done.221
  1194.5 4.4 collective-permute-start.225
  1201.5 15.5 %collective-permute-done.197 = bf16[1024,512]{1,0:T(8,128)(2,1)S(1)} collective-permute-done((bf16[1024,512]{1,0:T(8,128)(2,1)S(1)}, bf16[1024,512]{1,0:T(8,128)(2,1)S(1)}, u32[]{:S(2)}, u32[]{:S(2)}) %collective-permute-start.197) | collective-permute-done | bytes 1048608 | tf_op jit(solution)/shard_map/ppermute | solution.py:362
  1219.6 14.1 %collective-permute-done.225 = bf16[512,1024]{1,0:T(8,128)(2,1)S(1)} collective-permute-done((bf16[512,1024]{1,0:T(8,128)(2,1)S(1)}, bf16[512,1024]{1,0:T(8,128)(2,1)S(1)}, u32[]{:S(2)}, u32[]{:S(2)}) %collective-permute-start.225) | collective-permute-done | bytes 1048608 | tf_op jit(solution)/shard_map/ppermute | solution.py:362
  1241.1 20.6 %collective-permute-done.212 = bf16[1024,512]{1,0:T(8,128)(2,1)S(1)} collective-permute-done((bf16[1024,512]{1,0:T(8,128)(2,1)S(1)}, bf16[1024,512]{1,0:T(8,128)(2,1)S(1)}, u32[]{:S(2)}, u32[]{:S(2)}) %collective-permute-start.212) | collective-permute-done | bytes 1048608 | tf_op jit(solution)/shard_map/ppermute | solution.py:366
  1264.9 19.3 %collective-permute-done.240 = bf16[512,1024]{1,0:T(8,128)(2,1)S(1)} collective-permute-done((bf16[512,1024]{1,0:T(8,128)(2,1)S(1)}, bf16[512,1024]{1,0:T(8,128)(2,1)S(1)}, u32[]{:S(2)}, u32[]{:S(2)}) %collective-permute-start.240) | collective-permute-done | bytes 1048608 | tf_op jit(solution)/shard_map/ppermute | solution.py:366
  1288.3 18.3 %collective-permute-done.199 = bf16[1024,512]{1,0:T(8,128)(2,1)S(1)} collective-permute-done((bf16[1024,512]{1,0:T(8,128)(2,1)S(1)}, bf16[1024,512]{1,0:T(8,128)(2,1)S(1)}, u32[]{:S(2)}, u32[]{:S(2)}) %collective-permute-start.199) | collective-permute-done | bytes 1048608 | tf_op jit(solution)/shard_map/ppermute | solution.py:366
  1310.1 12.4 collective-permute-done.227
  (1475 shorter events, 611.2 us)
Async XLA Ops:
  7.2 804.5 %all-reduce.2.cloned.1.call-start = ((), (), s32[]{:S(2)}) async-start(), calls=%async_computation | async-start | bytes 196608 | tf_op jit(solution)/shard_map/psum | solution.py:618
  58.4 34.3 %collective-permute-start.44 = (bf16[3072,128]{1,0:T(8,128)(2,1)S(1)}, bf16[3072,128]{1,0:T(8,128)(2,1)S(1)}, u32[]{:S(2)}, u32[]{:S(2)}) collective-permute-start(bf16[3072,128]{1,0:T(8,128)(2,1)S(1)} %get-tuple-element.198), channel_id=1, source_target_pairs={{0,8},{4,12},{8,0},{12,4},{1,9},{5,13},{9,1},{13,5},{2,10},{6,14},... | collective-permute-start | bytes 2359304 | tf_op jit(solution)/shard_map/ppermute | solution.py:326
  60.0 35.1 %collective-permute-start.2 = (bf16[3072,128]{1,0:T(8,128)(2,1)S(1)}, bf16[3072,128]{1,0:T(8,128)(2,1)S(1)}, u32[]{:S(2)}, u32[]{:S(2)}) collective-permute-start(bf16[3072,128]{1,0:T(8,128)(2,1)S(1)} %get-tuple-element.199), channel_id=1, source_target_pairs={{0,16},{16,0},{1,17},{17,1},{2,18},{18,2},{3,19},{19,3},{4,20},{20... | collective-permute-start | bytes 2359304 | tf_op jit(solution)/shard_map/ppermute | solution.py:326
  60.1 36.7 %collective-permute-start.41 = (bf16[3072,128]{1,0:T(8,128)(2,1)S(1)}, bf16[3072,128]{1,0:T(8,128)(2,1)S(1)}, u32[]{:S(2)}, u32[]{:S(2)}) collective-permute-start(bf16[3072,128]{1,0:T(8,128)(2,1)S(1)} %get-tuple-element.198), channel_id=1, source_target_pairs={{0,16},{16,0},{1,17},{17,1},{2,18},{18,2},{3,19},{19,3},{4,20},{20... | collective-permute-start | bytes 2359304 | tf_op jit(solution)/shard_map/ppermute | solution.py:326
  77.3 28.3 %collective-permute-start.8 = (bf16[1536,128]{1,0:T(8,128)(2,1)S(1)}, bf16[1536,128]{1,0:T(8,128)(2,1)S(1)}, u32[]{:S(2)}, u32[]{:S(2)}) collective-permute-start(bf16[1536,128]{1,0:T(8,128)(2,1)S(1)} %slice.1248), channel_id=1, source_target_pairs={{0,4},{4,0},{8,12},{12,8},{1,5},{5,1},{9,13},{13,9},{2,6},{6,2},{1... | collective-permute-start | bytes 1179656 | tf_op jit(solution)/shard_map/ppermute | solution.py:326
  95.2 62.3 %collective-permute-start.31 = (bf16[1024,512]{1,0:T(8,128)(2,1)}, bf16[1024,512]{1,0:T(8,128)(2,1)S(1)}, u32[]{:S(2)}, u32[]{:S(2)}) collective-permute-start(bf16[1024,512]{1,0:T(8,128)(2,1)} %get-tuple-element.152), channel_id=1, source_target_pairs={{0,8},{4,12},{8,0},{12,4},{1,9},{5,13},{9,1},{13,5},{2,10},{6,14},... | collective-permute-start | bytes 3145736 | tf_op jit(solution)/shard_map/ppermute | solution.py:326
  96.8 61.2 %collective-permute-start.27 = (bf16[1024,512]{1,0:T(8,128)(2,1)}, bf16[1024,512]{1,0:T(8,128)(2,1)S(1)}, u32[]{:S(2)}, u32[]{:S(2)}) collective-permute-start(bf16[1024,512]{1,0:T(8,128)(2,1)} %get-tuple-element.152), channel_id=1, source_target_pairs={{0,4},{4,0},{8,12},{12,8},{1,5},{5,1},{9,13},{13,9},{2,6},{6,2},{1... | collective-permute-start | bytes 3145736 | tf_op jit(solution)/shard_map/ppermute | solution.py:326
  97.3 62.3 %collective-permute-start.32 = (bf16[512,1024]{1,0:T(8,128)(2,1)}, bf16[512,1024]{1,0:T(8,128)(2,1)S(1)}, u32[]{:S(2)}, u32[]{:S(2)}) collective-permute-start(bf16[512,1024]{1,0:T(8,128)(2,1)} %get-tuple-element.150), channel_id=1, source_target_pairs={{0,8},{4,12},{8,0},{12,4},{1,9},{5,13},{9,1},{13,5},{2,10},{6,14},... | collective-permute-start | bytes 3145736 | tf_op jit(solution)/shard_map/ppermute | solution.py:326
  105.6 28.4 %collective-permute-start.47 = (bf16[1536,128]{1,0:T(8,128)(2,1)S(1)}, bf16[1536,128]{1,0:T(8,128)(2,1)S(1)}, u32[]{:S(2)}, u32[]{:S(2)}) collective-permute-start(bf16[1536,128]{1,0:T(8,128)(2,1)S(1)} %slice.1298), channel_id=1, source_target_pairs={{0,4},{4,0},{8,12},{12,8},{1,5},{5,1},{9,13},{13,9},{2,6},{6,2},{1... | collective-permute-start | bytes 1179656 | tf_op jit(solution)/shard_map/ppermute | solution.py:326
  106.6 49.9 %collective-permute-start.46 = (bf16[1536,128]{1,0:T(8,128)(2,1)S(1)}, bf16[1536,128]{1,0:T(8,128)(2,1)S(1)}, u32[]{:S(2)}, u32[]{:S(2)}) collective-permute-start(bf16[1536,128]{1,0:T(8,128)(2,1)S(1)} %slice.1296), channel_id=1, source_target_pairs={{0,8},{4,12},{8,0},{12,4},{1,9},{5,13},{9,1},{13,5},{2,10},{6,14},... | collective-permute-start | bytes 1179656 | tf_op jit(solution)/shard_map/ppermute | solution.py:326
  133.9 27.5 %collective-permute-start.28 = (bf16[512,1024]{1,0:T(8,128)(2,1)}, bf16[512,1024]{1,0:T(8,128)(2,1)S(1)}, u32[]{:S(2)}, u32[]{:S(2)}) collective-permute-start(bf16[512,1024]{1,0:T(8,128)(2,1)} %get-tuple-element.150), channel_id=1, source_target_pairs={{0,4},{4,0},{8,12},{12,8},{1,5},{5,1},{9,13},{13,9},{2,6},{6,2},{1... | collective-permute-start | bytes 3145736 | tf_op jit(solution)/shard_map/ppermute | solution.py:326
  156.4 26.4 %collective-permute-start.63 = (bf16[1024,512]{1,0:T(8,128)(2,1)}, bf16[1024,512]{1,0:T(8,128)(2,1)}, u32[]{:S(2)}, u32[]{:S(2)}) collective-permute-start(bf16[1024,512]{1,0:T(8,128)(2,1)} %get-tuple-element.151), channel_id=1, source_target_pairs={{0,8},{4,12},{8,0},{12,4},{1,9},{5,13},{9,1},{13,5},{2,10},{6,14},... | collective-permute-start | bytes 3145736 | tf_op jit(solution)/shard_map/ppermute | solution.py:326
  157.5 27.5 %collective-permute-start.59 = (bf16[1024,512]{1,0:T(8,128)(2,1)}, bf16[1024,512]{1,0:T(8,128)(2,1)S(1)}, u32[]{:S(2)}, u32[]{:S(2)}) collective-permute-start(bf16[1024,512]{1,0:T(8,128)(2,1)} %get-tuple-element.151), channel_id=1, source_target_pairs={{0,4},{4,0},{8,12},{12,8},{1,5},{5,1},{9,13},{13,9},{2,6},{6,2},{1... | collective-permute-start | bytes 3145736 | tf_op jit(solution)/shard_map/ppermute | solution.py:326
  158.0 44.6 %collective-permute-start.64 = (bf16[512,1024]{1,0:T(8,128)(2,1)}, bf16[512,1024]{1,0:T(8,128)(2,1)S(1)}, u32[]{:S(2)}, u32[]{:S(2)}) collective-permute-start(bf16[512,1024]{1,0:T(8,128)(2,1)} %get-tuple-element.149), channel_id=1, source_target_pairs={{0,8},{4,12},{8,0},{12,4},{1,9},{5,13},{9,1},{13,5},{2,10},{6,14},... | collective-permute-start | bytes 3145736 | tf_op jit(solution)/shard_map/ppermute | solution.py:326
  159.6 43.8 %collective-permute-start.60 = (bf16[512,1024]{1,0:T(8,128)(2,1)}, bf16[512,1024]{1,0:T(8,128)(2,1)S(1)}, u32[]{:S(2)}, u32[]{:S(2)}) collective-permute-start(bf16[512,1024]{1,0:T(8,128)(2,1)} %get-tuple-element.149), channel_id=1, source_target_pairs={{0,4},{4,0},{8,12},{12,8},{1,5},{5,1},{9,13},{13,9},{2,6},{6,2},{1... | collective-permute-start | bytes 3145736 | tf_op jit(solution)/shard_map/ppermute | solution.py:326
  161.4 42.4 %collective-permute-start.4 = (bf16[3072,128]{1,0:T(8,128)(2,1)S(1)}, bf16[3072,128]{1,0:T(8,128)(2,1)S(1)}, u32[]{:S(2)}, u32[]{:S(2)}) collective-permute-start(bf16[3072,128]{1,0:T(8,128)(2,1)S(1)} %collective-permute-done.3), channel_id=1, source_target_pairs={{0,16},{16,0},{1,17},{17,1},{2,18},{18,2},{3,19},{19,3},{4,20},{20... | collective-permute-start | bytes 2359304 | tf_op jit(solution)/shard_map/ppermute | solution.py:326
  203.9 49.0 %collective-permute-start.36 = (bf16[512,512]{1,0:T(8,128)(2,1)S(1)}, bf16[512,512]{1,0:T(8,128)(2,1)S(1)}, u32[]{:S(2)}, u32[]{:S(2)}) collective-permute-start(bf16[512,512]{1,0:T(8,128)(2,1)S(1)} %slice.1282), channel_id=1, source_target_pairs={{0,8},{4,12},{8,0},{12,4},{1,9},{5,13},{9,1},{13,5},{2,10},{6,14},... | collective-permute-start | bytes 1572872 | tf_op jit(solution)/shard_map/ppermute | solution.py:326
  208.1 32.6 %collective-permute-start.67 = (bf16[512,512]{1,0:T(8,128)(2,1)S(1)}, bf16[512,512]{1,0:T(8,128)(2,1)S(1)}, u32[]{:S(2)}, u32[]{:S(2)}) collective-permute-start(bf16[512,512]{1,0:T(8,128)(2,1)S(1)} %slice.1331), channel_id=1, source_target_pairs={{0,4},{4,0},{8,12},{12,8},{1,5},{5,1},{9,13},{13,9},{2,6},{6,2},{1... | collective-permute-start | bytes 1572872 | tf_op jit(solution)/shard_map/ppermute | solution.py:326
  209.3 41.4 %collective-permute-start.69 = (bf16[256,1024]{1,0:T(8,128)(2,1)S(1)}, bf16[256,1024]{1,0:T(8,128)(2,1)S(1)}, u32[]{:S(2)}, u32[]{:S(2)}) collective-permute-start(bf16[256,1024]{1,0:T(8,128)(2,1)S(1)} %slice.1334), channel_id=1, source_target_pairs={{0,4},{4,0},{8,12},{12,8},{1,5},{5,1},{9,13},{13,9},{2,6},{6,2},{1... | collective-permute-start | bytes 1572872 | tf_op jit(solution)/shard_map/ppermute | solution.py:326
  218.3 34.8 %collective-permute-start.38 = (bf16[256,1024]{1,0:T(8,128)(2,1)S(1)}, bf16[256,1024]{1,0:T(8,128)(2,1)S(1)}, u32[]{:S(2)}, u32[]{:S(2)}) collective-permute-start(bf16[256,1024]{1,0:T(8,128)(2,1)S(1)} %slice.1285), channel_id=1, source_target_pairs={{0,8},{4,12},{8,0},{12,4},{1,9},{5,13},{9,1},{13,5},{2,10},{6,14},... | collective-permute-start | bytes 1572872 | tf_op jit(solution)/shard_map/ppermute | solution.py:326
  229.5 34.7 %collective-permute-start.9 = (bf16[3072,128]{1,0:T(8,128)(2,1)S(1)}, bf16[3072,128]{1,0:T(8,128)(2,1)S(1)}, u32[]{:S(2)}, u32[]{:S(2)}) collective-permute-start(bf16[3072,128]{1,0:T(8,128)(2,1)S(1)} %constant_dynamic-update-slice_fusion), channel_id=1, source_target_pairs={{0,16},{16,0},{1,17},{17,1},{2,18},{18,2},{3,19},{19,3},{4,20},{20... | collective-permute-start | bytes 2359304 | tf_op jit(solution)/shard_map/ppermute | solution.py:326
  252.9 65.3 %collective-permute-start.25 = (bf16[1024,512]{1,0:T(8,128)(2,1)}, bf16[1024,512]{1,0:T(8,128)(2,1)}, u32[]{:S(2)}, u32[]{:S(2)}) collective-permute-start(bf16[1024,512]{1,0:T(8,128)(2,1)} %get-tuple-element.152), channel_id=1, source_target_pairs={{0,16},{16,0},{1,17},{17,1},{2,18},{18,2},{3,19},{19,3},{4,20},{20... | collective-permute-start | bytes 3145736 | tf_op jit(solution)/shard_map/ppermute | solution.py:326
  253.1 75.6 %collective-permute-start.26 = (bf16[512,1024]{1,0:T(8,128)(2,1)}, bf16[512,1024]{1,0:T(8,128)(2,1)}, u32[]{:S(2)}, u32[]{:S(2)}) collective-permute-start(bf16[512,1024]{1,0:T(8,128)(2,1)} %get-tuple-element.150), channel_id=1, source_target_pairs={{0,16},{16,0},{1,17},{17,1},{2,18},{18,2},{3,19},{19,3},{4,20},{20... | collective-permute-start | bytes 3145736 | tf_op jit(solution)/shard_map/ppermute | solution.py:326
  253.7 173.5 %collective-permute-start.57 = (bf16[1024,512]{1,0:T(8,128)(2,1)}, bf16[1024,512]{1,0:T(8,128)(2,1)}, u32[]{:S(2)}, u32[]{:S(2)}) collective-permute-start(bf16[1024,512]{1,0:T(8,128)(2,1)} %get-tuple-element.151), channel_id=1, source_target_pairs={{0,16},{16,0},{1,17},{17,1},{2,18},{18,2},{3,19},{19,3},{4,20},{20... | collective-permute-start | bytes 3145736 | tf_op jit(solution)/shard_map/ppermute | solution.py:326
  263.4 169.0 %collective-permute-start.58 = (bf16[512,1024]{1,0:T(8,128)(2,1)}, bf16[512,1024]{1,0:T(8,128)(2,1)}, u32[]{:S(2)}, u32[]{:S(2)}) collective-permute-start(bf16[512,1024]{1,0:T(8,128)(2,1)} %get-tuple-element.149), channel_id=1, source_target_pairs={{0,16},{16,0},{1,17},{17,1},{2,18},{18,2},{3,19},{19,3},{4,20},{20... | collective-permute-start | bytes 3145736 | tf_op jit(solution)/shard_map/ppermute | solution.py:326
  264.3 67.0 %collective-permute-start.48 = (bf16[3072,128]{1,0:T(8,128)(2,1)}, bf16[3072,128]{1,0:T(8,128)(2,1)}, u32[]{:S(2)}, u32[]{:S(2)}) collective-permute-start(bf16[3072,128]{1,0:T(8,128)(2,1)} %constant_dynamic-update-slice_fusion.15), channel_id=1, source_target_pairs={{0,16},{16,0},{1,17},{17,1},{2,18},{18,2},{3,19},{19,3},{4,20},{20... | collective-permute-start | bytes 2359304 | tf_op jit(solution)/shard_map/ppermute | solution.py:326
  343.2 91.4 %collective-permute-start.65 = (bf16[1024,512]{1,0:T(8,128)(2,1)}, bf16[1024,512]{1,0:T(8,128)(2,1)}, u32[]{:S(2)}, u32[]{:S(2)}) collective-permute-start(bf16[1024,512]{1,0:T(8,128)(2,1)} %collective-permute-done.63), channel_id=1, source_target_pairs={{0,16},{16,0},{1,17},{17,1},{2,18},{18,2},{3,19},{19,3},{4,20},{20... | collective-permute-start | bytes 3145736 | tf_op jit(solution)/shard_map/ppermute | solution.py:326
  347.7 66.4 %collective-permute-start.71 = (bf16[1024,512]{1,0:T(8,128)(2,1)}, bf16[1024,512]{1,0:T(8,128)(2,1)}, u32[]{:S(2)}, u32[]{:S(2)}) collective-permute-start(bf16[1024,512]{1,0:T(8,128)(2,1)} %constant_dynamic-update-slice_fusion.26), channel_id=1, source_target_pairs={{0,16},{16,0},{1,17},{17,1},{2,18},{18,2},{3,19},{19,3},{4,20},{20... | collective-permute-start | bytes 3145736 | tf_op jit(solution)/shard_map/ppermute | solution.py:326
  348.9 70.9 %collective-permute-start.72 = (bf16[512,1024]{1,0:T(8,128)(2,1)}, bf16[512,1024]{1,0:T(8,128)(2,1)}, u32[]{:S(2)}, u32[]{:S(2)}) collective-permute-start(bf16[512,1024]{1,0:T(8,128)(2,1)} %constant_dynamic-update-slice_fusion.28), channel_id=1, source_target_pairs={{0,16},{16,0},{1,17},{17,1},{2,18},{18,2},{3,19},{19,3},{4,20},{20... | collective-permute-start | bytes 3145736 | tf_op jit(solution)/shard_map/ppermute | solution.py:326
  667.2 332.5 %collective-permute-start.73 = (bf16[512,1024]{1,0:T(8,128)(2,1)}, bf16[512,1024]{1,0:T(8,128)(2,1)}, u32[]{:S(2)}, u32[]{:S(2)}) collective-permute-start(bf16[512,1024]{1,0:T(8,128)(2,1)} %get-tuple-element.148), channel_id=1, source_target_pairs={{0,16},{16,0},{1,17},{17,1},{2,18},{18,2},{3,19},{19,3},{4,20},{20... | collective-permute-start | bytes 3145736 | tf_op jit(solution)/shard_map/ppermute | solution.py:326
  675.8 140.2 %collective-permute-start.148 = (bf16[1024,128]{1,0:T(8,128)(2,1)}, bf16[1024,128]{1,0:T(8,128)(2,1)S(1)}, u32[]{:S(2)}, u32[]{:S(2)}) collective-permute-start(bf16[1024,128]{1,0:T(8,128)(2,1)} %get-tuple-element.194), channel_id=1, source_target_pairs={{0,16},{16,0},{1,17},{17,1},{2,18},{18,2},{3,19},{19,3},{4,20},{20... | collective-permute-start | bytes 786440 | tf_op jit(solution)/shard_map/ppermute | solution.py:326
  676.1 139.8 %collective-permute-start.147 = (bf16[1024,128]{1,0:T(8,128)(2,1)}, bf16[1024,128]{1,0:T(8,128)(2,1)}, u32[]{:S(2)}, u32[]{:S(2)}) collective-permute-start(bf16[1024,128]{1,0:T(8,128)(2,1)} %get-tuple-element.195), channel_id=1, source_target_pairs={{0,16},{16,0},{1,17},{17,1},{2,18},{18,2},{3,19},{19,3},{4,20},{20... | collective-permute-start | bytes 786440 | tf_op jit(solution)/shard_map/ppermute | solution.py:326
  676.3 140.2 %collective-permute-start.145 = (bf16[1024,128]{1,0:T(8,128)(2,1)}, bf16[1024,128]{1,0:T(8,128)(2,1)}, u32[]{:S(2)}, u32[]{:S(2)}) collective-permute-start(bf16[1024,128]{1,0:T(8,128)(2,1)} %get-tuple-element.196), channel_id=1, source_target_pairs={{0,16},{16,0},{1,17},{17,1},{2,18},{18,2},{3,19},{19,3},{4,20},{20... | collective-permute-start | bytes 786440 | tf_op jit(solution)/shard_map/ppermute | solution.py:326
  676.7 139.9 %collective-permute-start.144 = (bf16[1024,128]{1,0:T(8,128)(2,1)}, bf16[1024,128]{1,0:T(8,128)(2,1)}, u32[]{:S(2)}, u32[]{:S(2)}) collective-permute-start(bf16[1024,128]{1,0:T(8,128)(2,1)} %get-tuple-element.197), channel_id=1, source_target_pairs={{0,16},{16,0},{1,17},{17,1},{2,18},{18,2},{3,19},{19,3},{4,20},{20... | collective-permute-start | bytes 786440 | tf_op jit(solution)/shard_map/ppermute | solution.py:326
  834.4 46.9 %collective-permute-start.146 = (bf16[512,128]{1,0:T(8,128)(2,1)S(1)}, bf16[512,128]{1,0:T(8,128)(2,1)S(1)}, u32[]{:S(2)}, u32[]{:S(2)}) collective-permute-start(bf16[512,128]{1,0:T(8,128)(2,1)S(1)} %slice.1850), channel_id=1, source_target_pairs={{0,4},{4,0},{8,12},{12,8},{1,5},{5,1},{9,13},{13,9},{2,6},{6,2},{1... | collective-permute-start | bytes 393224 | tf_op jit(solution)/shard_map/ppermute | solution.py:326
  834.9 47.3 %collective-permute-start.153 = (bf16[512,128]{1,0:T(8,128)(2,1)S(1)}, bf16[512,128]{1,0:T(8,128)(2,1)S(1)}, u32[]{:S(2)}, u32[]{:S(2)}) collective-permute-start(bf16[512,128]{1,0:T(8,128)(2,1)S(1)} %slice.1849), channel_id=1, source_target_pairs={{0,8},{4,12},{8,0},{12,4},{1,9},{5,13},{9,1},{13,5},{2,10},{6,14},... | collective-permute-start | bytes 393224 | tf_op jit(solution)/shard_map/ppermute | solution.py:326
  924.1 52.0 %collective-permute-start.200 = (bf16[1024,512]{1,0:T(8,128)(2,1)S(1)}, bf16[1024,512]{1,0:T(8,128)(2,1)S(1)}, u32[]{:S(2)}, u32[]{:S(2)}) collective-permute-start(bf16[1024,512]{1,0:T(8,128)(2,1)S(1)} %copy-done.261), channel_id=1, source_target_pairs={{0,16},{16,0},{1,17},{17,1},{2,18},{18,2},{3,19},{19,3},{4,20},{20... | collective-permute-start | bytes 3145736 | tf_op jit(solution)/shard_map/ppermute | solution.py:326
  925.3 52.2 %collective-permute-start.203 = (bf16[1024,512]{1,0:T(8,128)(2,1)S(1)}, bf16[1024,512]{1,0:T(8,128)(2,1)S(1)}, u32[]{:S(2)}, u32[]{:S(2)}) collective-permute-start(bf16[1024,512]{1,0:T(8,128)(2,1)S(1)} %copy-done.260), channel_id=1, source_target_pairs={{0,16},{16,0},{1,17},{17,1},{2,18},{18,2},{3,19},{19,3},{4,20},{20... | collective-permute-start | bytes 3145736 | tf_op jit(solution)/shard_map/ppermute | solution.py:326
  1009.1 55.0 %collective-permute-start.205 = (bf16[512,512]{1,0:T(8,128)(2,1)S(1)}, bf16[512,512]{1,0:T(8,128)(2,1)S(1)}, u32[]{:S(2)}, u32[]{:S(2)}) collective-permute-start(bf16[512,512]{1,0:T(8,128)(2,1)S(1)} %get-tuple-element.208), channel_id=1, source_target_pairs={{0,4},{4,0},{8,12},{12,8},{1,5},{5,1},{9,13},{13,9},{2,6},{6,2},{1... | collective-permute-start | bytes 1572872 | tf_op jit(solution)/shard_map/ppermute | solution.py:326
  1010.1 89.8 %collective-permute-start.202 = (bf16[512,512]{1,0:T(8,128)(2,1)S(1)}, bf16[512,512]{1,0:T(8,128)(2,1)S(1)}, u32[]{:S(2)}, u32[]{:S(2)}) collective-permute-start(bf16[512,512]{1,0:T(8,128)(2,1)S(1)} %slice.1842), channel_id=1, source_target_pairs={{0,4},{4,0},{8,12},{12,8},{1,5},{5,1},{9,13},{13,9},{2,6},{6,2},{1... | collective-permute-start | bytes 1572872 | tf_op jit(solution)/shard_map/ppermute | solution.py:326
  1011.4 54.1 %collective-permute-start.207 = (bf16[512,512]{1,0:T(8,128)(2,1)S(1)}, bf16[512,512]{1,0:T(8,128)(2,1)S(1)}, u32[]{:S(2)}, u32[]{:S(2)}) collective-permute-start(bf16[512,512]{1,0:T(8,128)(2,1)S(1)} %get-tuple-element.209), channel_id=1, source_target_pairs={{0,8},{4,12},{8,0},{12,4},{1,9},{5,13},{9,1},{13,5},{2,10},{6,14},... | collective-permute-start | bytes 1572872 | tf_op jit(solution)/shard_map/ppermute | solution.py:326
  1011.7 35.4 %collective-permute-start.156 = (bf16[1024,128]{1,0:T(8,128)(2,1)S(1)}, bf16[1024,128]{1,0:T(8,128)(2,1)S(1)}, u32[]{:S(2)}, u32[]{:S(2)}) collective-permute-start(bf16[1024,128]{1,0:T(8,128)(2,1)S(1)} %add_convert_fusion.44), channel_id=1, source_target_pairs={{1,0},{2,3},{5,4},{6,7},{9,8},{10,11},{13,12},{14,15},{17,16},{18,... | collective-permute-start | bytes 786440 | tf_op jit(solution)/shard_map/ppermute | solution.py:366
  1013.1 41.0 %collective-permute-start.128 = (bf16[1024,128]{1,0:T(8,128)(2,1)S(1)}, bf16[1024,128]{1,0:T(8,128)(2,1)S(1)}, u32[]{:S(2)}, u32[]{:S(2)}) collective-permute-start(bf16[1024,128]{1,0:T(8,128)(2,1)S(1)} %add_convert_fusion.48), channel_id=1, source_target_pairs={{1,0},{2,3},{5,4},{6,7},{9,8},{10,11},{13,12},{14,15},{17,16},{18,... | collective-permute-start | bytes 786440 | tf_op jit(solution)/shard_map/ppermute | solution.py:366
  1074.6 24.5 %collective-permute-start.220 = (bf16[256,1024]{1,0:T(8,128)(2,1)S(1)}, bf16[256,1024]{1,0:T(8,128)(2,1)S(1)}, u32[]{:S(2)}, u32[]{:S(2)}) collective-permute-start(bf16[256,1024]{1,0:T(8,128)(2,1)S(1)} %get-tuple-element.202), channel_id=1, source_target_pairs={{0,4},{4,0},{8,12},{12,8},{1,5},{5,1},{9,13},{13,9},{2,6},{6,2},{1... | collective-permute-start | bytes 1572872 | tf_op jit(solution)/shard_map/ppermute | solution.py:326
  1099.2 24.6 %collective-permute-start.206 = (bf16[512,512]{1,0:T(8,128)(2,1)S(1)}, bf16[512,512]{1,0:T(8,128)(2,1)S(1)}, u32[]{:S(2)}, u32[]{:S(2)}) collective-permute-start(bf16[512,512]{1,0:T(8,128)(2,1)S(1)} %fusion.78), channel_id=1, source_target_pairs={{0,8},{4,12},{8,0},{12,4},{1,9},{5,13},{9,1},{13,5},{2,10},{6,14},... | collective-permute-start | bytes 1572872 | tf_op jit(solution)/shard_map/ppermute | solution.py:326
  1113.9 32.4 %collective-permute-start.234 = (bf16[256,1024]{1,0:T(8,128)(2,1)S(1)}, bf16[256,1024]{1,0:T(8,128)(2,1)S(1)}, u32[]{:S(2)}, u32[]{:S(2)}) collective-permute-start(bf16[256,1024]{1,0:T(8,128)(2,1)S(1)} %fusion.66), channel_id=1, source_target_pairs={{0,8},{4,12},{8,0},{12,4},{1,9},{5,13},{9,1},{13,5},{2,10},{6,14},... | collective-permute-start | bytes 1572872 | tf_op jit(solution)/shard_map/ppermute | solution.py:326
  1137.0 31.7 %collective-permute-start.193 = (bf16[512,512]{1,0:T(8,128)(2,1)S(1)}, bf16[512,512]{1,0:T(8,128)(2,1)S(1)}, u32[]{:S(2)}, u32[]{:S(2)}) collective-permute-start(bf16[512,512]{1,0:T(8,128)(2,1)S(1)} %fusion.84), channel_id=1, source_target_pairs={{0,8},{4,12},{8,0},{12,4},{1,9},{5,13},{9,1},{13,5},{2,10},{6,14},... | collective-permute-start | bytes 1572872 | tf_op jit(solution)/shard_map/ppermute | solution.py:326
  1158.2 30.7 %collective-permute-start.221 = (bf16[256,1024]{1,0:T(8,128)(2,1)S(1)}, bf16[256,1024]{1,0:T(8,128)(2,1)S(1)}, u32[]{:S(2)}, u32[]{:S(2)}) collective-permute-start(bf16[256,1024]{1,0:T(8,128)(2,1)S(1)} %fusion.72), channel_id=1, source_target_pairs={{0,8},{4,12},{8,0},{12,4},{1,9},{5,13},{9,1},{13,5},{2,10},{6,14},... | collective-permute-start | bytes 1572872 | tf_op jit(solution)/shard_map/ppermute | solution.py:326
  1169.5 25.0 %collective-permute-start.238 = (bf16[512,1024]{1,0:T(8,128)(2,1)S(1)}, bf16[512,1024]{1,0:T(8,128)(2,1)S(1)}, u32[]{:S(2)}, u32[]{:S(2)}) collective-permute-start(bf16[512,1024]{1,0:T(8,128)(2,1)S(1)} %pad_maximum_fusion.3), channel_id=1, source_target_pairs={{0,1},{3,2},{4,5},{7,6},{8,9},{11,10},{12,13},{15,14},{16,17},{19,... | collective-permute-start | bytes 3145736 | tf_op jit(solution)/shard_map/ppermute | solution.py:362
  1171.5 45.5 %collective-permute-start.197 = (bf16[1024,512]{1,0:T(8,128)(2,1)S(1)}, bf16[1024,512]{1,0:T(8,128)(2,1)S(1)}, u32[]{:S(2)}, u32[]{:S(2)}) collective-permute-start(bf16[1024,512]{1,0:T(8,128)(2,1)S(1)} %pad_maximum_fusion), channel_id=1, source_target_pairs={{0,1},{3,2},{4,5},{7,6},{8,9},{11,10},{12,13},{15,14},{16,17},{19,... | collective-permute-start | bytes 3145736 | tf_op jit(solution)/shard_map/ppermute | solution.py:362
  1190.1 28.5 %collective-permute-start.211 = (bf16[1024,512]{1,0:T(8,128)(2,1)S(1)}, bf16[1024,512]{1,0:T(8,128)(2,1)S(1)}, u32[]{:S(2)}, u32[]{:S(2)}) collective-permute-start(bf16[1024,512]{1,0:T(8,128)(2,1)S(1)} %add_convert_fusion.7), channel_id=1, source_target_pairs={{1,2},{2,1},{5,6},{6,5},{9,10},{10,9},{13,14},{14,13},{17,18},{18,... | collective-permute-start | bytes 3145736 | tf_op jit(solution)/shard_map/ppermute | solution.py:364
  1194.5 39.2 %collective-permute-start.225 = (bf16[512,1024]{1,0:T(8,128)(2,1)S(1)}, bf16[512,1024]{1,0:T(8,128)(2,1)S(1)}, u32[]{:S(2)}, u32[]{:S(2)}) collective-permute-start(bf16[512,1024]{1,0:T(8,128)(2,1)S(1)} %pad_maximum_fusion.2), channel_id=1, source_target_pairs={{0,1},{3,2},{4,5},{7,6},{8,9},{11,10},{12,13},{15,14},{16,17},{19,... | collective-permute-start | bytes 3145736 | tf_op jit(solution)/shard_map/ppermute | solution.py:362
  1199.4 37.4 %collective-permute-start.171 = (bf16[128,1024]{1,0:T(8,128)(2,1)S(1)}, bf16[128,1024]{1,0:T(8,128)(2,1)S(1)}, u32[]{:S(2)}, u32[]{:S(2)}) collective-permute-start(bf16[128,1024]{1,0:T(8,128)(2,1)S(1)} %add_convert_fusion.42), channel_id=1, source_target_pairs={{1,0},{2,3},{5,4},{6,7},{9,8},{10,11},{13,12},{14,15},{17,16},{18,... | collective-permute-start | bytes 786440 | tf_op jit(solution)/shard_map/ppermute | solution.py:366
  1200.7 34.9 %collective-permute-start.239 = (bf16[512,1024]{1,0:T(8,128)(2,1)S(1)}, bf16[512,1024]{1,0:T(8,128)(2,1)S(1)}, u32[]{:S(2)}, u32[]{:S(2)}) collective-permute-start(bf16[512,1024]{1,0:T(8,128)(2,1)S(1)} %add_convert_fusion.1), channel_id=1, source_target_pairs={{1,2},{2,1},{5,6},{6,5},{9,10},{10,9},{13,14},{14,13},{17,18},{18,... | collective-permute-start | bytes 3145736 | tf_op jit(solution)/shard_map/ppermute | solution.py:364
  1233.7 28.0 %collective-permute-start.212 = (bf16[1024,512]{1,0:T(8,128)(2,1)S(1)}, bf16[1024,512]{1,0:T(8,128)(2,1)S(1)}, u32[]{:S(2)}, u32[]{:S(2)}) collective-permute-start(bf16[1024,512]{1,0:T(8,128)(2,1)S(1)} %add_convert_fusion.6), channel_id=1, source_target_pairs={{1,0},{2,3},{5,4},{6,7},{9,8},{10,11},{13,12},{14,15},{17,16},{18,... | collective-permute-start | bytes 3145736 | tf_op jit(solution)/shard_map/ppermute | solution.py:366
  1235.6 27.5 %collective-permute-start.226 = (bf16[512,1024]{1,0:T(8,128)(2,1)S(1)}, bf16[512,1024]{1,0:T(8,128)(2,1)S(1)}, u32[]{:S(2)}, u32[]{:S(2)}) collective-permute-start(bf16[512,1024]{1,0:T(8,128)(2,1)S(1)} %add_convert_fusion.4), channel_id=1, source_target_pairs={{1,2},{2,1},{5,6},{6,5},{9,10},{10,9},{13,14},{14,13},{17,18},{18,... | collective-permute-start | bytes 3145736 | tf_op jit(solution)/shard_map/ppermute | solution.py:364
  1236.8 48.8 %collective-permute-start.158 = (bf16[1024,128]{1,0:T(8,128)(2,1)S(1)}, bf16[1024,128]{1,0:T(8,128)(2,1)S(1)}, u32[]{:S(2)}, u32[]{:S(2)}) collective-permute-start(bf16[1024,128]{1,0:T(8,128)(2,1)S(1)} %get-tuple-element.67), channel_id=1, source_target_pairs={{16,0},{17,1},{18,2},{19,3},{20,4},{21,5},{22,6},{23,7},{24,8},{25... | collective-permute-start | bytes 786440 | tf_op jit(solution)/shard_map/ppermute | solution.py:599
  1238.1 46.0 %collective-permute-start.240 = (bf16[512,1024]{1,0:T(8,128)(2,1)S(1)}, bf16[512,1024]{1,0:T(8,128)(2,1)S(1)}, u32[]{:S(2)}, u32[]{:S(2)}) collective-permute-start(bf16[512,1024]{1,0:T(8,128)(2,1)S(1)} %add_convert_fusion), channel_id=1, source_target_pairs={{1,0},{2,3},{5,4},{6,7},{9,8},{10,11},{13,12},{14,15},{17,16},{18,... | collective-permute-start | bytes 3145736 | tf_op jit(solution)/shard_map/ppermute | solution.py:366
  1239.5 47.5 %collective-permute-start.130 = (bf16[1024,128]{1,0:T(8,128)(2,1)S(1)}, bf16[1024,128]{1,0:T(8,128)(2,1)S(1)}, u32[]{:S(2)}, u32[]{:S(2)}) collective-permute-start(bf16[1024,128]{1,0:T(8,128)(2,1)S(1)} %get-tuple-element.65), channel_id=1, source_target_pairs={{16,0},{17,1},{18,2},{19,3},{20,4},{21,5},{22,6},{23,7},{24,8},{25... | collective-permute-start | bytes 786440 | tf_op jit(solution)/shard_map/ppermute | solution.py:599
  1261.7 44.9 %collective-permute-start.199 = (bf16[1024,512]{1,0:T(8,128)(2,1)S(1)}, bf16[1024,512]{1,0:T(8,128)(2,1)S(1)}, u32[]{:S(2)}, u32[]{:S(2)}) collective-permute-start(bf16[1024,512]{1,0:T(8,128)(2,1)S(1)} %add_convert_fusion.9), channel_id=1, source_target_pairs={{1,0},{2,3},{5,4},{6,7},{9,8},{10,11},{13,12},{14,15},{17,16},{18,... | collective-permute-start | bytes 3145736 | tf_op jit(solution)/shard_map/ppermute | solution.py:366
  1263.1 44.8 %collective-permute-start.213 = (bf16[1024,512]{1,0:T(8,128)(2,1)S(1)}, bf16[1024,512]{1,0:T(8,128)(2,1)S(1)}, u32[]{:S(2)}, u32[]{:S(2)}) collective-permute-start(bf16[1024,512]{1,0:T(8,128)(2,1)S(1)} %broadcast_select_fusion.2), channel_id=1, source_target_pairs={{0,16},{1,17},{2,18},{3,19},{4,20},{5,21},{6,22},{7,23},{8,24},{9,... | collective-permute-start | bytes 3145736 | tf_op jit(solution)/shard_map/ppermute | solution.py:598
  1284.2 38.4 %collective-permute-start.227 = (bf16[512,1024]{1,0:T(8,128)(2,1)S(1)}, bf16[512,1024]{1,0:T(8,128)(2,1)S(1)}, u32[]{:S(2)}, u32[]{:S(2)}) collective-permute-start(bf16[512,1024]{1,0:T(8,128)(2,1)S(1)} %add_convert_fusion.3), channel_id=1, source_target_pairs={{1,0},{2,3},{5,4},{6,7},{9,8},{10,11},{13,12},{14,15},{17,16},{18,... | collective-permute-start | bytes 3145736 | tf_op jit(solution)/shard_map/ppermute | solution.py:366
  1285.6 36.9 %collective-permute-start.241 = (bf16[512,1024]{1,0:T(8,128)(2,1)S(1)}, bf16[512,1024]{1,0:T(8,128)(2,1)S(1)}, u32[]{:S(2)}, u32[]{:S(2)}) collective-permute-start(bf16[512,1024]{1,0:T(8,128)(2,1)S(1)} %broadcast_select_fusion), channel_id=1, source_target_pairs={{0,16},{1,17},{2,18},{3,19},{4,20},{5,21},{6,22},{7,23},{8,24},{9,... | collective-permute-start | bytes 3145736 | tf_op jit(solution)/shard_map/ppermute | solution.py:598
  1287.0 38.1 %collective-permute-start.102 = (bf16[1024,128]{1,0:T(8,128)(2,1)S(1)}, bf16[1024,128]{1,0:T(8,128)(2,1)S(1)}, u32[]{:S(2)}, u32[]{:S(2)}) collective-permute-start(bf16[1024,128]{1,0:T(8,128)(2,1)S(1)} %get-tuple-element.63), channel_id=1, source_target_pairs={{16,0},{17,1},{18,2},{19,3},{20,4},{21,5},{22,6},{23,7},{24,8},{25... | collective-permute-start | bytes 786440 | tf_op jit(solution)/shard_map/ppermute | solution.py:599
  (473 other events, 4034.8 us)
Sparse Core Ops, SparseCore 0:
  691.7 119.9 all-reduce.1

commit v2 on v0

--- a/solution.py
+++ b/solution.py
@@ -1,9 +1,12 @@
+import functools
 from functools import partial
 import math
 
 import jax
 import jax.numpy as jnp
 from jax import lax
+from jax.experimental import pallas as pl
+from jax.experimental.pallas import tpu as pltpu
 from jax.sharding import PartitionSpec as P
 
 HEAD_DIM = 64
@@ -204,7 +207,7 @@
     return (grad_in, matrix_grads, vector_grads)
 
 
-def on_device(
+def pipelined(
     token_in,
     cotangent,
     w_qkv,
@@ -320,6 +323,891 @@
         gain_part[None],
         shift_part[None],
     )
+
+
+MESH = pl.DeviceIdType.MESH
+
+
+def low(value):
+    return value.astype(jnp.bfloat16)
+
+
+def high(value):
+    return value.astype(jnp.float32)
+
+
+def remote(src, dst, send, recv, device):
+    return pltpu.make_async_remote_copy(
+        src_ref=src, dst_ref=dst, send_sem=send, recv_sem=recv, device_id=device, device_id_type=MESH
+    )
+
+
+def neighbours():
+    c, p, d = lax.axis_index("section"), lax.axis_index("mp"), lax.axis_index("dp")
+    return {
+        "core": (1 - c, p, d),
+        "x": (c, p + 1 - 2 * lax.rem(p, 2), d),
+        "y": (c, lax.rem(p + 2, 4), d),
+        "across": (c, p, 3 - d),
+        "inner": (c, p, jnp.where(d == 0, 1, 2)),
+        "outer": (c, p, jnp.where(d == 1, 0, 3)),
+    }
+
+
+def places():
+    p = lax.axis_index("mp")
+    return [p, p + 1 - 2 * lax.rem(p, 2), lax.rem(p + 2, 4), 3 - p]
+
+
+def greet(near, is_end):
+    barrier = pltpu.get_barrier_semaphore()
+
+    def signal(device):
+        pl.semaphore_signal(barrier, inc=1, device_id=device, device_id_type=MESH)
+
+    for name in ("core", "x", "y"):
+        signal(near[name])
+
+    @pl.when(is_end)
+    def _():
+        signal(near["inner"])
+        pl.semaphore_wait(barrier, 4)
+
+    @pl.when(jnp.logical_not(is_end))
+    def _():
+        signal(near["outer"])
+        signal(near["across"])
+        pl.semaphore_wait(barrier, 5)
+
+
+CHUNKS = 24
+
+
+def reduce_kernel(
+    left, right, out,
+    lbuf, rbuf, sendc, recvc, keep, x1s, x1r, y1s, y1r, part, base, x2s, x2r, y2s, y2r, acc,
+    zk, zs1, zr1, zs2, zr2, zs3, zr3,
+    lsem, cs, cr, x1ss, x1rs, y1ss, y1rs, x2ss, x2rs, y2ss, y2rs, z1ss, z1rs, z2ss, z2rs, z3ss, z3rs, os, orr,
+):
+    c, d = lax.axis_index("section"), lax.axis_index("dp")
+    near = neighbours()
+    spots = places()
+    is_end = (d == 0) | (d == 3)
+    is_mid = jnp.logical_not(is_end)
+    greet(near, is_end)
+    rows = sendc.shape[2]
+    half = rows // 2
+
+    def loads(s):
+        layer, k, slot = 1 - s // 12, lax.rem(s, 12), lax.rem(s, 2)
+        stride = jnp.where(k < 8, 4, 1)
+        first = jnp.where(k < 4, k, jnp.where(k < 8, 12 + k, jnp.where(k == 8, 32, 36 + 4 * (k - 9))))
+        kind = jnp.where(k < 4, 0, jnp.where(k < 8, 1, jnp.where(k == 8, 2, 3)))
+        copies = [
+            pltpu.make_async_copy(left.at[layer, first + stride * p], lbuf.at[slot, p], lsem.at[slot, p])
+            for p in range(4)
+        ]
+        copies.append(pltpu.make_async_copy(right.at[layer, kind], rbuf.at[slot], lsem.at[slot, 4]))
+        return copies
+
+    def core_copy(s):
+        a, b = lax.rem(s, 2), lax.rem(s, 4)
+        return remote(sendc.at[a], recvc.at[b], cs.at[a], cr.at[b], near["core"])
+
+    def link_copy(s, src, dst, ss, rs, name):
+        a, b = lax.rem(s, 2), lax.rem(s, 4)
+        return remote(src.at[a], dst.at[b], ss.at[a], rs.at[b], near[name])
+
+    x1 = lambda s: link_copy(s, x1s, x1r, x1ss, x1rs, "x")
+    y1 = lambda s: link_copy(s, y1s, y1r, y1ss, y1rs, "y")
+    x2 = lambda s: link_copy(s, x2s, x2r, x2ss, x2rs, "x")
+    y2 = lambda s: link_copy(s, y2s, y2r, y2ss, y2rs, "y")
+    z1 = lambda s: link_copy(s, zs1, zr1, z1ss, z1rs, "inner")
+    z2 = lambda s: link_copy(s, zs2, zr2, z2ss, z2rs, "across")
+
+    def z3(s):
+        b = lax.rem(s, 6)
+        return remote(zs3.at[b], zr3.at[b], z3ss.at[b], z3rs.at[b], near["outer"])
+
+    def stage0(s):
+        slot = lax.rem(s, 2)
+        for copy in loads(s):
+            copy.wait()
+
+        @pl.when(s + 1 < CHUNKS)
+        def _():
+            for copy in loads(s + 1):
+                copy.start()
+
+        for r in range(4):
+            whole = lax.dot_general(
+                lbuf[slot, spots[r]], rbuf[slot], (((0,), (0,)), ((), ())), preferred_element_type=jnp.float32
+            )
+            keep[slot, r] = jnp.where(c == 0, whole[:rows], whole[rows:])
+            sendc[slot, r] = low(jnp.where(c == 0, whole[rows:], whole[:rows]))
+        core_copy(s).start()
+
+    def stage1(s):
+        a, b = lax.rem(s, 2), lax.rem(s, 4)
+        core_copy(s).wait()
+        far = keep[a, 3] + high(recvc[b, 3])
+        x1s[a, 0] = low(far[:half])
+        y1s[a, 0] = low(far[half:])
+        by_x = keep[a, 1] + high(recvc[b, 1])
+        x1s[a, 1] = low(by_x[:half])
+        part[a, 0] = by_x[half:]
+        by_y = keep[a, 2] + high(recvc[b, 2])
+        y1s[a, 1] = low(by_y[half:])
+        part[a, 1] = by_y[:half]
+        x1(s).start()
+        y1(s).start()
+        base[a] = keep[a, 0] + high(recvc[b, 0])
+
+    def stage2(s):
+        a, b = lax.rem(s, 2), lax.rem(s, 4)
+        x1(s).wait()
+        y1(s).wait()
+        y2s[a] = low(part[a, 1] + high(x1r[b, 0]))
+        x2s[a] = low(part[a, 0] + high(y1r[b, 0]))
+        own = base[a]
+        acc[a, pl.ds(0, half)] = own[:half] + high(x1r[b, 1])
+        acc[a, pl.ds(half, half)] = own[half:] + high(y1r[b, 1])
+        x2(s).start()
+        y2(s).start()
+
+    def stage3(s):
+        a, b = lax.rem(s, 2), lax.rem(s, 4)
+        x2(s).wait()
+        y2(s).wait()
+        own = acc[a]
+        top = own[:half] + high(y2r[b])
+        end = own[half:] + high(x2r[b])
+
+        @pl.when(is_end)
+        def _():
+            zs1[a, pl.ds(0, half)] = low(top)
+            zs1[a, pl.ds(half, half)] = low(end)
+            z1(s).start()
+
+        @pl.when(is_mid)
+        def _():
+            zk[a, pl.ds(0, half)] = top
+            zk[a, pl.ds(half, half)] = end
+
+    def stage4(s):
+        a, b = lax.rem(s, 2), lax.rem(s, 4)
+
+        @pl.when(is_end)
+        def _():
+            z1(s).wait_send()
+
+        @pl.when(is_mid)
+        def _():
+            z1(s).wait_recv()
+            zs2[a] = low(zk[a] + high(zr1[b]))
+            z2(s).start()
+
+    def stage5(s):
+        a, b = lax.rem(s, 2), lax.rem(s, 4)
+
+        @pl.when(is_mid)
+        def _():
+            z2(s).wait()
+            zs3[lax.rem(s, 6)] = low(high(zs2[a]) + high(zr2[b]))
+            z3(s).start()
+
+    def stage6(s, begin):
+        layer, k, b = 1 - s // 12, lax.rem(s, 12), lax.rem(s, 6)
+
+        def finish(source):
+            @pl.when(layer == c)
+            def _():
+                copy = pltpu.make_async_copy(source.at[b], out.at[k, c], os.at[b])
+                copy.start() if begin else copy.wait()
+
+            @pl.when(layer != c)
+            def _():
+                copy = remote(source.at[b], out.at[k, c], os.at[b], orr.at[k], near["core"])
+                copy.start() if begin else copy.wait_send()
+
+        @pl.when(is_end)
+        def _():
+            if begin:
+                z3(s).wait_recv()
+            finish(zr3)
+
+        @pl.when(is_mid)
+        def _():
+            if begin:
+                z3(s).wait_send()
+            finish(zs3)
+
+    for copy in loads(0):
+        copy.start()
+
+    def step(i, carry):
+        def run(stage, lag, *extra):
+            @pl.when((i >= lag) & (i < CHUNKS + lag))
+            def _():
+                stage(i - lag, *extra)
+
+        run(stage1, 1)
+        run(stage0, 0)
+        run(stage2, 2)
+        run(stage3, 3)
+        run(stage4, 4)
+        run(stage5, 5)
+        run(stage6, 6, True)
+        run(stage6, 7, False)
+        return carry
+
+    lax.fori_loop(0, CHUNKS + 8, step, 0)
+    for k in range(12):
+        remote(zs3.at[0], out.at[k, 1 - c], os.at[0], orr.at[k], near["core"]).wait_recv()
+
+
+def grad_reduce(left, right):
+    rows, wide = left.shape[2:]
+    block, width = wide // 2, right.shape[3]
+    half = block // 2
+    bf, f32, dma = jnp.bfloat16, jnp.float32, pltpu.SemaphoreType.DMA
+    v = pltpu.VMEM
+    return pl.pallas_call(
+        reduce_kernel,
+        out_shape=jax.ShapeDtypeStruct((12, 2, block, width), bf),
+        in_specs=[pl.BlockSpec(memory_space=pl.ANY)] * 2,
+        out_specs=pl.BlockSpec(memory_space=pl.ANY),
+        scratch_shapes=[
+            v((2, 4, rows, wide), bf), v((2, rows, width), bf),
+            v((2, 4, block, width), bf), v((4, 4, block, width), bf), v((2, 4, block, width), f32),
+            v((2, 2, half, width), bf), v((4, 2, half, width), bf), v((2, 2, half, width), bf), v((4, 2, half, width), bf),
+            v((2, 2, half, width), f32), v((2, block, width), f32),
+            v((2, half, width), bf), v((4, half, width), bf), v((2, half, width), bf), v((4, half, width), bf),
+            v((2, block, width), f32),
+            v((2, block, width), f32), v((2, block, width), bf), v((4, block, width), bf),
+            v((2, block, width), bf), v((4, block, width), bf), v((6, block, width), bf), v((6, block, width), bf),
+            dma((2, 5)),
+        ] + [dma((n,)) for n in (2, 4) * 7] + [dma((6,)), dma((6,))] + [dma((6,)), dma((12,))],
+        compiler_params=pltpu.CompilerParams(collective_id=1, has_side_effects=True, vmem_limit_bytes=50 * 2**20),
+    )(left, right)
+
+
+TRIPLES = 8
+
+
+def gather_kernel(
+    shard, vec, norms, full, vecs, all_norms,
+    ini_s, ini_r, loc, x1ss, x1rs, y1ss, y1rs, x2ss, x2rs, y2ss, y2rs, zs, zr, cs, cr, vs, vr, vloc,
+):
+    c, p, d = lax.axis_index("section"), lax.axis_index("mp"), lax.axis_index("dp")
+    near = neighbours()
+    near["pair"] = (c, p, d + 1 - 2 * lax.rem(d, 2))
+    spots = places()
+    rows = shard.shape[1] // 2
+    half = rows // 2
+    odd = lax.rem(d, 2)
+    others = [(cc, spots[r], d) for r in range(4) for cc in (c, 1 - c)][1:]
+
+    barrier = pltpu.get_barrier_semaphore()
+    for device in others + [near["pair"]]:
+        pl.semaphore_signal(barrier, inc=1, device_id=device, device_id_type=MESH)
+    pl.semaphore_wait(barrier, 8)
+
+    def place_of(s, spot, h):
+        k = lax.rem(s, 12)
+        b, kind = (k - 4) // 2, lax.rem(k, 2)
+        row = jnp.where(k < 4, k * 1024 + spot * 256, 4096 + kind * 4096 + spot * 1024 + b * 256) * (rows // 128)
+        return s // 12, row + h * rows
+
+    def block(s, spot, h, start=0, size=rows):
+        layer, row = place_of(s, spot, h)
+        return full.at[layer, pl.ds(pl.multiple_of(row + start, half), size)]
+
+    def init(k):
+        layer, row = place_of(12 * c + k, p, 0)
+        there = full.at[layer, pl.ds(pl.multiple_of(row, half), 2 * rows)]
+        src = shard.at[k]
+        return pltpu.make_async_copy(src, there, loc.at[k]), remote(src, there, ini_s.at[k], ini_r.at[k], near["core"])
+
+    def init_wait(k):
+        layer, row = place_of(12 * (1 - c) + k, p, 0)
+        there = full.at[layer, pl.ds(pl.multiple_of(row, half), 2 * rows)]
+        remote(there, there, ini_s.at[k], ini_r.at[k], near["core"]).wait_recv()
+
+    def small():
+        copies = [remote(vec, vecs.at[c, p], vs.at[i], vr.at[c, p], device) for i, device in enumerate(others)]
+        copies.append(remote(norms, all_norms.at[c], vs.at[7], vr.at[0, 4], near["core"]))
+        return copies
+
+    vec_local = pltpu.make_async_copy(vec, vecs.at[c, p], vloc.at[0])
+    norm_local = pltpu.make_async_copy(norms, all_norms.at[c], vloc.at[1])
+
+    def first(s, name):
+        ss, rs = (x1ss, x1rs) if name == "x" else (y1ss, y1rs)
+        b = block(s, p, c)
+        return remote(b, b, ss.at[s], rs.at[s], near[name])
+
+    def arrived(s, name):
+        ss, rs = (x1ss, x1rs) if name == "x" else (y1ss, y1rs)
+        b = block(s, spots[1] if name == "x" else spots[2], c)
+        return remote(b, b, ss.at[s], rs.at[s], near[name])
+
+    def relay(s, name):
+        if name == "x":
+            b = block(s, spots[2], c, 0, half)
+            return remote(b, b, x2ss.at[s], x2rs.at[s], near["x"])
+        b = block(s, spots[1], c, half, half)
+        return remote(b, b, y2ss.at[s], y2rs.at[s], near["y"])
+
+    def relayed(s, name):
+        if name == "x":
+            b = block(s, spots[3], c, 0, half)
+            return remote(b, b, x2ss.at[s], x2rs.at[s], near["x"])
+        b = block(s, spots[3], c, half, half)
+        return remote(b, b, y2ss.at[s], y2rs.at[s], near["y"])
+
+    def to_pair(s, r):
+        b = block(s, spots[r], c)
+        return remote(b, b, zs.at[s, r - 1], zr.at[s, r - 1], near["pair"])
+
+    def to_core(s, r):
+        b = block(s, spots[r], c)
+        return remote(b, b, cs.at[s, r - 1], cr.at[s, r - 1], near["core"])
+
+    def from_core(s, r):
+        b = block(s, spots[r], 1 - c)
+        return remote(b, b, cs.at[s, r - 1], cr.at[s, r - 1], near["core"])
+
+    def stage_a(t):
+        for j in range(3):
+            s = 3 * t + j
+
+            @pl.when(s // 12 != c)
+            def _():
+                init_wait(lax.rem(s, 12))
+
+        for s in (3 * t, 3 * t + 1 + odd):
+            first(s, "x").start()
+            first(s, "y").start()
+
+    def stage_b(t):
+        for n, s in enumerate((3 * t, 3 * t + 1 + odd)):
+            arrived(s, "x").wait_recv()
+            relay(s, "y").start()
+            arrived(s, "y").wait_recv()
+            relay(s, "x").start()
+            for r in (1, 2):
+                to_core(s, r).start()
+                if n:
+                    to_pair(s, r).start()
+
+    def stage_c(t):
+        for n, s in enumerate((3 * t, 3 * t + 1 + odd)):
+            relayed(s, "x").wait_recv()
+            relayed(s, "y").wait_recv()
+            to_core(s, 3).start()
+            if n:
+                to_pair(s, 3).start()
+
+    def stage_d(t):
+        s = 3 * t + 2 - odd
+        for r in (1, 2, 3):
+            to_pair(s, r).wait_recv()
+            to_core(s, r).start()
+
+    def stage_e(t):
+        for j in range(3):
+            for r in (1, 2, 3):
+                from_core(3 * t + j, r).wait_recv()
+
+    def stage_f(t):
+        for n, s in enumerate((3 * t, 3 * t + 1 + odd)):
+            first(s, "x").wait_send()
+            first(s, "y").wait_send()
+            relay(s, "x").wait_send()
+            relay(s, "y").wait_send()
+            for r in (1, 2, 3):
+                if n:
+                    to_pair(s, r).wait_send()
+        for j in range(3):
+            for r in (1, 2, 3):
+                to_core(3 * t + j, r).wait_send()
+
+    def begin(k, carry):
+        for copy in init(k):
+            copy.start()
+        return carry
+
+    lax.fori_loop(0, 12, begin, 0)
+    vec_local.start()
+    norm_local.start()
+    for copy in small():
+        copy.start()
+
+    def local_done(k, carry):
+        init(k)[0].wait()
+        return carry
+
+    lax.fori_loop(0, 12, local_done, 0)
+
+    def step(i, carry):
+        def run(stage, lag):
+            @pl.when((i >= lag) & (i < TRIPLES + lag))
+            def _():
+                stage(i - lag)
+
+        for lag, stage in enumerate((stage_a, stage_b, stage_c, stage_d, stage_e, stage_f)):
+            run(stage, lag)
+        return carry
+
+    lax.fori_loop(0, TRIPLES + 5, step, 0)
+
+    def sent(k, carry):
+        init(k)[1].wait_send()
+        return carry
+
+    lax.fori_loop(0, 12, sent, 0)
+    vec_local.wait()
+    norm_local.wait()
+    for copy in small():
+        copy.wait_send()
+    for cc, spot in [(cc, spots[r]) for r in range(4) for cc in (c, 1 - c)][1:]:
+        remote(vec, vecs.at[cc, spot], vs.at[0], vr.at[cc, spot], near["core"]).wait_recv()
+    remote(norms, all_norms.at[1 - c], vs.at[7], vr.at[0, 4], near["core"]).wait_recv()
+
+
+def weight_gather(shard, vec, norms):
+    block, width = shard.shape[2:]
+    dma = pltpu.SemaphoreType.DMA
+    return pl.pallas_call(
+        gather_kernel,
+        out_shape=(
+            jax.ShapeDtypeStruct((2, 96 * block, width), shard.dtype),
+            jax.ShapeDtypeStruct((2, 4) + vec.shape, vec.dtype),
+            jax.ShapeDtypeStruct((2,) + norms.shape, norms.dtype),
+        ),
+        in_specs=[pl.BlockSpec(memory_space=pltpu.VMEM)] + [pl.BlockSpec(memory_space=pl.ANY)] * 2,
+        out_specs=[pl.BlockSpec(memory_space=pl.ANY)] * 3,
+        scratch_shapes=[dma((12,))] * 3 + [dma((24,))] * 8 + [dma((24, 3))] * 4 + [dma((8,)), dma((2, 5)), dma((2,))],
+        compiler_params=pltpu.CompilerParams(collective_id=0, has_side_effects=True, vmem_limit_bytes=16 * 2**20),
+    )(shard.reshape(12, 2 * block, width), vec, norms)
+
+
+SCALE = 0.125
+
+
+def dot(a, b):
+    return jnp.dot(a, b, preferred_element_type=jnp.float32)
+
+
+def dot_tn(a, b):
+    return lax.dot_general(a, b, (((0,), (0,)), ((), ())), preferred_element_type=jnp.float32)
+
+
+def dot_nt(a, b):
+    return lax.dot_general(a, b, (((1,), (1,)), ((), ())), preferred_element_type=jnp.float32)
+
+
+def standard(values):
+    average = jnp.mean(values, axis=-1, keepdims=True)
+    centered = values - average
+    variance = jnp.mean(centered * centered, axis=-1, keepdims=True)
+    scale = lax.rsqrt(variance + 1e-05)
+    return centered * scale, scale
+
+
+def softmax(q, k):
+    scores = dot_nt(q * jnp.asarray(SCALE, q.dtype), k)
+    exponent = jnp.exp(scores - jnp.max(scores, axis=-1, keepdims=True))
+    return exponent * (1.0 / jnp.sum(exponent, axis=-1, keepdims=True))
+
+
+def by_rows(rows, step, body):
+    def run(i, carry):
+        body(pl.ds(pl.multiple_of(i * step, step), step))
+        return carry
+
+    lax.fori_loop(0, rows // step, run, 0)
+
+
+def attention_block(x, w, vec, save, acc, dim):
+    rows = x[...]
+    q = low(dot_nt(rows, w[0]) + vec[0:1])
+    k = low(dot_nt(rows, w[1]))
+    v = low(dot_nt(rows, w[2]) + vec[1:2])
+    save[0], save[1], save[2] = q, k, v
+    for j in range(q.shape[1] // dim):
+        cols = slice(j * dim, (j + 1) * dim)
+        save[3, :, cols] = low(dot(low(softmax(q[:, cols], k[:, cols])), v[:, cols]))
+    acc[...] += dot(save[3], w[3])
+
+
+def ffn_block(hb, w, bias, save, acc):
+    z = dot_nt(hb[...], w[0]) + bias
+    inner = 0.5 + 0.5 * lax.erf(z * math.sqrt(0.5))
+    g = low(z * inner)
+    save[0] = g
+    save[1] = low(inner + z * jnp.exp(-0.5 * z * z) * (1.0 / math.sqrt(2.0 * math.pi)))
+    acc[...] += dot(g, w[1])
+
+
+def first_norm(x, nrm, acc, u1, hb):
+    def run(rows):
+        u = acc[rows] + nrm[0:1] + high(x[rows])
+        u1[rows] = u
+        h = standard(u)[0] * nrm[2:3] + nrm[4:5]
+        hb[rows] = low(h)
+        acc[rows] = h + nrm[1:2]
+
+    by_rows(acc.shape[0], 64, run)
+
+
+def second_norm(nrm, acc, u2, out):
+    def run(rows):
+        u = acc[rows]
+        u2[rows] = u
+        out[rows] = low(standard(u)[0] * nrm[3:4] + nrm[5:6])
+
+    by_rows(acc.shape[0], 64, run)
+
+
+def norm_back(u, grad, gain, sums, at, out_low, out_acc):
+    def run(rows):
+        g = high(grad[rows])
+        xhat, scale = standard(u[rows])
+        scaled = g * gain
+        du = scale * (
+            scaled
+            - jnp.mean(scaled, axis=-1, keepdims=True)
+            - xhat * jnp.mean(scaled * xhat, axis=-1, keepdims=True)
+        )
+        out_low[rows] = low(du)
+        out_acc[rows] = du
+        for row, term in ((at[0], du), (at[1], g * xhat), (at[2], g)):
+            sums[row : row + 1] += jnp.sum(term, axis=0, keepdims=True)
+
+    by_rows(u.shape[0], 64, run)
+
+
+def ffn_back_block(dfb, w, gd, acc, dz_out):
+    dz = low(dot_nt(dfb[...], w[1]) * high(gd))
+    dz_out[...] = dz
+    acc[...] += dot(dz, w[0])
+    return jnp.sum(high(dz), axis=0, keepdims=True)
+
+
+def attention_back_block(dab, w, qkv, dq_out, dk_out, dv_out, acc, dim):
+    dob = low(dot_nt(dab[...], w[3]))
+    for j in range(dob.shape[1] // dim):
+        cols = slice(j * dim, (j + 1) * dim)
+        q, k, v, do = qkv[0, :, cols], qkv[1, :, cols], qkv[2, :, cols], dob[:, cols]
+        a = softmax(q, k)
+        da = dot_nt(do, v)
+        ds = low(a * (da - jnp.sum(a * da, axis=-1, keepdims=True)))
+        dv_out[:, cols] = low(dot_tn(low(a), do))
+        dq_out[:, cols] = low(dot(ds, k) * SCALE)
+        dk_out[:, cols] = low(dot_tn(ds, q) * SCALE)
+    acc[...] += dot(dq_out[...], w[0]) + dot(dk_out[...], w[1]) + dot(dv_out[...], w[2])
+
+
+def weight_copies(full, layer, kind, p, b, buf, sem, rows):
+    width = 4 * rows
+    if kind == 0:
+        starts = [c * width + p * rows for c in range(4)]
+    else:
+        starts = [4 * width + t * 4 * width + p * width + b * rows for t in range(2)]
+    return [
+        pltpu.make_async_copy(full.at[layer, pl.ds(pl.multiple_of(start, rows), rows)], buf.at[n], sem.at[n])
+        for n, start in enumerate(starts)
+    ]
+
+
+def forward_kernel(dim, x_in, full, vecs, norms, qkvo, gd, us, hbs, outs,
+                   x, acc, u, hb, wa, wf, sa, sf, wasem, wfsem, sasem, sfsem, usem):
+    rows = wa.shape[2]
+    x[...] = x_in[...]
+
+    def one(copy):
+        copy.start()
+        copy.wait()
+
+    def layer_step(l, carry):
+        nrm = norms.at[l]
+        acc[...] = jnp.zeros_like(acc)
+
+        def attn(p, slot):
+            return weight_copies(full, l, 0, p, 0, wa.at[slot], wasem.at[slot], rows)
+
+        def ffn(n, slot):
+            return weight_copies(full, l, 1, lax.rem(n, 4), n // 4, wf.at[slot], wfsem.at[slot], rows)
+
+        for copy in attn(0, 0) + ffn(0, 0):
+            copy.start()
+
+        def attn_step(p, carry):
+            slot = lax.rem(p, 2)
+            for copy in attn(p, slot):
+                copy.wait()
+
+            @pl.when(p < 3)
+            def _():
+                for copy in attn(p + 1, 1 - slot):
+                    copy.start()
+
+            attention_block(x, wa.at[slot], vecs[l, p], sa, acc, dim)
+            one(pltpu.make_async_copy(sa, qkvo.at[l, p], sasem))
+            return carry
+
+        lax.fori_loop(0, 4, attn_step, 0)
+        first_norm(x, nrm, acc, u, hb)
+        one(pltpu.make_async_copy(u, us.at[l, 0], usem))
+        one(pltpu.make_async_copy(hb, hbs.at[l], usem))
+
+        def ffn_step(n, carry):
+            slot = lax.rem(n, 2)
+            for copy in ffn(n, slot):
+                copy.wait()
+
+            @pl.when(n < 15)
+            def _():
+                for copy in ffn(n + 1, 1 - slot):
+                    copy.start()
+
+            p, b = lax.rem(n, 4), n // 4
+            ffn_block(hb, wf.at[slot], vecs[l, p, pl.ds(2 + b, 1)], sf, acc)
+            one(pltpu.make_async_copy(sf, gd.at[l, 4 * p + b], sfsem))
+            return carry
+
+        lax.fori_loop(0, 16, ffn_step, 0)
+        second_norm(nrm, acc, u, x)
+        one(pltpu.make_async_copy(u, us.at[l, 1], usem))
+        one(pltpu.make_async_copy(x, outs.at[l], usem))
+        return carry
+
+    lax.fori_loop(0, 2, layer_step, 0)
+
+
+def forward(dim, x, full, vecs, norms):
+    seq, width = x.shape
+    rows = width // 4
+    bf, f32, dma, v = jnp.bfloat16, jnp.float32, pltpu.SemaphoreType.DMA, pltpu.VMEM
+    hbm, vmem = pl.BlockSpec(memory_space=pl.ANY), pl.BlockSpec(memory_space=pltpu.VMEM)
+    S = jax.ShapeDtypeStruct
+    return pl.pallas_call(
+        functools.partial(forward_kernel, dim),
+        out_shape=(S((2, 4, 4, seq, rows), bf), S((2, 16, 2, seq, rows), bf), S((2, 2, seq, width), f32),
+                   S((2, seq, width), bf), S((2, seq, width), bf)),
+        in_specs=[vmem, hbm, vmem, vmem],
+        out_specs=[hbm] * 5,
+        scratch_shapes=[v((seq, width), bf), v((seq, width), f32), v((seq, width), f32), v((seq, width), bf),
+                        v((2, 4, rows, width), bf), v((2, 2, rows, width), bf), v((4, seq, rows), bf), v((2, seq, rows), bf),
+                        dma((2, 4)), dma((2, 2)), dma(()), dma(()), dma(())],
+        compiler_params=pltpu.CompilerParams(vmem_limit_bytes=50 * 2**20),
+    )(x, full, vecs, norms)
+
+
+def backward_kernel(dim, x_in, cot, full, vecs, norms, qkvo, gd, us, hbs, outs, left, right, dxs, sums, vgrads,
+                    L, R, acc, g, u, wa, wf, da, df, wasem, wfsem, dasem, dfsem, lsem, osem):
+    rows = wa.shape[2]
+    sums[...] = jnp.zeros_like(sums)
+    vgrads[...] = jnp.zeros_like(vgrads)
+
+    def one(copy):
+        copy.start()
+        copy.wait()
+
+    def layer_step(i, carry):
+        l = 1 - i
+        nrm, sm, vg = norms.at[l], sums.at[l], vgrads.at[l]
+
+        @pl.when(i == 0)
+        def _():
+            one(pltpu.make_async_copy(cot, g, osem))
+            one(pltpu.make_async_copy(outs.at[0], R.at[3], osem))
+
+        @pl.when(i == 1)
+        def _():
+            one(pltpu.make_async_copy(x_in, R.at[3], osem))
+
+        one(pltpu.make_async_copy(hbs.at[l], R.at[1], osem))
+
+        def ld(n, carry):
+            one(pltpu.make_async_copy(gd.at[l, n, 0], L.at[n], osem))
+            return carry
+
+        lax.fori_loop(0, 16, ld, 0)
+
+        def ldo(n, carry):
+            one(pltpu.make_async_copy(qkvo.at[l, n, 3], L.at[32 + n], osem))
+            return carry
+
+        lax.fori_loop(0, 4, ldo, 0)
+        one(pltpu.make_async_copy(us.at[l, 1], u, osem))
+        norm_back(u, g, nrm[3:4], sm, (1, 3, 5), R.at[0], acc)
+
+        def attn(p, slot):
+            return weight_copies(full, l, 0, p, 0, wa.at[slot], wasem.at[slot], rows) + [
+                pltpu.make_async_copy(qkvo.at[l, p], da.at[slot], dasem.at[slot])
+            ]
+
+        def ffn(n, slot):
+            return weight_copies(full, l, 1, lax.rem(n, 4), n // 4, wf.at[slot], wfsem.at[slot], rows) + [
+                pltpu.make_async_copy(gd.at[l, 4 * lax.rem(n, 4) + n // 4, 1], df.at[slot], dfsem.at[slot])
+            ]
+
+        for copy in attn(0, 0) + ffn(0, 0):
+            copy.start()
+
+        def ffn_step(n, carry):
+            slot = lax.rem(n, 2)
+            for copy in ffn(n, slot):
+                copy.wait()
+
+            @pl.when(n < 15)
+            def _():
+                for copy in ffn(n + 1, 1 - slot):
+                    copy.start()
+
+            p, b = lax.rem(n, 4), n // 4
+            vg[p, pl.ds(2 + b, 1)] = ffn_back_block(R.at[0], wf.at[slot], df[slot], acc, L.at[16 + 4 * p + b])
+            return carry
+
+        lax.fori_loop(0, 16, ffn_step, 0)
+        one(pltpu.make_async_copy(us.at[l, 0], u, osem))
+        norm_back(u, acc, nrm[2:3], sm, (0, 2, 4), R.at[2], acc)
+
+        def attn_step(p, carry):
+            slot = lax.rem(p, 2)
+            for copy in attn(p, slot):
+                copy.wait()
+
+            @pl.when(p < 3)
+            def _():
+                for copy in attn(p + 1, 1 - slot):
+                    copy.start()
+
+            attention_back_block(
+                R.at[2], wa.at[slot], da.at[slot], L.at[36 + p], L.at[40 + p], L.at[44 + p], acc, dim
+            )
+            vg[p, 0:1] = jnp.sum(high(L[36 + p]), axis=0, keepdims=True)
+            vg[p, 1:2] = jnp.sum(high(L[44 + p]), axis=0, keepdims=True)
+            return carry
+
+        lax.fori_loop(0, 4, attn_step, 0)
+        by_rows(acc.shape[0], 64, lambda r: g.__setitem__(r, low(acc[r])))
+        one(pltpu.make_async_copy(g, dxs.at[l], osem))
+        one(pltpu.make_async_copy(L, left.at[l], osem))
+        one(pltpu.make_async_copy(R, right.at[l], osem))
+        return carry
+
+    lax.fori_loop(0, 2, layer_step, 0)
+
+
+def backward(dim, x, cot, full, vecs, norms, saved):
+    seq, width = x.shape
+    rows = width // 4
+    bf, f32, dma, v = jnp.bfloat16, jnp.float32, pltpu.SemaphoreType.DMA, pltpu.VMEM
+    hbm, vmem = pl.BlockSpec(memory_space=pl.ANY), pl.BlockSpec(memory_space=pltpu.VMEM)
+    S = jax.ShapeDtypeStruct
+    return pl.pallas_call(
+        functools.partial(backward_kernel, dim),
+        out_shape=(S((2, 48, seq, rows), bf), S((2, 4, seq, width), bf), S((2, seq, width), bf),
+                   S((2, 8, width), f32), S((2, 4, 8, rows), f32)),
+        in_specs=[hbm, hbm, hbm, vmem, vmem] + [hbm] * 5,
+        out_specs=[hbm, hbm, hbm, vmem, vmem],
+        scratch_shapes=[v((48, seq, rows), bf), v((4, seq, width), bf), v((seq, width), f32), v((seq, width), bf),
+                        v((seq, width), f32),
+                        v((2, 4, rows, width), bf), v((2, 2, rows, width), bf), v((2, 4, seq, rows), bf), v((2, seq, rows), bf),
+                        dma((2, 4)), dma((2, 2)), dma((2,)), dma((2,)), dma(()), dma(())],
+        compiler_params=pltpu.CompilerParams(vmem_limit_bytes=56 * 2**20),
+    )(x, cot, full, vecs, norms, *saved)
+
+
+def butterfly(value):
+    for axis, bits in (("section", 1), ("mp", 2), ("dp", 2)):
+        for bit in range(bits):
+            pairs = [(i, i ^ (1 << bit)) for i in range(lax.axis_size(axis))]
+            value = value + lax.ppermute(value, axis, pairs)
+    return value
+
+
+def by_page(
+    token_in,
+    cotangent,
+    w_qkv,
+    qv_bias,
+    w_attn_out,
+    w_ffn_in,
+    ffn_in_bias,
+    w_ffn_out,
+    out_biases,
+    norm_gains,
+    norm_shifts,
+):
+    core, place = lax.axis_index("section"), lax.axis_index("mp")
+    is_first = core == 0
+    width = token_in.shape[2]
+    quarter = width // 4
+    x = lax.dynamic_index_in_dim(token_in, core, 0, keepdims=False)
+    cot = lax.dynamic_index_in_dim(cotangent, core, 0, keepdims=False)
+    ffn_in_t = w_ffn_in[0].T.reshape(4, 1, quarter, width)
+    ffn = jnp.concatenate([ffn_in_t, w_ffn_out[0].reshape(4, 1, quarter, width)], axis=1)
+    shard = jnp.concatenate(
+        [w_qkv[0].transpose(0, 2, 1), w_attn_out, ffn.reshape(8, quarter, width)], axis=0
+    ).reshape(12, 2, quarter // 2, width)
+    vec = high(jnp.concatenate([qv_bias[0], ffn_in_bias[0].reshape(4, quarter)], axis=0))
+    vec = jnp.pad(vec, ((0, 2), (0, 0)))
+    norms = jnp.concatenate([out_biases[0], norm_gains[0], norm_shifts[0]], axis=0)
+    norms = jnp.pad(norms, ((0, 2), (0, 0)))
+    full, vecs, all_norms = weight_gather(shard, vec, norms)
+    saved = forward(HEAD_DIM, x, full, vecs, all_norms)
+    left, right, grads, sums, vector_grads = backward(HEAD_DIM, x, cot, full, vecs, all_norms, saved)
+    parts = grad_reduce(left, right)
+    outs = saved[4]
+
+    def trade(both):
+        own = lax.dynamic_index_in_dim(both, core, 0)
+        received = swap_core(lax.dynamic_index_in_dim(both, 1 - core, 0))
+        return jnp.where(is_first, jnp.concatenate([own, received]), jnp.concatenate([received, own]))
+
+    flat = jnp.concatenate([vector_grads.reshape(2, -1), sums.reshape(2, -1)], axis=1).reshape(2, -1, quarter)
+    flat = lax.dynamic_index_in_dim(butterfly(flat), core, 0, keepdims=False)
+    own = lax.dynamic_slice_in_dim(flat, place * 8, 8, 0)
+    rows = flat[32:].reshape(8, width)
+    piece = width // (lax.axis_size("mp") * lax.axis_size("dp"))
+    begin = (place * lax.axis_size("dp") + lax.axis_index("dp")) * piece
+    rows = lax.dynamic_slice_in_dim(rows, begin, piece, 1)
+    parts = parts.reshape(12, quarter, width)
+    return (
+        trade(outs)[None],
+        trade(grads)[None],
+        high(parts[9:12].transpose(0, 2, 1))[None],
+        own[0:2][None],
+        high(parts[8])[None],
+        high(parts[4:8].reshape(width, width).T)[None],
+        own[2:6].reshape(1, width),
+        high(parts[0:4].reshape(width, width))[None],
+        rows[0:2][None],
+        rows[2:4][None],
+        rows[4:6][None],
+    )
+
+
+def swap_core(value):
+    return lax.ppermute(value, "section", [(0, 1), (1, 0)])
+
+
+def on_device(*args):
+    token_in, w_qkv, ffn_in = args[0], args[2], args[5]
+    fits = (
+        lax.axis_size("section") == 2
+        and lax.axis_size("mp") == 4
+        and lax.axis_size("dp") == 4
+        and token_in.shape == (2, SEQ, 1024)
+        and w_qkv.shape[3] == 256
+        and ffn_in.shape[2] == 1024
+    )
+    return by_page(*args) if fits else pipelined(*args)
 
 
 def solution(mesh):

time: 3860 us -> 752 us (0.19)
  waiting for transfers between devices: 2660 us -> 6.9 us
  Pallas kernels: 0 us -> 686 us
  matrix products: 599 us -> 0 us
  local copies, waits for them, and re-layouts: 303 us -> 31.5 us
  other arithmetic: 220 us -> 20.1 us
    all_gather x18 -> x0, waiting for transfers between devices: 955 us -> none  [the longest x6 323 us: layer_forward(): gathered = lax.all_gather(token_rows, 'mp', axis=0, tiled=True)]
    reduce_scatter x18 -> x0, waiting for transfers between devices: 819 us -> none  [the longest x6 310 us: layer_forward(): lax.psum_scatter(ffn_part.astype(jnp.bfloat16), 'mp', scatter_dimension=0...]
    pallas_call x0 -> x4, Pallas kernels: none -> 686 us  [the longest x1 237 us: grad_reduce(): pl.pallas_call(reduce_kernel, out_shape=jax.ShapeDtypeStruct((12, 2, bloc...]
    psum x3 -> x0, waiting for transfers between devices: 665 us -> none  [backward_step(): lax.psum(grad_one.astype(jnp.bfloat16), 'dp').astype(jnp.float32)]
    dot_general x66 -> x0, matrix products: 569 us -> none  [the longest x6 105 us: layer_forward(): ffn_part = jnp.dot(activated, w_ffn_out, preferred_element_type=jnp.float32)]
    unnamed x6 -> x0, waiting for transfers between devices: 218 us -> none
    squeeze x27 -> x2, local copies, waits for them, and re-layouts: 98 us -> 2.79 us  [the longest x1 2.71 us: by_page(): cot = lax.dynamic_index_in_dim(cotangent, core, 0, keepdims=False)]
    another operation x30 -> x1, local copies, waits for them, and re-layouts: 75.7 us -> 0.01 us  [by_page(): ffn_in_bias[0].reshape(4, quarter)]
  transfers between devices with their start and end apart: 48 -> 7, of which waited for: 45 -> 3; matrix products, arithmetic and copies ran while one was open for 4% -> 4% of each run, Pallas kernels for 0% -> 32%
where the time goes in v2:
time: 752 us; the launch traced here: 749 us
  Pallas kernels  686 us (91%)
  local copies, waits for them, and re-layouts  31.5 us (4%)
  other arithmetic  20.1 us (3%)
    pallas_call x1, Pallas kernels, grad_reduce(): pl.pallas_call(reduce_kernel, out_shape=jax.ShapeDtypeStruct((12, 2, bloc...  237 us
    pallas_call x1, Pallas kernels, backward(): pl.pallas_call(functools.partial(backward_kernel, dim), out_shape=(S((2,...  174 us
    pallas_call x1, Pallas kernels, weight_gather(): pl.pallas_call(gather_kernel, out_shape=(jax.ShapeDtypeStruct((2, 96 * bl...  165 us
    pallas_call x1, Pallas kernels, forward(): pl.pallas_call(functools.partial(forward_kernel, dim), out_shape=(S((2, 4...  111 us
  transfers between devices with their start and end apart: 7, of which 3 were waited for; matrix products, arithmetic and copies ran while one was open for 4% of the time, Pallas kernels for 32%

profile of v2, /device:TPU:0, one launch (start us, length us, event | category | flops | bytes accessed | tf_op | source)
XLA Modules:
  0.0 748.8 jit_solution(10797235863387901439)
XLA Ops:
  0.6 0.0 copy-start
  0.7 4.1 copy.27
  4.8 2.6 copy.22
  7.3 0.0 copy-done.16
  7.4 0.0 copy-done
  7.4 0.0 copy-start.7
  7.4 0.0 copy-start.10
  7.4 0.1 dynamic-slice_bitcast_fusion.3.x_in
  7.5 0.0 copy-start.2
  7.5 2.7 dynamic-slice_bitcast_fusion.1.cot
  10.2 0.0 copy-done.7
  10.2 0.3 copy-done.10
  10.5 0.4 pad_maximum_fusion.1
  10.9 0.3 copy-done.17
  11.2 0.7 copy-done.8
  11.9 0.1 copy-done.11
  12.0 3.2 pad_maximum_fusion.shard
  15.2 0.0 copy-done.13
  15.2 0.0 copy-done.14
  15.2 0.0 copy-done.15
  15.3 164.7 %shard_map.194 = (bf16[2,12288,1024]{2,1,0:T(8,128)(2,1)}, f32[2,4,8,256]{3,2,1,0:T(8,128)S(1)}, f32[2,8,1024]{2,1,0:T(8,128)S(1)}) custom-call(bf16[12,256,1024]{2,1,0:T(8,128)(2,1)S(1)} %pad_maximum_fusion.shard, f32[8,256]{1,0:T(8,128)S(1)} %fusion.3.vec, f32[8,1024]{1,0:T(8,128)S(1)} %select_maximum_fusion.norms), custom_call_target="tpu_custom_call" | custom-call | tf_op jit(solution)/shard_map/pallas_call | solution.py:782
  180.0 0.0 copy-start.4
  180.0 0.0 copy-start.5
  180.0 110.7 %shard_map.195 = (bf16[2,4,4,512,256]{4,3,2,1,0:T(8,128)(2,1)}, bf16[2,16,2,512,256]{4,3,2,1,0:T(8,128)(2,1)}, f32[2,2,512,1024]{3,2,1,0:T(8,128)}, bf16[2,512,1...) custom-call(bf16[512,1024]{1,0:T(8,128)(2,1)S(1)} %dynamic-slice_bitcast_fusion.3.x_in, ...), custom_call_target="tpu_custom_call" | custom-call | tf_op jit(solution)/shard_map/pallas_call | solution.py:996
  290.8 0.0 copy-done.4
  290.8 0.0 copy-done.5
  290.8 0.0 copy-start.3
  290.8 1.3 copy-done.3
  292.1 174.2 %shard_map.196 = (bf16[2,48,512,256]{3,2,1,0:T(8,128)(2,1)}, bf16[2,4,512,1024]{3,2,1,0:T(8,128)(2,1)}, bf16[2,512,1024]{2,1,0:T(8,128)(2,1)}, f32[2,8,1024]{2,1,0:T(8,128)}, f32[2,4,8,256]{3,2,1,0:T(8,128)}) custom-call(bf16[512,1024]{1,0:T(8,128)(2,1)} %copy-done.2, bf16[512,1024]{1,0:T(8,128)(2,1)} %dynamic-slice_bitcast_fusion.1.cot, ...), custom_call_target="tpu_custom_call" | custom-call | tf_op jit(solution)/shard_map/pallas_call | solution.py:1112
  466.3 0.9 concatenate.81
  467.2 0.9 pad_maximum_fusion.2
  468.0 0.5 collective-permute-start.2
  468.5 3.2 dynamic-slice_bitcast_fusion
  471.7 0.1 collective-permute-start.1
  471.9 1.5 dynamic-slice_bitcast_fusion.2
  473.4 0.4 collective-permute-start
  473.8 236.7 %shard_map.197 = bf16[12,2,128,1024]{3,2,1,0:T(8,128)(2,1)} custom-call(bf16[2,48,512,256]{3,2,1,0:T(8,128)(2,1)} %get-tuple-element.33.left, bf16[2,4,512,1024]{3,2,1,0:T(8,128)(2,1)} %get-tuple-element.34.right), custom_call_target="tpu_custom_call" | custom-call | tf_op jit(solution)/shard_map/pallas_call | solution.py:575
  710.4 0.0 collective-permute-done.2
  710.5 0.0 copy-done.12
  710.5 0.6 collective-permute-start.3
  711.1 4.0 fusion.5
  715.2 0.4 collective-permute-done.3
  715.5 1.1 collective-permute-start.4
  716.7 2.6 bitcast_convert_fusion
  719.3 1.3 collective-permute-done.4
  720.6 0.0 slice-start.1
  720.6 0.1 collective-permute-start.5
  720.7 0.0 slice-done
  720.7 0.5 bitcast_convert_fusion.1
  721.2 5.2 collective-permute-done.5
  726.5 0.3 collective-permute-start.6
  726.7 1.1 bitcast_convert_fusion.2
  727.9 5.3 copy.26
  733.2 4.1 convert.13
  737.3 2.4 copy.25
  739.6 0.0 collective-permute-done.6
  739.7 0.6 copy.28
  740.3 0.6 constant_dynamic-slice_fusion
  740.9 0.1 constant_dynamic-slice_fusion.1
  741.0 0.6 slice_bitcast_fusion
  741.5 0.0 collective-permute-done.1
  741.5 3.9 maximum_select_fusion.1
  745.5 0.0 collective-permute-done
  745.5 3.3 maximum_select_fusion
  (29 shorter events, 0.2 us)
Async XLA Ops:
  0.6 6.7 copy-start
  4.8 2.6 copy-start.16
  7.4 2.8 copy-start.7
  7.4 3.1 copy-start.10
  7.5 172.5 %copy-start.2 = (bf16[512,1024]{1,0:T(8,128)(2,1)}, bf16[512,1024]{1,0:T(8,128)(2,1)S(1)}, u32[]{:S(2)}) copy-start(bf16[512,1024]{1,0:T(8,128)(2,1)S(1)} %dynamic-slice_bitcast_fusion.3.x_in) | copy-start | bytes 3145732
  10.5 0.7 copy-start.17
  10.5 1.4 copy-start.8
  10.5 1.5 copy-start.11
  12.0 3.2 copy-start.13
  12.0 3.2 copy-start.14
  12.0 3.2 copy-start.15
  180.0 110.8 %copy-start.4 = (f32[2,4,8,256]{3,2,1,0:T(8,128)}, f32[2,4,8,256]{3,2,1,0:T(8,128)S(1)}, u32[]{:S(2)}) copy-start(f32[2,4,8,256]{3,2,1,0:T(8,128)S(1)} %get-tuple-element.25.vecs) | copy-start | bytes 196612
  180.0 110.8 %copy-start.5 = (f32[2,8,1024]{2,1,0:T(8,128)}, f32[2,8,1024]{2,1,0:T(8,128)S(1)}, u32[]{:S(2)}) copy-start(f32[2,8,1024]{2,1,0:T(8,128)S(1)} %get-tuple-element.26.norms) | copy-start | bytes 196612
  290.8 1.3 copy-start.3
  468.0 242.4 %collective-permute-start.2 = (f32[2,64,256]{2,1,0:T(8,128)S(1)}, f32[2,64,256]{2,1,0:T(8,128)S(1)}, u32[]{:S(2)}, u32[]{:S(2)}) collective-permute-start(f32[2,64,256]{2,1,0:T(8,128)S(1)} %pad_maximum_fusion.2), channel_id=1, source_target_pairs={{0,16},{16,0},{1,17},{17,1},{2,18},{18,2},{3,19},{19,3},{4,20},{20... | collective-permute-start | bytes 393224 | tf_op jit(solution)/shard_map/ppermute | solution.py:1130
  468.5 3.4 copy-start.6
  471.7 269.8 %collective-permute-start.1 = (bf16[1,512,1024]{2,1,0:T(8,128)(2,1)}, bf16[1,512,1024]{2,1,0:T(8,128)(2,1)}, u32[]{:S(2)}, u32[]{:S(2)}) collective-permute-start(bf16[1,512,1024]{2,1,0:T(8,128)(2,1)} %get-tuple-element.40), channel_id=1, source_target_pairs={{0,16},{16,0},{1,17},{17,1},{2,18},{18,2},{3,19},{19,3},{4,20},{20... | collective-permute-start | bytes 3145736 | tf_op jit(solution)/shard_map/ppermute | solution.py:1197
  473.4 272.1 %collective-permute-start = (bf16[1,512,1024]{2,1,0:T(8,128)(2,1)}, bf16[1,512,1024]{2,1,0:T(8,128)(2,1)}, u32[]{:S(2)}, u32[]{:S(2)}) collective-permute-start(bf16[1,512,1024]{2,1,0:T(8,128)(2,1)} %get-tuple-element.42), channel_id=1, source_target_pairs={{0,16},{16,0},{1,17},{17,1},{2,18},{18,2},{3,19},{19,3},{4,20},{20... | collective-permute-start | bytes 3145736 | tf_op jit(solution)/shard_map/ppermute | solution.py:1197
  473.8 236.7 %copy-start.12 = (f32[2,4,8,256]{3,2,1,0:T(8,128)S(1)}, f32[2,4,8,256]{3,2,1,0:T(8,128)}, u32[]{:S(2)}) copy-start(f32[2,4,8,256]{3,2,1,0:T(8,128)} %get-tuple-element.35) | copy-start | bytes 196612
  710.5 5.0 collective-permute-start.3
  715.5 5.0 collective-permute-start.4
  719.3 1.4 slice-start
  720.6 6.1 slice-start.1
  720.6 5.8 collective-permute-start.5
  726.5 13.2 %collective-permute-start.6 = (f32[2,64,256]{2,1,0:T(8,128)S(1)}, f32[2,64,256]{2,1,0:T(8,128)S(1)}, u32[]{:S(2)}, u32[]{:S(2)}) collective-permute-start(f32[2,64,256]{2,1,0:T(8,128)S(1)} %add.51), channel_id=1, source_target_pairs={{0,2},{1,3},{2,0},{3,1},{4,6},{5,7},{6,4},{7,5},{8,10},{9,11},{10,... | collective-permute-start | bytes 393224 | tf_op jit(solution)/shard_map/ppermute | solution.py:1130
  741.5 4.0 copy-start.9
  745.5 3.3 copy-start.1

commit v3 on v0

--- a/solution.py
+++ b/solution.py
@@ -1,9 +1,12 @@
+import functools
 from functools import partial
 import math
 
 import jax
 import jax.numpy as jnp
 from jax import lax
+from jax.experimental import pallas as pl
+from jax.experimental.pallas import tpu as pltpu
 from jax.sharding import PartitionSpec as P
 
 HEAD_DIM = 64
@@ -204,7 +207,7 @@
     return (grad_in, matrix_grads, vector_grads)
 
 
-def on_device(
+def pipelined(
     token_in,
     cotangent,
     w_qkv,
@@ -320,6 +323,968 @@
         gain_part[None],
         shift_part[None],
     )
+
+
+MESH = pl.DeviceIdType.MESH
+CHUNKS = 24
+TRIPLES = 8
+SCALE = 0.125
+
+
+def low(value):
+    return value.astype(jnp.bfloat16)
+
+
+def high(value):
+    return value.astype(jnp.float32)
+
+
+def remote(src, dst, send, recv, device):
+    return pltpu.make_async_remote_copy(
+        src_ref=src, dst_ref=dst, send_sem=send, recv_sem=recv, device_id=device, device_id_type=MESH
+    )
+
+
+def neighbours():
+    c, p, d = lax.axis_index("section"), lax.axis_index("mp"), lax.axis_index("dp")
+    return {
+        "core": (1 - c, p, d),
+        "x": (c, p + 1 - 2 * lax.rem(p, 2), d),
+        "y": (c, lax.rem(p + 2, 4), d),
+        "across": (c, p, 3 - d),
+        "inner": (c, p, jnp.where(d == 0, 1, 2)),
+        "outer": (c, p, jnp.where(d == 1, 0, 3)),
+    }
+
+
+def places():
+    p = lax.axis_index("mp")
+    return [p, p + 1 - 2 * lax.rem(p, 2), lax.rem(p + 2, 4), 3 - p]
+
+
+def dot(a, b):
+    return jnp.dot(a, b, preferred_element_type=jnp.float32)
+
+
+def dot_tn(a, b):
+    return lax.dot_general(a, b, (((0,), (0,)), ((), ())), preferred_element_type=jnp.float32)
+
+
+def dot_nt(a, b):
+    return lax.dot_general(a, b, (((1,), (1,)), ((), ())), preferred_element_type=jnp.float32)
+
+
+def standard(values):
+    average = jnp.mean(values, axis=-1, keepdims=True)
+    centered = values - average
+    variance = jnp.mean(centered * centered, axis=-1, keepdims=True)
+    scale = lax.rsqrt(variance + 1e-05)
+    return centered * scale, scale
+
+
+def softmax(q, k):
+    scores = dot_nt(q * jnp.asarray(SCALE, q.dtype), k)
+    exponent = jnp.exp(scores - jnp.max(scores, axis=-1, keepdims=True))
+    return exponent * (1.0 / jnp.sum(exponent, axis=-1, keepdims=True))
+
+
+def by_rows(rows, step, body):
+    def run(i, carry):
+        body(pl.ds(pl.multiple_of(i * step, step), step))
+        return carry
+
+    lax.fori_loop(0, rows // step, run, 0)
+
+
+def ffn_block(hb, w, bias, save, acc):
+    z = dot_nt(hb[...], w[0]) + bias
+    inner = 0.5 + 0.5 * lax.erf(z * math.sqrt(0.5))
+    g = low(z * inner)
+    save[0] = g
+    save[1] = low(inner + z * jnp.exp(-0.5 * z * z) * (1.0 / math.sqrt(2.0 * math.pi)))
+    acc[...] += dot(g, w[1])
+
+
+def first_norm(x, nrm, acc, u1, hb):
+    def run(rows):
+        u = acc[rows] + nrm[0:1] + high(x[rows])
+        u1[rows] = u
+        h = standard(u)[0] * nrm[2:3] + nrm[4:5]
+        hb[rows] = low(h)
+        acc[rows] = h + nrm[1:2]
+
+    by_rows(acc.shape[0], 64, run)
+
+
+def second_norm(nrm, acc, u2, out):
+    def run(rows):
+        u = acc[rows]
+        u2[rows] = u
+        out[rows] = low(standard(u)[0] * nrm[3:4] + nrm[5:6])
+
+    by_rows(acc.shape[0], 64, run)
+
+
+def norm_back(u, grad, gain, sums, at, out_low, out_acc):
+    def run(rows):
+        g = high(grad[rows])
+        xhat, scale = standard(u[rows])
+        scaled = g * gain
+        du = scale * (
+            scaled
+            - jnp.mean(scaled, axis=-1, keepdims=True)
+            - xhat * jnp.mean(scaled * xhat, axis=-1, keepdims=True)
+        )
+        out_low[rows] = low(du)
+        out_acc[rows] = du
+        for row, term in ((at[0], du), (at[1], g * xhat), (at[2], g)):
+            sums[row : row + 1] += jnp.sum(term, axis=0, keepdims=True)
+
+    by_rows(u.shape[0], 64, run)
+
+
+def ffn_back_block(dfb, w, gd, acc, dz_out):
+    dz = low(dot_nt(dfb[...], w[1]) * high(gd))
+    dz_out[...] = dz
+    acc[...] += dot(dz, w[0])
+    return jnp.sum(high(dz), axis=0, keepdims=True)
+
+
+def attention_back_block(dab, w, qkv, dq_out, dk_out, dv_out, acc, dim):
+    dob = low(dot_nt(dab[...], w[3]))
+    for j in range(dob.shape[1] // dim):
+        cols = slice(j * dim, (j + 1) * dim)
+        q, k, v, do = qkv[0, :, cols], qkv[1, :, cols], qkv[2, :, cols], dob[:, cols]
+        a = softmax(q, k)
+        da = dot_nt(do, v)
+        ds = low(a * (da - jnp.sum(a * da, axis=-1, keepdims=True)))
+        dv_out[:, cols] = low(dot_tn(low(a), do))
+        dq_out[:, cols] = low(dot(ds, k) * SCALE)
+        dk_out[:, cols] = low(dot_tn(ds, q) * SCALE)
+    acc[...] += dot(dq_out[...], w[0]) + dot(dk_out[...], w[1]) + dot(dv_out[...], w[2])
+
+
+def weight_copies(full, layer, kind, p, b, buf, sem, rows):
+    width = 4 * rows
+    if kind == 0:
+        starts = [c * width + p * rows for c in range(4)]
+    else:
+        starts = [4 * width + t * 4 * width + p * width + b * rows for t in range(2)]
+    return [
+        pltpu.make_async_copy(full.at[layer, pl.ds(pl.multiple_of(start, rows), rows)], buf.at[n], sem.at[n])
+        for n, start in enumerate(starts)
+    ]
+
+
+def project_block(x, w, vec, save, dim):
+    rows = x[...]
+    q = low(dot_nt(rows, w[0]) + vec[0:1])
+    k = low(dot_nt(rows, w[1]))
+    v = low(dot_nt(rows, w[2]) + vec[1:2])
+    save[0], save[1], save[2] = q, k, v
+    for j in range(q.shape[1] // dim):
+        cols = slice(j * dim, (j + 1) * dim)
+        save[3, :, cols] = low(dot(low(softmax(q[:, cols], k[:, cols])), v[:, cols]))
+
+
+def gather_forward_kernel(
+    dim, x_in, shard, vec, norm_in, full, vecs, norms, qkvo, gd, us, hbs, outs,
+    x, acc, u, hb, wa, wf, sa, sf, wasem, wfsem, sasem, sfsem, usem,
+    ini_s, ini_r, loc, x1ss, x1rs, y1ss, y1rs, x2ss, x2rs, y2ss, y2rs, zs, zr, cs, cr, vs, vr, vloc,
+):
+    c, p, d = lax.axis_index("section"), lax.axis_index("mp"), lax.axis_index("dp")
+    near = neighbours()
+    near["pair"] = (c, p, d + 1 - 2 * lax.rem(d, 2))
+    spots = places()
+    rows = shard.shape[1] // 2
+    half = rows // 2
+    odd = lax.rem(d, 2)
+    others = [(cc, spots[r], d) for r in range(4) for cc in (c, 1 - c)][1:]
+
+    barrier = pltpu.get_barrier_semaphore()
+    for device in others + [near["pair"]]:
+        pl.semaphore_signal(barrier, inc=1, device_id=device, device_id_type=MESH)
+    pl.semaphore_wait(barrier, 8)
+
+    def place_of(s, spot, h):
+        k = lax.rem(s, 12)
+        b, kind = (k - 4) // 2, lax.rem(k, 2)
+        row = jnp.where(k < 4, k * 8 + spot * 2, 32 + kind * 32 + spot * 8 + b * 2)
+        return s // 12, (row + h) * rows
+
+    def block(s, spot, h, start=0, size=rows):
+        layer, row = place_of(s, spot, h)
+        return full.at[layer, pl.ds(pl.multiple_of(row + start, half), size)]
+
+    def init_place(k, layer):
+        row = place_of(12 * layer + k, p, 0)[1]
+        return full.at[layer, pl.ds(pl.multiple_of(row, half), 2 * rows)]
+
+    def init_local(k):
+        return pltpu.make_async_copy(shard.at[k], init_place(k, c), loc.at[k])
+
+    def init_remote(k):
+        return remote(shard.at[k], init_place(k, c), ini_s.at[k], ini_r.at[k], near["core"])
+
+    def init_wait(k):
+        there = init_place(k, 1 - c)
+        remote(there, there, ini_s.at[k], ini_r.at[k], near["core"]).wait_recv()
+
+    def small():
+        copies = [remote(vec, vecs.at[c, p], vs.at[i], vr.at[c, p], device) for i, device in enumerate(others)]
+        copies.append(remote(norm_in, norms.at[c], vs.at[7], vr.at[0, 4], near["core"]))
+        return copies
+
+    def small_local():
+        return [
+            pltpu.make_async_copy(vec, vecs.at[c, p], vloc.at[0]),
+            pltpu.make_async_copy(norm_in, norms.at[c], vloc.at[1]),
+        ]
+
+    def hop(s, spot, name, pick):
+        ss, rs = (x1ss, x1rs) if pick == "x" else (y1ss, y1rs)
+        b = block(s, spot, c)
+        return remote(b, b, ss.at[s], rs.at[s], near[name])
+
+    def first(s, name):
+        return hop(s, p, name, name)
+
+    def arrived(s, name):
+        return hop(s, spots[1] if name == "x" else spots[2], name, name)
+
+    def relay(s, name, spot=None):
+        if name == "x":
+            b = block(s, spots[2] if spot is None else spot, c, 0, half)
+            return remote(b, b, x2ss.at[s], x2rs.at[s], near["x"])
+        b = block(s, spots[1] if spot is None else spot, c, half, half)
+        return remote(b, b, y2ss.at[s], y2rs.at[s], near["y"])
+
+    def relayed(s, name):
+        return relay(s, name, spots[3])
+
+    def to_pair(s, r):
+        b = block(s, spots[r], c)
+        return remote(b, b, zs.at[s, r - 1], zr.at[s, r - 1], near["pair"])
+
+    def to_core(s, r):
+        b = block(s, spots[r], c)
+        return remote(b, b, cs.at[s, r - 1], cr.at[s, r - 1], near["core"])
+
+    def from_core(s, r):
+        b = block(s, spots[r], 1 - c)
+        return remote(b, b, cs.at[s, r - 1], cr.at[s, r - 1], near["core"])
+
+    def stage_a(t):
+        for j in range(3):
+            s = 3 * t + j
+
+            @pl.when(s // 12 != c)
+            def _():
+                init_wait(lax.rem(s, 12))
+
+        for s in (3 * t, 3 * t + 1 + odd):
+            first(s, "x").start()
+            first(s, "y").start()
+
+    def stage_b(t):
+        for n, s in enumerate((3 * t, 3 * t + 1 + odd)):
+            arrived(s, "x").wait_recv()
+            relay(s, "y").start()
+            arrived(s, "y").wait_recv()
+            relay(s, "x").start()
+            for r in (1, 2):
+                to_core(s, r).start()
+                if n:
+                    to_pair(s, r).start()
+
+    def stage_c(t):
+        for n, s in enumerate((3 * t, 3 * t + 1 + odd)):
+            relayed(s, "x").wait_recv()
+            relayed(s, "y").wait_recv()
+            to_core(s, 3).start()
+            if n:
+                to_pair(s, 3).start()
+
+    def stage_d(t):
+        s = 3 * t + 2 - odd
+        for r in (1, 2, 3):
+            to_pair(s, r).wait_recv()
+            to_core(s, r).start()
+
+    def stage_e(t):
+        for j in range(3):
+            for r in (1, 2, 3):
+                from_core(3 * t + j, r).wait_recv()
+
+    def stage_f(t):
+        for n, s in enumerate((3 * t, 3 * t + 1 + odd)):
+            first(s, "x").wait_send()
+            first(s, "y").wait_send()
+            relay(s, "x").wait_send()
+            relay(s, "y").wait_send()
+            for r in (1, 2, 3):
+                if n:
+                    to_pair(s, r).wait_send()
+        for j in range(3):
+            for r in (1, 2, 3):
+                to_core(3 * t + j, r).wait_send()
+
+    wide = 2 * rows
+
+    def attn(l, q, slot):
+        return weight_copies(full, l, 0, q, 0, wa.at[slot], wasem.at[slot], wide)[:3]
+
+    def attn_out(l, q, slot):
+        return weight_copies(full, l, 0, q, 0, wa.at[slot], wasem.at[slot], wide)[3]
+
+    def ffn(l, n, slot):
+        return weight_copies(full, l, 1, lax.rem(n, 4), n // 4, wf.at[slot], wfsem.at[slot], wide)
+
+    def save_attn(l, q, slot):
+        return pltpu.make_async_copy(sa.at[q], qkvo.at[l, q], sasem.at[slot])
+
+    def save_ffn(l, n, slot):
+        return pltpu.make_async_copy(sf.at[slot], gd.at[l, 4 * lax.rem(n, 4) + n // 4], sfsem.at[slot])
+
+    def attention_segment(l):
+        for copy in attn(l, 0, 0):
+            copy.start()
+
+        def run(q, carry):
+            slot = lax.rem(q, 2)
+            for copy in attn(l, q, slot):
+                copy.wait()
+
+            @pl.when(q < 3)
+            def _():
+                for copy in attn(l, q + 1, 1 - slot):
+                    copy.start()
+
+            project_block(x, wa.at[slot], vecs[l, q], sa.at[q], dim)
+            save_attn(l, q, q).start()
+            return carry
+
+        lax.fori_loop(0, 4, run, 0)
+
+    def ffn_segment(l, begin, count):
+        for copy in ffn(l, begin, 0):
+            copy.start()
+
+        def run(m, carry):
+            slot = lax.rem(m, 2)
+            n = begin + m
+            for copy in ffn(l, n, slot):
+                copy.wait()
+
+            @pl.when(m < count - 1)
+            def _():
+                for copy in ffn(l, n + 1, 1 - slot):
+                    copy.start()
+
+            @pl.when(m >= 2)
+            def _():
+                save_ffn(l, n - 2, slot).wait()
+
+            ffn_block(hb, wf.at[slot], vecs[l, lax.rem(n, 4), pl.ds(2 + n // 4, 1)], sf.at[slot], acc)
+            save_ffn(l, n, slot).start()
+            return carry
+
+        lax.fori_loop(0, count, run, 0)
+        for m in (count - 2, count - 1):
+            save_ffn(l, begin + m, m % 2).wait()
+
+    def keep(l, which):
+        if which == 2:
+            return pltpu.make_async_copy(hb, hbs.at[l], usem.at[2])
+        if which == 3:
+            return pltpu.make_async_copy(x, outs.at[l], usem.at[3])
+        return pltpu.make_async_copy(u, us.at[l, which], usem.at[which])
+
+    def out_segment(l):
+        for q in range(2):
+            attn_out(l, q, q).start()
+        acc[...] = jnp.zeros_like(acc)
+        for q in range(4):
+            attn_out(l, q, q % 2).wait()
+            acc[...] += dot(sa[q, 3], wa[q % 2, 3])
+            if q < 2:
+                attn_out(l, q + 2, q).start()
+        for q in range(4):
+            save_attn(l, q, q).wait()
+
+        @pl.when(l == 1)
+        def _():
+            keep(0, 1).wait()
+
+        first_norm(x, norms.at[l], acc, u, hb)
+        keep(l, 0).start()
+        keep(l, 2).start()
+
+    def end_segment(l):
+        keep(l, 0).wait()
+        keep(l, 2).wait()
+
+        @pl.when(l == 1)
+        def _():
+            keep(0, 3).wait()
+
+        second_norm(norms.at[l], acc, u, x)
+        keep(l, 1).start()
+        keep(l, 3).start()
+
+    def compute(t):
+        l, part = t // 4, lax.rem(t, 4)
+
+        @pl.when(t == 0)
+        def _():
+            for copy in small_local():
+                copy.wait()
+            for copy in small():
+                copy.wait_send()
+            for cc, spot in [(cc, spots[r]) for r in range(4) for cc in (c, 1 - c)][1:]:
+                remote(vec, vecs.at[cc, spot], vs.at[0], vr.at[cc, spot], near["core"]).wait_recv()
+            remote(norm_in, norms.at[1 - c], vs.at[7], vr.at[0, 4], near["core"]).wait_recv()
+
+        @pl.when(part == 0)
+        def _():
+            attention_segment(l)
+
+        @pl.when(part == 1)
+        def _():
+            out_segment(l)
+
+        @pl.when(part > 0)
+        def _():
+            ffn_segment(l, 4 * (part - 1), 4)
+
+        @pl.when(part == 3)
+        def _():
+            ffn_segment(l, 12, 4)
+            end_segment(l)
+
+    def begin(k, carry):
+        init_local(k).start()
+        init_remote(k).start()
+        return carry
+
+    lax.fori_loop(0, 12, begin, 0)
+    for copy in small_local() + small():
+        copy.start()
+    x[...] = x_in[...]
+
+    def local_done(k, carry):
+        init_local(k).wait()
+        return carry
+
+    lax.fori_loop(0, 12, local_done, 0)
+
+    def step(i, carry):
+        def run(stage, lag):
+            @pl.when((i >= lag) & (i < TRIPLES + lag))
+            def _():
+                stage(i - lag)
+
+        for lag, stage in enumerate((stage_a, stage_b, stage_c, stage_d, stage_e)):
+            run(stage, lag)
+        run(compute, 4)
+        run(stage_f, 5)
+        return carry
+
+    lax.fori_loop(0, TRIPLES + 5, step, 0)
+
+    def sent(k, carry):
+        init_remote(k).wait_send()
+        return carry
+
+    lax.fori_loop(0, 12, sent, 0)
+    keep(1, 1).wait()
+    keep(1, 3).wait()
+
+
+def gather_forward(dim, x, shard, vec, norms):
+    rows, width = shard.shape[1:]
+    seq = x.shape[0]
+    bf, f32, dma, v = jnp.bfloat16, jnp.float32, pltpu.SemaphoreType.DMA, pltpu.VMEM
+    hbm, vmem = pl.BlockSpec(memory_space=pl.ANY), pl.BlockSpec(memory_space=pltpu.VMEM)
+    S = jax.ShapeDtypeStruct
+    return pl.pallas_call(
+        functools.partial(gather_forward_kernel, dim),
+        out_shape=(
+            S((2, 48 * rows, width), bf), S((2, 4) + vec.shape, f32), S((2,) + norms.shape, f32),
+            S((2, 4, 4, seq, rows), bf), S((2, 16, 2, seq, rows), bf), S((2, 2, seq, width), f32),
+            S((2, seq, width), bf), S((2, seq, width), bf),
+        ),
+        in_specs=[vmem, vmem, vmem, vmem],
+        out_specs=[hbm, vmem, vmem] + [hbm] * 5,
+        scratch_shapes=[
+            v((seq, width), bf), v((seq, width), f32), v((seq, width), f32), v((seq, width), bf),
+            v((2, 4, rows, width), bf), v((2, 2, rows, width), bf), v((4, 4, seq, rows), bf), v((2, 2, seq, rows), bf),
+            dma((2, 4)), dma((2, 2)), dma((4,)), dma((2,)), dma((4,)),
+        ] + [dma((12,))] * 3 + [dma((24,))] * 8 + [dma((24, 3))] * 4 + [dma((8,)), dma((2, 5)), dma((2,))],
+        compiler_params=pltpu.CompilerParams(collective_id=0, has_side_effects=True, vmem_limit_bytes=56 * 2**20),
+    )(x, shard, vec, norms)
+
+
+def backward_reduce_kernel(
+    dim, x_in, cot, full, vecs, norms, qkvo, gd, us, hbs, outs, out, dxs, totals,
+    left, right, acc, g, u, wa, wf, da, df, trades,
+    sendc, recvc, keep, x1s, x1r, y1s, y1r, part, base, x2s, x2r, y2s, y2r, mid,
+    zk, zs1, zr1, zs2, zr2, zs3, zr3,
+    wasem, wfsem, dasem, dfsem, gsem, osem4, bsem, tss, trs,
+    cs, cr, x1ss, x1rs, y1ss, y1rs, x2ss, x2rs, y2ss, y2rs, z1ss, z1rs, z2ss, z2rs, z3ss, z3rs, os, orr,
+):
+    c, p, d = lax.axis_index("section"), lax.axis_index("mp"), lax.axis_index("dp")
+    near = neighbours()
+    near["pair"] = (c, p, d + 1 - 2 * lax.rem(d, 2))
+    near["far"] = (c, p, lax.rem(d + 2, 4))
+    spots = places()
+    is_end = (d == 0) | (d == 3)
+    is_mid = jnp.logical_not(is_end)
+    rows = sendc.shape[2]
+    half = rows // 2
+    wide = 2 * rows
+
+    barrier = pltpu.get_barrier_semaphore()
+
+    def signal(device):
+        pl.semaphore_signal(barrier, inc=1, device_id=device, device_id_type=MESH)
+
+    for name in ("core", "x", "y", "pair", "far"):
+        signal(near[name])
+
+    @pl.when(is_end)
+    def _():
+        pl.semaphore_wait(barrier, 5)
+
+    @pl.when(is_mid)
+    def _():
+        signal(near["across"])
+        pl.semaphore_wait(barrier, 6)
+
+    def core_copy(s):
+        a, b = lax.rem(s, 2), lax.rem(s, 4)
+        return remote(sendc.at[a], recvc.at[b], cs.at[a], cr.at[b], near["core"])
+
+    def link_copy(s, src, dst, ss, rs, name):
+        a, b = lax.rem(s, 2), lax.rem(s, 4)
+        return remote(src.at[a], dst.at[b], ss.at[a], rs.at[b], near[name])
+
+    x1 = lambda s: link_copy(s, x1s, x1r, x1ss, x1rs, "x")
+    y1 = lambda s: link_copy(s, y1s, y1r, y1ss, y1rs, "y")
+    x2 = lambda s: link_copy(s, x2s, x2r, x2ss, x2rs, "x")
+    y2 = lambda s: link_copy(s, y2s, y2r, y2ss, y2rs, "y")
+    z1 = lambda s: link_copy(s, zs1, zr1, z1ss, z1rs, "inner")
+    z2 = lambda s: link_copy(s, zs2, zr2, z2ss, z2rs, "across")
+
+    def z3(s):
+        b = lax.rem(s, 6)
+        return remote(zs3.at[b], zr3.at[b], z3ss.at[b], z3rs.at[b], near["outer"])
+
+    def stage0(s):
+        k, slot = lax.rem(s, 12), lax.rem(s, 2)
+        stride = jnp.where(k < 8, 4, 1)
+        first = jnp.where(k < 4, k, jnp.where(k < 8, 12 + k, jnp.where(k == 8, 32, 36 + 4 * (k - 9))))
+        kind = jnp.where(k < 4, 0, jnp.where(k < 8, 1, jnp.where(k == 8, 2, 3)))
+        for r in range(4):
+            whole = dot_tn(left[first + stride * spots[r]], right[kind])
+            keep[slot, r] = jnp.where(c == 0, whole[:rows], whole[rows:])
+            sendc[slot, r] = low(jnp.where(c == 0, whole[rows:], whole[:rows]))
+        core_copy(s).start()
+
+    def stage1(s):
+        a, b = lax.rem(s, 2), lax.rem(s, 4)
+        core_copy(s).wait()
+        far = keep[a, 3] + high(recvc[b, 3])
+        x1s[a, 0] = low(far[:half])
+        y1s[a, 0] = low(far[half:])
+        by_x = keep[a, 1] + high(recvc[b, 1])
+        x1s[a, 1] = low(by_x[:half])
+        part[a, 0] = by_x[half:]
+        by_y = keep[a, 2] + high(recvc[b, 2])
+        y1s[a, 1] = low(by_y[half:])
+        part[a, 1] = by_y[:half]
+        x1(s).start()
+        y1(s).start()
+        base[a] = keep[a, 0] + high(recvc[b, 0])
+
+    def stage2(s):
+        a, b = lax.rem(s, 2), lax.rem(s, 4)
+        x1(s).wait()
+        y1(s).wait()
+        y2s[a] = low(part[a, 1] + high(x1r[b, 0]))
+        x2s[a] = low(part[a, 0] + high(y1r[b, 0]))
+        own = base[a]
+        mid[a, pl.ds(0, half)] = own[:half] + high(x1r[b, 1])
+        mid[a, pl.ds(half, half)] = own[half:] + high(y1r[b, 1])
+        x2(s).start()
+        y2(s).start()
+
+    def stage3(s):
+        a, b = lax.rem(s, 2), lax.rem(s, 4)
+        x2(s).wait()
+        y2(s).wait()
+        own = mid[a]
+        top = own[:half] + high(y2r[b])
+        end = own[half:] + high(x2r[b])
+
+        @pl.when(is_end)
+        def _():
+            zs1[a, pl.ds(0, half)] = low(top)
+            zs1[a, pl.ds(half, half)] = low(end)
+            z1(s).start()
+
+        @pl.when(is_mid)
+        def _():
+            zk[a, pl.ds(0, half)] = top
+            zk[a, pl.ds(half, half)] = end
+
+    def stage4(s):
+        a, b = lax.rem(s, 2), lax.rem(s, 4)
+
+        @pl.when(is_end)
+        def _():
+            z1(s).wait_send()
+
+        @pl.when(is_mid)
+        def _():
+            z1(s).wait_recv()
+            zs2[a] = low(zk[a] + high(zr1[b]))
+            z2(s).start()
+
+    def stage5(s):
+        a, b = lax.rem(s, 2), lax.rem(s, 4)
+
+        @pl.when(is_mid)
+        def _():
+            z2(s).wait()
+            zs3[lax.rem(s, 6)] = low(high(zs2[a]) + high(zr2[b]))
+            z3(s).start()
+
+    def stage6(s, begin):
+        layer, k, b = 1 - s // 12, lax.rem(s, 12), lax.rem(s, 6)
+
+        def finish(source):
+            @pl.when(layer == c)
+            def _():
+                copy = pltpu.make_async_copy(source.at[b], out.at[k, c], os.at[b])
+                copy.start() if begin else copy.wait()
+
+            @pl.when(layer != c)
+            def _():
+                copy = remote(source.at[b], out.at[k, c], os.at[b], orr.at[k], near["core"])
+                copy.start() if begin else copy.wait_send()
+
+        @pl.when(is_end)
+        def _():
+            if begin:
+                z3(s).wait_recv()
+            finish(zr3)
+
+        @pl.when(is_mid)
+        def _():
+            if begin:
+                z3(s).wait_send()
+            finish(zs3)
+
+    def load_g(l, n):
+        return pltpu.make_async_copy(gd.at[l, n, 0], left.at[n], gsem.at[n])
+
+    def load_o(l, n):
+        return pltpu.make_async_copy(qkvo.at[l, n, 3], left.at[32 + n], osem4.at[n])
+
+    def load_h(l):
+        return pltpu.make_async_copy(hbs.at[l], right.at[1], bsem.at[0])
+
+    def load_x(source):
+        return pltpu.make_async_copy(source, right.at[3], bsem.at[1])
+
+    def load_u(l, which):
+        return pltpu.make_async_copy(us.at[l, which], u, bsem.at[2])
+
+    def ffn(l, n, slot):
+        return weight_copies(full, l, 1, lax.rem(n, 4), n // 4, wf.at[slot], wfsem.at[slot], wide) + [
+            pltpu.make_async_copy(gd.at[l, 4 * lax.rem(n, 4) + n // 4, 1], df.at[slot], dfsem.at[slot])
+        ]
+
+    def attn(l, q, slot):
+        return weight_copies(full, l, 0, q, 0, wa.at[slot], wasem.at[slot], wide) + [
+            pltpu.make_async_copy(qkvo.at[l, q], da.at[slot], dasem.at[slot])
+        ]
+
+    def store_dx(l):
+        return pltpu.make_async_copy(g, dxs.at[l], bsem.at[3])
+
+    def ahead(l):
+        load_u(l, 1).start()
+        for copy in ffn(l, 0, 0) + attn(l, 0, 0):
+            copy.start()
+
+    def operands(l):
+        def run(n, carry):
+            load_g(l, n).start()
+            return carry
+
+        lax.fori_loop(0, 16, run, 0)
+        for n in range(4):
+            load_o(l, n).start()
+        load_h(l).start()
+
+    def operands_there(l):
+        def run(n, carry):
+            load_g(l, n).wait()
+            return carry
+
+        lax.fori_loop(0, 16, run, 0)
+        for n in range(4):
+            load_o(l, n).wait()
+        load_h(l).wait()
+
+    def top_segment(l):
+        load_u(l, 1).wait()
+        norm_back(u, g, norms[l, 3:4], totals.at[l], (1, 3, 5), right.at[0], acc)
+        load_u(l, 0).start()
+
+        @pl.when(l == 1)
+        def _():
+            operands_there(1)
+
+    def ffn_segment(l, b):
+        def run(q, carry):
+            n = 4 * b + q
+            slot = lax.rem(n, 2)
+            for copy in ffn(l, n, slot):
+                copy.wait()
+
+            @pl.when(n < 15)
+            def _():
+                for copy in ffn(l, n + 1, 1 - slot):
+                    copy.start()
+
+            row = ffn_back_block(right.at[0], wf.at[slot], df[slot], acc, left.at[16 + 4 * q + b])
+            totals[l, pl.ds(10 + b, 1), pl.ds(pl.multiple_of(q * wide, wide), wide)] = row
+            return carry
+
+        lax.fori_loop(0, 4, run, 0)
+
+    def middle_segment(l):
+        load_u(l, 0).wait()
+        norm_back(u, acc, norms[l, 2:3], totals.at[l], (0, 2, 4), right.at[2], acc)
+
+    def attention_segment(l, q):
+        slot = lax.rem(q, 2)
+        for copy in attn(l, q, slot):
+            copy.wait()
+
+        @pl.when(q < 3)
+        def _():
+            for copy in attn(l, q + 1, 1 - slot):
+                copy.start()
+
+        dq, dk, dv = left.at[36 + q], left.at[40 + q], left.at[44 + q]
+        attention_back_block(right.at[2], wa.at[slot], da.at[slot], dq, dk, dv, acc, dim)
+        cols = pl.ds(pl.multiple_of(q * wide, wide), wide)
+        totals[l, 8:9, cols] = jnp.sum(high(dq[...]), axis=0, keepdims=True)
+        totals[l, 9:10, cols] = jnp.sum(high(dv[...]), axis=0, keepdims=True)
+
+    def end_segment(l):
+        by_rows(acc.shape[0], 64, lambda r: g.__setitem__(r, low(acc[r])))
+        store_dx(l).start()
+
+        @pl.when(l == 1)
+        def _():
+            ahead(0)
+
+    def segment(i):
+        l, j = 1 - i // 9, lax.rem(i, 9)
+
+        @pl.when(i == 9)
+        def _():
+            operands(0)
+            store_dx(1).wait()
+
+        @pl.when(j == 0)
+        def _():
+            top_segment(l)
+
+        @pl.when(j < 4)
+        def _():
+            ffn_segment(l, j)
+
+        @pl.when(j == 4)
+        def _():
+            middle_segment(l)
+
+        @pl.when((j >= 4) & (j < 8))
+        def _():
+            attention_segment(l, j - 4)
+
+        @pl.when(j == 8)
+        def _():
+            end_segment(l)
+
+        @pl.when(i == 8)
+        def _():
+            load_x(outs.at[0]).wait()
+
+        @pl.when(i == 12)
+        def _():
+            operands_there(0)
+            load_x(x_in).start()
+
+        @pl.when(i == 16)
+        def _():
+            load_x(x_in).wait()
+
+    def trade(k, name):
+        copy = remote(totals, trades.at[k], tss.at[k], trs.at[k], near[name])
+        copy.start()
+        copy.wait()
+        totals[...] += trades[k]
+
+    first_rows = pltpu.make_async_copy(cot, g, bsem.at[3])
+    first_rows.start()
+    ahead(1)
+    operands(1)
+    load_x(outs.at[0]).start()
+    totals[...] = jnp.zeros_like(totals)
+    first_rows.wait()
+
+    def step(i, carry):
+        def run(stage, lag, *extra):
+            @pl.when((i >= lag) & (i < CHUNKS + lag))
+            def _():
+                stage(i - lag, *extra)
+
+        run(stage1, 1)
+
+        @pl.when(i < 18)
+        def _():
+            segment(i)
+
+        run(stage0, 0)
+        run(stage2, 2)
+        run(stage3, 3)
+        run(stage4, 4)
+        run(stage5, 5)
+        run(stage6, 6, True)
+        run(stage6, 7, False)
+        for k, name in enumerate(("core", "x", "y", "pair", "far")):
+
+            @pl.when(i == 19 + k)
+            def _():
+                trade(k, name)
+
+        return carry
+
+    lax.fori_loop(0, CHUNKS + 8, step, 0)
+    store_dx(0).wait()
+    for k in range(12):
+        remote(zs3.at[0], out.at[k, 1 - c], os.at[0], orr.at[k], near["core"]).wait_recv()
+
+
+def backward_reduce(dim, x, cot, full, vecs, norms, saved):
+    seq, width = x.shape
+    wide = width // 4
+    block, half = wide // 2, wide // 4
+    bf, f32, dma, v = jnp.bfloat16, jnp.float32, pltpu.SemaphoreType.DMA, pltpu.VMEM
+    hbm, vmem = pl.BlockSpec(memory_space=pl.ANY), pl.BlockSpec(memory_space=pltpu.VMEM)
+    S = jax.ShapeDtypeStruct
+    return pl.pallas_call(
+        functools.partial(backward_reduce_kernel, dim),
+        out_shape=(S((12, 2, block, width), bf), S((2, seq, width), bf), S((2, 16, width), f32)),
+        in_specs=[hbm, hbm, hbm, vmem, vmem] + [hbm] * 5,
+        out_specs=[hbm, hbm, vmem],
+        scratch_shapes=[
+            v((48, seq, wide), bf), v((4, seq, width), bf), v((seq, width), f32), v((seq, width), bf),
+            v((seq, width), f32),
+            v((2, 4, wide, width), bf), v((2, 2, wide, width), bf), v((2, 4, seq, wide), bf), v((2, seq, wide), bf),
+            v((5, 2, 16, width), f32),
+            v((2, 4, block, width), bf), v((4, 4, block, width), bf), v((2, 4, block, width), f32),
+            v((2, 2, half, width), bf), v((4, 2, half, width), bf), v((2, 2, half, width), bf), v((4, 2, half, width), bf),
+            v((2, 2, half, width), f32), v((2, block, width), f32),
+            v((2, half, width), bf), v((4, half, width), bf), v((2, half, width), bf), v((4, half, width), bf),
+            v((2, block, width), f32),
+            v((2, block, width), f32), v((2, block, width), bf), v((4, block, width), bf),
+            v((2, block, width), bf), v((4, block, width), bf), v((6, block, width), bf), v((6, block, width), bf),
+            dma((2, 4)), dma((2, 2)), dma((2,)), dma((2,)), dma((16,)), dma((4,)), dma((4,)), dma((5,)), dma((5,)),
+        ] + [dma((n,)) for n in (2, 4) * 7] + [dma((6,)), dma((6,))] + [dma((6,)), dma((12,))],
+        compiler_params=pltpu.CompilerParams(collective_id=1, has_side_effects=True, vmem_limit_bytes=63 * 2**20),
+    )(x, cot, full, vecs, norms, *saved)
+
+
+def swap_core(value):
+    return lax.ppermute(value, "section", [(0, 1), (1, 0)])
+
+
+def by_page(
+    token_in,
+    cotangent,
+    w_qkv,
+    qv_bias,
+    w_attn_out,
+    w_ffn_in,
+    ffn_in_bias,
+    w_ffn_out,
+    out_biases,
+    norm_gains,
+    norm_shifts,
+):
+    core, place = lax.axis_index("section"), lax.axis_index("mp")
+    is_first = core == 0
+    width = token_in.shape[2]
+    quarter = width // 4
+    x = lax.dynamic_index_in_dim(token_in, core, 0, keepdims=False)
+    cot = lax.dynamic_index_in_dim(cotangent, core, 0, keepdims=False)
+    ffn_in_t = w_ffn_in[0].T.reshape(4, 1, quarter, width)
+    ffn = jnp.concatenate([ffn_in_t, w_ffn_out[0].reshape(4, 1, quarter, width)], axis=1)
+    shard = jnp.concatenate(
+        [w_qkv[0].transpose(0, 2, 1), w_attn_out, ffn.reshape(8, quarter, width)], axis=0
+    )
+    vec = high(jnp.concatenate([qv_bias[0], ffn_in_bias[0].reshape(4, quarter)], axis=0))
+    vec = jnp.pad(vec, ((0, 2), (0, 0)))
+    norms = jnp.concatenate([out_biases[0], norm_gains[0], norm_shifts[0]], axis=0)
+    norms = jnp.pad(norms, ((0, 2), (0, 0)))
+    full, vecs, all_norms, *saved = gather_forward(HEAD_DIM, x, shard, vec, norms)
+    parts, grads, totals = backward_reduce(HEAD_DIM, x, cot, full, vecs, all_norms, saved)
+    outs = saved[4]
+
+    def trade(both):
+        own = lax.dynamic_index_in_dim(both, core, 0)
+        received = swap_core(lax.dynamic_index_in_dim(both, 1 - core, 0))
+        return jnp.where(is_first, jnp.concatenate([own, received]), jnp.concatenate([received, own]))
+
+    totals = lax.dynamic_index_in_dim(totals, core, 0, keepdims=False)
+    own = lax.dynamic_slice_in_dim(totals[8:], place * quarter, quarter, 1)
+    piece = width // (lax.axis_size("mp") * lax.axis_size("dp"))
+    begin = (place * lax.axis_size("dp") + lax.axis_index("dp")) * piece
+    rows = lax.dynamic_slice_in_dim(totals[:8], begin, piece, 1)
+    parts = parts.reshape(12, quarter, width)
+    return (
+        trade(outs)[None],
+        trade(grads)[None],
+        high(parts[9:12].transpose(0, 2, 1))[None],
+        own[0:2][None],
+        high(parts[8])[None],
+        high(parts[4:8].reshape(width, width).T)[None],
+        own[2:6].reshape(1, width),
+        high(parts[0:4].reshape(width, width))[None],
+        rows[0:2][None],
+        rows[2:4][None],
+        rows[4:6][None],
+    )
+
+
+def on_device(*args):
+    token_in, w_qkv, ffn_in = args[0], args[2], args[5]
+    fits = (
+        lax.axis_size("section") == 2
+        and lax.axis_size("mp") == 4
+        and lax.axis_size("dp") == 4
+        and token_in.shape == (2, SEQ, 1024)
+        and w_qkv.shape[3] == 256
+        and ffn_in.shape[2] == 1024
+    )
+    return by_page(*args) if fits else pipelined(*args)
 
 
 def solution(mesh):

time: 3860 us -> 558 us (0.14)
  waiting for transfers between devices: 2660 us -> 0.01 us
  matrix products: 599 us -> 0 us
  Pallas kernels: 0 us -> 498 us
  local copies, waits for them, and re-layouts: 303 us -> 29.6 us
  other arithmetic: 220 us -> 27.3 us
    all_gather x18 -> x0, waiting for transfers between devices: 955 us -> none  [the longest x6 323 us: layer_forward(): gathered = lax.all_gather(token_rows, 'mp', axis=0, tiled=True)]
    reduce_scatter x18 -> x0, waiting for transfers between devices: 819 us -> none  [the longest x6 310 us: layer_forward(): lax.psum_scatter(ffn_part.astype(jnp.bfloat16), 'mp', scatter_dimension=0...]
    psum x3 -> x0, waiting for transfers between devices: 665 us -> none  [backward_step(): lax.psum(grad_one.astype(jnp.bfloat16), 'dp').astype(jnp.float32)]
    dot_general x66 -> x0, matrix products: 569 us -> none  [the longest x6 105 us: layer_forward(): ffn_part = jnp.dot(activated, w_ffn_out, preferred_element_type=jnp.float32)]
    pallas_call x0 -> x2, Pallas kernels: none -> 498 us  [the longest x1 292 us: backward_reduce(): pl.pallas_call(functools.partial(backward_reduce_kernel, dim), out_shape=...]
    unnamed x6 -> x0, waiting for transfers between devices: 218 us -> none
    squeeze x27 -> x2, local copies, waits for them, and re-layouts: 98 us -> 3.45 us  [the longest x1 2.42 us: by_page(): x = lax.dynamic_index_in_dim(token_in, core, 0, keepdims=False)]
    another operation x30 -> x1, local copies, waits for them, and re-layouts: 75.7 us -> 0.01 us  [by_page(): ffn_in_bias[0].reshape(4, quarter)]
  transfers between devices with their start and end apart: 48 -> 2, of which waited for: 45 -> 0; matrix products, arithmetic and copies ran while one was open for 4% -> 5% of each run, Pallas kernels for 0% -> 0%
where the time goes in v3:
time: 558 us; the launch traced here: 556 us
  Pallas kernels  498 us (89%)
  local copies, waits for them, and re-layouts  29.6 us (5%)
  other arithmetic  27.3 us (5%)
    pallas_call x1, Pallas kernels, backward_reduce(): pl.pallas_call(functools.partial(backward_reduce_kernel, dim), out_shape=...  292 us
    pallas_call x1, Pallas kernels, gather_forward(): pl.pallas_call(functools.partial(gather_forward_kernel, dim), out_shape=(...  206 us
  transfers between devices with their start and end apart: 2, of which 0 were waited for; matrix products, arithmetic and copies ran while one was open for 5% of the time, Pallas kernels for 0%

profile of v3, /device:TPU:0, one launch (start us, length us, event | category | flops | bytes accessed | tf_op | source)
XLA Modules:
  0.0 555.9 jit_solution(1836833723265518620)
XLA Ops:
  0.6 2.9 copy.27
  3.5 0.0 copy-start.9
  3.5 2.6 copy.22
  6.1 0.0 copy-done.9
  6.2 0.0 copy-start.5
  6.2 2.4 dynamic-slice_bitcast_fusion.3.x_in
  8.6 0.0 copy-done.5
  8.6 1.0 dynamic-slice_bitcast_fusion.1.cot
  9.6 0.0 copy-start.10
  9.6 0.0 copy-start.4
  9.6 4.0 pad_maximum_fusion.1
  13.7 0.0 copy-done.10
  13.7 0.6 fusion.3.vec
  14.3 0.0 copy-done.4
  14.3 0.0 copy-start.6
  14.3 0.0 copy-start.7
  14.3 0.0 copy-start.8
  14.3 6.1 %pad_maximum_fusion.shard = bf16[12,256,1024]{2,1,0:T(8,128)(2,1)} fusion(bf16[8,256,1024]{2,1,0:T(8,128)(2,1)} %bitcast.45, bf16[1,256,1024]{2,1,0:T(8,128)(2,1)S(1)} %copy-done.4, bf16[3,256,1024]{2,1,0:T(8,128)(2,1)} %bitcast.48), kind=kLoop, calls=%fused_computation | loop fusion | flops 6291456 | bytes 12582912 | tf_op jit(solution)/shard_map/concatenate | solution.py:1240
  20.4 0.0 copy-done.6
  20.4 0.0 copy-done.7
  20.4 0.0 copy-done.8
  20.4 0.6 select_maximum_fusion.norm_in
  21.0 205.5 %shard_map.194 = (bf16[2,12288,1024]{2,1,0:T(8,128)(2,1)}, f32[2,4,8,256]{3,2,1,0:T(8,128)}, f32[2,8,1024]{2,1,0:T(8,128)}, bf16[2,4,4,512,256]{4,3,2,1,0:T(8,12...) custom-call(bf16[512,1024]{1,0:T(8,128)(2,1)} %dynamic-slice_bitcast, ...), custom_call_target="tpu_custom_call" | custom-call | tf_op jit(solution)/shard_map/pallas_call | solution.py:810
  226.6 292.3 %shard_map.195 = (bf16[12,2,128,1024]{3,2,1,0:T(8,128)(2,1)}, bf16[2,512,1024]{2,1,0:T(8,128)(2,1)}, f32[2,16,1024]{2,1,0:T(8,128)}) custom-call(bf16[512,1024]{1,0:T(8,128)(2,1)} %dynamic-slice_bitcast_fusion.3.x_in, bf16[512,1024]{1,0:T(8,128)(2,1)} %dynamic-slice_bitcast_fusion.1.cot, bf16[2,12288,1024]{2,1,0:T(8,128)(2,1)} %get-tuple-element.23.full, ...), custom_call_target="tpu_custom_call" | custom-call | tf_op jit(solution)/shard_map/pallas_call | solution.py:1192
  518.9 0.0 copy-start
  518.9 0.0 copy-start.1
  518.9 3.2 dynamic-slice_bitcast_fusion
  522.1 0.0 collective-permute-start.1
  522.1 0.0 copy-done
  522.1 1.5 dynamic-slice_bitcast_fusion.2
  523.6 0.5 collective-permute-start
  524.1 0.3 copy-done.1
  524.5 1.8 fusion.4
  526.3 0.2 slice.44
  526.4 2.6 bitcast_convert_fusion
  529.0 0.5 bitcast_convert_fusion.1
  529.5 1.9 slice.47
  531.4 5.3 copy.26
  536.8 4.1 convert.13
  540.8 2.4 copy.25
  543.2 0.0 copy-start.2
  543.2 1.4 dynamic-slice.4
  544.6 0.8 dynamic-slice_bitcast_fusion.4
  545.3 0.6 copy.28
  545.9 0.7 constant_dynamic-slice_fusion
  546.7 0.6 fusion.5
  547.3 2.1 bitcast_convert_fusion.2
  549.4 0.0 collective-permute-done.1
  549.4 0.0 copy-done.2
  549.4 0.0 copy-start.3
  549.4 3.3 maximum_select_fusion.1
  552.7 0.0 collective-permute-done
  552.7 0.0 copy-done.3
  552.7 3.3 maximum_select_fusion
  (2 shorter events, 0.0 us)
Async XLA Ops:
  3.5 2.6 copy-start.9
  6.2 2.4 copy-start.5
  9.6 4.1 copy-start.10
  9.6 4.7 copy-start.4
  14.3 6.1 %copy-start.6 = (f32[1,2,1024]{2,1,0:T(2,128)S(1)}, f32[1,2,1024]{2,1,0:T(2,128)}, u32[]{:S(2)}) copy-start(f32[1,2,1024]{2,1,0:T(2,128)} %param.21) | copy-start | bytes 24580
  14.3 6.1 %copy-start.7 = (f32[1,2,1024]{2,1,0:T(2,128)S(1)}, f32[1,2,1024]{2,1,0:T(2,128)}, u32[]{:S(2)}) copy-start(f32[1,2,1024]{2,1,0:T(2,128)} %param.20) | copy-start | bytes 24580
  14.3 6.1 %copy-start.8 = (f32[1,2,1024]{2,1,0:T(2,128)S(1)}, f32[1,2,1024]{2,1,0:T(2,128)}, u32[]{:S(2)}) copy-start(f32[1,2,1024]{2,1,0:T(2,128)} %param.19) | copy-start | bytes 24580
  518.9 3.3 copy-start
  518.9 5.6 %copy-start.1 = (bf16[12,2,128,1024]{3,2,1,0:T(8,128)(2,1)S(1)}, bf16[12,2,128,1024]{3,2,1,0:T(8,128)(2,1)}, u32[]{:S(2)}) copy-start(bf16[12,2,128,1024]{3,2,1,0:T(8,128)(2,1)} %get-tuple-element.31) | copy-start | bytes 18874372
  522.1 27.2 %collective-permute-start.1 = (bf16[1,512,1024]{2,1,0:T(8,128)(2,1)}, bf16[1,512,1024]{2,1,0:T(8,128)(2,1)}, u32[]{:S(2)}, u32[]{:S(2)}) collective-permute-start(bf16[1,512,1024]{2,1,0:T(8,128)(2,1)} %get-tuple-element.36), channel_id=1, source_target_pairs={{0,16},{16,0},{1,17},{17,1},{2,18},{18,2},{3,19},{19,3},{4,20},{20... | collective-permute-start | bytes 3145736 | tf_op jit(solution)/shard_map/ppermute | solution.py:1216
  523.6 29.0 %collective-permute-start = (bf16[1,512,1024]{2,1,0:T(8,128)(2,1)}, bf16[1,512,1024]{2,1,0:T(8,128)(2,1)}, u32[]{:S(2)}, u32[]{:S(2)}) collective-permute-start(bf16[1,512,1024]{2,1,0:T(8,128)(2,1)} %get-tuple-element.38), channel_id=1, source_target_pairs={{0,16},{16,0},{1,17},{17,1},{2,18},{18,2},{3,19},{19,3},{4,20},{20... | collective-permute-start | bytes 3145736 | tf_op jit(solution)/shard_map/ppermute | solution.py:1216
  543.2 6.2 %copy-start.2 = (bf16[1,1,512,1024]{3,2,1,0:T(8,128)(2,1)S(1)}, bf16[1,1,512,1024]{3,2,1,0:T(8,128)(2,1)}, u32[]{:S(2)}) copy-start(bf16[1,1,512,1024]{3,2,1,0:T(8,128)(2,1)} %get-tuple-element.35) | copy-start | bytes 3145732
  549.4 3.3 copy-start.3

commit v4 on v3

--- a/solution.py
+++ b/solution.py
@@ -396,15 +396,6 @@
     lax.fori_loop(0, rows // step, run, 0)
 
 
-def ffn_block(hb, w, bias, save, acc):
-    z = dot_nt(hb[...], w[0]) + bias
-    inner = 0.5 + 0.5 * lax.erf(z * math.sqrt(0.5))
-    g = low(z * inner)
-    save[0] = g
-    save[1] = low(inner + z * jnp.exp(-0.5 * z * z) * (1.0 / math.sqrt(2.0 * math.pi)))
-    acc[...] += dot(g, w[1])
-
-
 def first_norm(x, nrm, acc, u1, hb):
     def run(rows):
         u = acc[rows] + nrm[0:1] + high(x[rows])
@@ -487,16 +478,23 @@
         save[3, :, cols] = low(dot(low(softmax(q[:, cols], k[:, cols])), v[:, cols]))
 
 
+def unit_values(hb, w, bias):
+    z = dot_nt(hb[...], w) + bias
+    inner = 0.5 + 0.5 * lax.erf(z * math.sqrt(0.5))
+    slope = inner + z * jnp.exp(-0.5 * z * z) * (1.0 / math.sqrt(2.0 * math.pi))
+    return low(z * inner), low(slope)
+
+
 def gather_forward_kernel(
-    dim, x_in, shard, vec, norm_in, full, vecs, norms, qkvo, gd, us, hbs, outs,
-    x, acc, u, hb, wa, wf, sa, sf, wasem, wfsem, sasem, sfsem, usem,
-    ini_s, ini_r, loc, x1ss, x1rs, y1ss, y1rs, x2ss, x2rs, y2ss, y2rs, zs, zr, cs, cr, vs, vr, vloc,
+    dim, tokens, w_qkv, w_out, w_up, w_down, vec, norm_in, full, vecs, norms, qkvo, gd, us, hbs, between, acts,
+    turned, x, acc, u, hb, wa, wf, sa, gb, sd, wasem, wfsem, sasem, gbsem, sdsem, usem,
+    ini_s, ini_r, loc, x1ss, x1rs, y1ss, y1rs, x2ss, x2rs, y2ss, y2rs, zs, zr, cs, cr, vs, vr, vloc, as_, ar,
 ):
     c, p, d = lax.axis_index("section"), lax.axis_index("mp"), lax.axis_index("dp")
     near = neighbours()
     near["pair"] = (c, p, d + 1 - 2 * lax.rem(d, 2))
     spots = places()
-    rows = shard.shape[1] // 2
+    rows = w_out.shape[0] // 2
     half = rows // 2
     odd = lax.rem(d, 2)
     others = [(cc, spots[r], d) for r in range(4) for cc in (c, 1 - c)][1:]
@@ -508,8 +506,7 @@
 
     def place_of(s, spot, h):
         k = lax.rem(s, 12)
-        b, kind = (k - 4) // 2, lax.rem(k, 2)
-        row = jnp.where(k < 4, k * 8 + spot * 2, 32 + kind * 32 + spot * 8 + b * 2)
+        row = jnp.where(k < 4, k * 8 + spot * 2, 32 + (k // 4 - 1) * 32 + spot * 8 + lax.rem(k, 4) * 2)
         return s // 12, (row + h) * rows
 
     def block(s, spot, h, start=0, size=rows):
@@ -520,11 +517,26 @@
         row = place_of(12 * layer + k, p, 0)[1]
         return full.at[layer, pl.ds(pl.multiple_of(row, half), 2 * rows)]
 
+    def turn(k):
+        if k < 3:
+            turned[k] = w_qkv[k].T
+        elif 4 <= k < 8:
+            turned[k - 1] = w_up[:, 2 * rows * (k - 4) : 2 * rows * (k - 3)].T
+
+    def chunk(k):
+        if k == 3:
+            return w_out
+        if k < 8:
+            return turned.at[k if k < 3 else k - 1]
+        return w_down.at[pl.ds(2 * rows * (k - 8), 2 * rows)]
+
+    def init_start(k):
+        turn(k)
+        pltpu.make_async_copy(chunk(k), init_place(k, c), loc.at[k]).start()
+        remote(chunk(k), init_place(k, c), ini_s.at[k], ini_r.at[k], near["core"]).start()
+
     def init_local(k):
-        return pltpu.make_async_copy(shard.at[k], init_place(k, c), loc.at[k])
-
-    def init_remote(k):
-        return remote(shard.at[k], init_place(k, c), ini_s.at[k], ini_r.at[k], near["core"])
+        return pltpu.make_async_copy(init_place(k, c), init_place(k, c), loc.at[k])
 
     def init_wait(k):
         there = init_place(k, 1 - c)
@@ -574,36 +586,49 @@
         b = block(s, spots[r], 1 - c)
         return remote(b, b, cs.at[s, r - 1], cr.at[s, r - 1], near["core"])
 
-    def stage_a(t):
-        for j in range(3):
-            s = 3 * t + j
-
-            @pl.when(s // 12 != c)
+    def sent_chunk(j):
+        t, n = j // 2, lax.rem(j, 2)
+        return 3 * t + (1 - n) * (1 + odd), n == 0
+
+    def stage_a(j):
+        s = sent_chunk(j)[0]
+        for m in range(3):
+            own = 3 * (j // 2) + m
+
+            @pl.when((own // 12 != c) & (lax.rem(j, 2) == 0))
             def _():
-                init_wait(lax.rem(s, 12))
-
-        for s in (3 * t, 3 * t + 1 + odd):
-            first(s, "x").start()
-            first(s, "y").start()
-
-    def stage_b(t):
-        for n, s in enumerate((3 * t, 3 * t + 1 + odd)):
-            arrived(s, "x").wait_recv()
-            relay(s, "y").start()
-            arrived(s, "y").wait_recv()
-            relay(s, "x").start()
+                init_wait(lax.rem(own, 12))
+
+            @pl.when((own // 12 == c) & (lax.rem(j, 2) == 0))
+            def _():
+                init_local(lax.rem(own, 12)).wait()
+
+        first(s, "x").start()
+        first(s, "y").start()
+
+    def stage_b(j):
+        s, shared = sent_chunk(j)
+        arrived(s, "x").wait_recv()
+        relay(s, "y").start()
+        arrived(s, "y").wait_recv()
+        relay(s, "x").start()
+        for r in (1, 2):
+            to_core(s, r).start()
+
+        @pl.when(shared)
+        def _():
             for r in (1, 2):
-                to_core(s, r).start()
-                if n:
-                    to_pair(s, r).start()
-
-    def stage_c(t):
-        for n, s in enumerate((3 * t, 3 * t + 1 + odd)):
-            relayed(s, "x").wait_recv()
-            relayed(s, "y").wait_recv()
-            to_core(s, 3).start()
-            if n:
-                to_pair(s, 3).start()
+                to_pair(s, r).start()
+
+    def stage_c(j):
+        s, shared = sent_chunk(j)
+        relayed(s, "x").wait_recv()
+        relayed(s, "y").wait_recv()
+        to_core(s, 3).start()
+
+        @pl.when(shared)
+        def _():
+            to_pair(s, 3).start()
 
     def stage_d(t):
         s = 3 * t + 2 - odd
@@ -631,179 +656,262 @@
 
     wide = 2 * rows
 
-    def attn(l, q, slot):
-        return weight_copies(full, l, 0, q, 0, wa.at[slot], wasem.at[slot], wide)[:3]
-
-    def attn_out(l, q, slot):
-        return weight_copies(full, l, 0, q, 0, wa.at[slot], wasem.at[slot], wide)[3]
-
-    def ffn(l, n, slot):
-        return weight_copies(full, l, 1, lax.rem(n, 4), n // 4, wf.at[slot], wfsem.at[slot], wide)
-
-    def save_attn(l, q, slot):
-        return pltpu.make_async_copy(sa.at[q], qkvo.at[l, q], sasem.at[slot])
-
-    def save_ffn(l, n, slot):
-        return pltpu.make_async_copy(sf.at[slot], gd.at[l, 4 * lax.rem(n, 4) + n // 4], sfsem.at[slot])
-
-    def attention_segment(l):
-        for copy in attn(l, 0, 0):
-            copy.start()
-
-        def run(q, carry):
-            slot = lax.rem(q, 2)
-            for copy in attn(l, q, slot):
-                copy.wait()
-
-            @pl.when(q < 3)
-            def _():
-                for copy in attn(l, q + 1, 1 - slot):
-                    copy.start()
-
-            project_block(x, wa.at[slot], vecs[l, q], sa.at[q], dim)
-            save_attn(l, q, q).start()
-            return carry
-
-        lax.fori_loop(0, 4, run, 0)
-
-    def ffn_segment(l, begin, count):
-        for copy in ffn(l, begin, 0):
-            copy.start()
-
-        def run(m, carry):
-            slot = lax.rem(m, 2)
-            n = begin + m
-            for copy in ffn(l, n, slot):
-                copy.wait()
-
-            @pl.when(m < count - 1)
-            def _():
-                for copy in ffn(l, n + 1, 1 - slot):
-                    copy.start()
-
-            @pl.when(m >= 2)
-            def _():
-                save_ffn(l, n - 2, slot).wait()
-
-            ffn_block(hb, wf.at[slot], vecs[l, lax.rem(n, 4), pl.ds(2 + n // 4, 1)], sf.at[slot], acc)
-            save_ffn(l, n, slot).start()
-            return carry
-
-        lax.fori_loop(0, count, run, 0)
-        for m in (count - 2, count - 1):
-            save_ffn(l, begin + m, m % 2).wait()
+    def weights(l, number, place, sem):
+        begin = pl.multiple_of(number * wide, wide)
+        return pltpu.make_async_copy(full.at[l, pl.ds(begin, wide)], place, sem)
+
+    def load_qkv(l, q):
+        return [weights(l, 4 * n + q, wa.at[q, n], wasem.at[q, n]) for n in range(3)]
+
+    def load(l, number, slot):
+        return weights(l, number, wf.at[slot], wfsem.at[slot])
+
+    def load_out(l, q):
+        return load(l, 12 + q, q)
+
+    def load_in(l, b, q, slot):
+        return load(l, 16 + 4 * q + b, slot)
+
+    def load_down(l, b, q, slot):
+        return load(l, 32 + 4 * q + b, slot)
+
+    def save_attn(l, q):
+        return pltpu.make_async_copy(sa.at[q], qkvo.at[l, q], sasem.at[q])
+
+    def save_g(l, n):
+        return pltpu.make_async_copy(gb.at[n], gd.at[l, n, 0], gbsem.at[n])
+
+    def save_d(l, n, slot):
+        return pltpu.make_async_copy(sd.at[slot], gd.at[l, n, 1], sdsem.at[slot])
 
     def keep(l, which):
         if which == 2:
             return pltpu.make_async_copy(hb, hbs.at[l], usem.at[2])
         if which == 3:
-            return pltpu.make_async_copy(x, outs.at[l], usem.at[3])
+            return pltpu.make_async_copy(x, between, usem.at[3])
         return pltpu.make_async_copy(u, us.at[l, which], usem.at[which])
 
+    def give(l, begin):
+        @pl.when(l == c)
+        def _():
+            copy = pltpu.make_async_copy(x, acts.at[c], as_.at[0])
+            copy.start() if begin else copy.wait()
+
+        @pl.when(l != c)
+        def _():
+            copy = remote(x, acts.at[c], as_.at[0], ar.at[0], near["core"])
+            copy.start() if begin else copy.wait_send()
+
+    def kept(l):
+        @pl.when(l == 0)
+        def _():
+            keep(0, 3).wait()
+
+        give(l, False)
+
+    def each(count, body):
+        def run(q, carry):
+            body(q)
+            return carry
+
+        lax.fori_loop(0, count, run, 0)
+
+    def attention_segment(l, q):
+        for copy in load_qkv(l, q):
+            copy.wait()
+        project_block(x, wa.at[q], vecs[l, q], sa.at[q], dim)
+        save_attn(l, q).start()
+
     def out_segment(l):
-        for q in range(2):
-            attn_out(l, q, q).start()
+        @pl.when(l == 1)
+        def _():
+            keep(0, 1).wait()
+
         acc[...] = jnp.zeros_like(acc)
-        for q in range(4):
-            attn_out(l, q, q % 2).wait()
-            acc[...] += dot(sa[q, 3], wa[q % 2, 3])
-            if q < 2:
-                attn_out(l, q + 2, q).start()
-        for q in range(4):
-            save_attn(l, q, q).wait()
-
-        @pl.when(l == 1)
-        def _():
-            keep(0, 1).wait()
-
+
+        def branch(q):
+            load_out(l, q).wait()
+            acc[...] += dot(sa[q, 3], wf[q])
+            load_in(l, 1, q, q).start()
+
+        each(4, branch)
         first_norm(x, norms.at[l], acc, u, hb)
         keep(l, 0).start()
         keep(l, 2).start()
 
+    def up_segment(l, b, slot):
+        def run(q):
+            load_in(l, b, q, slot + q).wait()
+            n, two = 4 * q + b, lax.rem(q, 2)
+
+            @pl.when(q >= 2)
+            def _():
+                save_d(l, n - 8, two).wait()
+
+            g, slope = unit_values(hb, wf[slot + q], vecs[l, q, pl.ds(2 + b, 1)])
+            gb[n] = g
+            sd[two] = slope
+            save_g(l, n).start()
+            save_d(l, n, two).start()
+
+        each(4, run)
+        for q in (2, 3):
+            save_d(l, 4 * q + b, q % 2).wait()
+
+    def down_segment(l, b, slot):
+        def run(q):
+            load_down(l, b, q, slot + q).wait()
+            acc[...] += dot(gb[4 * q + b], wf[slot + q])
+
+        each(4, run)
+
     def end_segment(l):
         keep(l, 0).wait()
         keep(l, 2).wait()
+        each(4, lambda q: save_attn(l, q).wait())
+        each(16, lambda n: save_g(l, n).wait())
 
         @pl.when(l == 1)
         def _():
-            keep(0, 3).wait()
+            kept(0)
 
         second_norm(norms.at[l], acc, u, x)
         keep(l, 1).start()
-        keep(l, 3).start()
-
-    def compute(t):
-        l, part = t // 4, lax.rem(t, 4)
-
-        @pl.when(t == 0)
-        def _():
-            for copy in small_local():
-                copy.wait()
-            for copy in small():
-                copy.wait_send()
-            for cc, spot in [(cc, spots[r]) for r in range(4) for cc in (c, 1 - c)][1:]:
-                remote(vec, vecs.at[cc, spot], vs.at[0], vr.at[cc, spot], near["core"]).wait_recv()
-            remote(norm_in, norms.at[1 - c], vs.at[7], vr.at[0, 4], near["core"]).wait_recv()
-
-        @pl.when(part == 0)
-        def _():
-            attention_segment(l)
-
-        @pl.when(part == 1)
-        def _():
+        give(l, True)
+
+        @pl.when(l == 0)
+        def _():
+            keep(0, 3).start()
+
+    def small_there():
+        for copy in small_local():
+            copy.wait()
+        for copy in small():
+            copy.wait_send()
+        for cc, spot in [(cc, spots[r]) for r in range(4) for cc in (c, 1 - c)][1:]:
+            remote(vec, vecs.at[cc, spot], vs.at[0], vr.at[cc, spot], near["core"]).wait_recv()
+        remote(norm_in, norms.at[1 - c], vs.at[7], vr.at[0, 4], near["core"]).wait_recv()
+
+    def compute(m):
+        l, part = m // 8, lax.rem(m, 8)
+
+        def at(number, body):
+            @pl.when(part == number)
+            def _():
+                body()
+
+        def attention_first():
+            for q in range(4):
+                for copy in load_qkv(l, q):
+                    copy.start()
+
+            @pl.when(m == 0)
+            def _():
+                small_there()
+                first_rows.wait()
+
+        def attention_half(begin):
+            each(2, lambda q: attention_segment(l, begin + q))
+
+        def out_part():
+            for q in range(4):
+                load_out(l, q).start()
+            for q in range(4):
+                load_in(l, 0, q, 4 + q).start()
             out_segment(l)
 
-        @pl.when(part > 0)
-        def _():
-            ffn_segment(l, 4 * (part - 1), 4)
-
-        @pl.when(part == 3)
-        def _():
-            ffn_segment(l, 12, 4)
+        def up_part():
+            for q in range(4):
+                load_in(l, 2, q, q).start()
+            for q in range(4):
+                load_in(l, 3, q, 4 + q).start()
+            up_segment(l, 2, 0)
+            for q in range(4):
+                load_down(l, 0, q, q).start()
+
+        def turn_part():
+            up_segment(l, 3, 4)
+            down_segment(l, 0, 0)
+
+        def down_part():
+            for b in (1, 2):
+                for q in range(4):
+                    load_down(l, b, q, 4 * (b - 1) + q).start()
+            down_segment(l, 1, 0)
+            for q in range(4):
+                load_down(l, 3, q, q).start()
+            down_segment(l, 2, 4)
+
+        def end_part():
+            down_segment(l, 3, 0)
             end_segment(l)
 
-    def begin(k, carry):
-        init_local(k).start()
-        init_remote(k).start()
-        return carry
-
-    lax.fori_loop(0, 12, begin, 0)
+        at(0, attention_first)
+
+        @pl.when(part < 2)
+        def _():
+            attention_half(2 * part)
+
+        at(2, out_part)
+
+        @pl.when((part == 2) | (part == 3))
+        def _():
+            b = part - 2
+            up_segment(l, b, 4 - 4 * b)
+
+        at(4, up_part)
+        at(5, turn_part)
+        at(6, down_part)
+        at(7, end_part)
+
+    first_rows = pltpu.make_async_copy(tokens.at[c], x, usem.at[4])
+    first_rows.start()
+    for k in range(3):
+        init_start(k)
     for copy in small_local() + small():
         copy.start()
-    x[...] = x_in[...]
-
-    def local_done(k, carry):
-        init_local(k).wait()
-        return carry
-
-    lax.fori_loop(0, 12, local_done, 0)
-
-    def step(i, carry):
+
+    def step(count, carry):
+        i = count - 1
+
         def run(stage, lag):
-            @pl.when((i >= lag) & (i < TRIPLES + lag))
+            @pl.when((i >= lag) & (i < 2 * TRIPLES + lag))
             def _():
                 stage(i - lag)
 
-        for lag, stage in enumerate((stage_a, stage_b, stage_c, stage_d, stage_e)):
-            run(stage, lag)
-        run(compute, 4)
-        run(stage_f, 5)
+        def run_late(stage, lag):
+            @pl.when((i >= lag) & (i < 2 * TRIPLES + lag) & (lax.rem(i - lag, 2) == 0))
+            def _():
+                stage((i - lag) // 2)
+
+        run(stage_a, -1)
+        run(stage_b, 1)
+        run(stage_c, 2)
+        run_late(stage_d, 4)
+        run_late(stage_e, 5)
+        run_late(stage_f, 6)
+        for t in range(3):
+
+            @pl.when(i == 2 * t)
+            def _():
+                for k in range(3 * t + 3, 3 * t + 6):
+                    init_start(k)
+
+        run(compute, 5)
         return carry
 
-    lax.fori_loop(0, TRIPLES + 5, step, 0)
-
-    def sent(k, carry):
-        init_remote(k).wait_send()
-        return carry
-
-    lax.fori_loop(0, 12, sent, 0)
+    lax.fori_loop(0, 2 * TRIPLES + 6, step, 0)
+
+    for k in range(12):
+        remote(chunk(k), init_place(k, c), ini_s.at[k], ini_r.at[k], near["core"]).wait_send()
     keep(1, 1).wait()
-    keep(1, 3).wait()
-
-
-def gather_forward(dim, x, shard, vec, norms):
-    rows, width = shard.shape[1:]
-    seq = x.shape[0]
+    kept(1)
+    remote(x, acts.at[1 - c], as_.at[0], ar.at[0], near["core"]).wait_recv()
+
+
+def gather_forward(dim, tokens, w_qkv, w_out, w_up, w_down, vec, norms):
+    rows, width = w_out.shape
+    seq = tokens.shape[1]
     bf, f32, dma, v = jnp.bfloat16, jnp.float32, pltpu.SemaphoreType.DMA, pltpu.VMEM
     hbm, vmem = pl.BlockSpec(memory_space=pl.ANY), pl.BlockSpec(memory_space=pltpu.VMEM)
     S = jax.ShapeDtypeStruct
@@ -812,25 +920,27 @@
         out_shape=(
             S((2, 48 * rows, width), bf), S((2, 4) + vec.shape, f32), S((2,) + norms.shape, f32),
             S((2, 4, 4, seq, rows), bf), S((2, 16, 2, seq, rows), bf), S((2, 2, seq, width), f32),
-            S((2, seq, width), bf), S((2, seq, width), bf),
+            S((2, seq, width), bf), S((seq, width), bf), S((2, seq, width), bf),
         ),
-        in_specs=[vmem, vmem, vmem, vmem],
-        out_specs=[hbm, vmem, vmem] + [hbm] * 5,
+        in_specs=[hbm] + [vmem] * 6,
+        out_specs=[hbm, vmem, vmem] + [hbm] * 6,
         scratch_shapes=[
+            v((7, rows, width), bf),
             v((seq, width), bf), v((seq, width), f32), v((seq, width), f32), v((seq, width), bf),
-            v((2, 4, rows, width), bf), v((2, 2, rows, width), bf), v((4, 4, seq, rows), bf), v((2, 2, seq, rows), bf),
-            dma((2, 4)), dma((2, 2)), dma((4,)), dma((2,)), dma((4,)),
-        ] + [dma((12,))] * 3 + [dma((24,))] * 8 + [dma((24, 3))] * 4 + [dma((8,)), dma((2, 5)), dma((2,))],
-        compiler_params=pltpu.CompilerParams(collective_id=0, has_side_effects=True, vmem_limit_bytes=56 * 2**20),
-    )(x, shard, vec, norms)
+            v((4, 3, rows, width), bf), v((8, rows, width), bf), v((4, 4, seq, rows), bf), v((16, seq, rows), bf),
+            v((2, seq, rows), bf), dma((4, 3)), dma((8,)), dma((4,)), dma((16,)), dma((2,)), dma((5,)),
+        ] + [dma((12,))] * 3 + [dma((24,))] * 8 + [dma((24, 3))] * 4
+        + [dma((8,)), dma((2, 5)), dma((2,)), dma((1,)), dma((1,))],
+        compiler_params=pltpu.CompilerParams(collective_id=0, has_side_effects=True, vmem_limit_bytes=60 * 2**20),
+    )(tokens, w_qkv, w_out, w_up, w_down, vec, norms)
 
 
 def backward_reduce_kernel(
-    dim, x_in, cot, full, vecs, norms, qkvo, gd, us, hbs, outs, out, dxs, totals,
+    dim, tokens, cots, full, norms, qkvo, gd, us, hbs, between, out, grads, totals,
     left, right, acc, g, u, wa, wf, da, df, trades,
     sendc, recvc, keep, x1s, x1r, y1s, y1r, part, base, x2s, x2r, y2s, y2r, mid,
     zk, zs1, zr1, zs2, zr2, zs3, zr3,
-    wasem, wfsem, dasem, dfsem, gsem, osem4, bsem, tss, trs,
+    wasem, wfsem, dasem, dfsem, gsem, osem4, bsem, gds, gdr, tss, trs,
     cs, cr, x1ss, x1rs, y1ss, y1rs, x2ss, x2rs, y2ss, y2rs, z1ss, z1rs, z2ss, z2rs, z3ss, z3rs, os, orr,
 ):
     c, p, d = lax.axis_index("section"), lax.axis_index("mp"), lax.axis_index("dp")
@@ -1011,8 +1121,16 @@
             pltpu.make_async_copy(qkvo.at[l, q], da.at[slot], dasem.at[slot])
         ]
 
-    def store_dx(l):
-        return pltpu.make_async_copy(g, dxs.at[l], bsem.at[3])
+    def store_dx(l, begin):
+        @pl.when(l == c)
+        def _():
+            copy = pltpu.make_async_copy(g, grads.at[c], gds.at[0])
+            copy.start() if begin else copy.wait()
+
+        @pl.when(l != c)
+        def _():
+            copy = remote(g, grads.at[c], gds.at[0], gdr.at[0], near["core"])
+            copy.start() if begin else copy.wait_send()
 
     def ahead(l):
         load_u(l, 1).start()
@@ -1088,7 +1206,7 @@
 
     def end_segment(l):
         by_rows(acc.shape[0], 64, lambda r: g.__setitem__(r, low(acc[r])))
-        store_dx(l).start()
+        store_dx(l, True)
 
         @pl.when(l == 1)
         def _():
@@ -1100,7 +1218,7 @@
         @pl.when(i == 9)
         def _():
             operands(0)
-            store_dx(1).wait()
+            store_dx(1, False)
 
         @pl.when(j == 0)
         def _():
@@ -1124,66 +1242,67 @@
 
         @pl.when(i == 8)
         def _():
-            load_x(outs.at[0]).wait()
+            load_x(between).wait()
 
         @pl.when(i == 12)
         def _():
             operands_there(0)
-            load_x(x_in).start()
+            load_x(tokens.at[c]).start()
 
         @pl.when(i == 16)
         def _():
-            load_x(x_in).wait()
-
-    def trade(k, name):
-        copy = remote(totals, trades.at[k], tss.at[k], trs.at[k], near[name])
-        copy.start()
-        copy.wait()
-        totals[...] += trades[k]
-
-    first_rows = pltpu.make_async_copy(cot, g, bsem.at[3])
+            load_x(tokens.at[c]).wait()
+
+    def trade(k):
+        return remote(totals, trades.at[k], tss.at[k], trs.at[k], near[("core", "x", "y", "pair", "far")[k]])
+
+    first_rows = pltpu.make_async_copy(cots.at[c], g, bsem.at[3])
     first_rows.start()
     ahead(1)
     operands(1)
-    load_x(outs.at[0]).start()
+    load_x(between).start()
     totals[...] = jnp.zeros_like(totals)
     first_rows.wait()
 
-    def step(i, carry):
+    def step(count, carry):
+        i = count - 1
+
         def run(stage, lag, *extra):
             @pl.when((i >= lag) & (i < CHUNKS + lag))
             def _():
                 stage(i - lag, *extra)
 
-        run(stage1, 1)
-
-        @pl.when(i < 18)
-        def _():
-            segment(i)
-
-        run(stage0, 0)
-        run(stage2, 2)
-        run(stage3, 3)
-        run(stage4, 4)
-        run(stage5, 5)
+        for lag, stage in enumerate((stage1, stage2, stage3, stage4, stage5)):
+            run(stage, lag + 1)
         run(stage6, 6, True)
         run(stage6, 7, False)
-        for k, name in enumerate(("core", "x", "y", "pair", "far")):
-
-            @pl.when(i == 19 + k)
+        for k in range(6):
+
+            @pl.when(i == 18 + k)
             def _():
-                trade(k, name)
+                if k:
+                    trade(k - 1).wait()
+                    totals[...] += trades[k - 1]
+                if k < 5:
+                    trade(k).start()
+
+        run(stage0, 0)
+
+        @pl.when(i < 17)
+        def _():
+            segment(i + 1)
 
         return carry
 
-    lax.fori_loop(0, CHUNKS + 8, step, 0)
-    store_dx(0).wait()
+    lax.fori_loop(0, CHUNKS + 9, step, 0)
+    store_dx(0, False)
+    remote(g, grads.at[1 - c], gds.at[0], gdr.at[0], near["core"]).wait_recv()
     for k in range(12):
         remote(zs3.at[0], out.at[k, 1 - c], os.at[0], orr.at[k], near["core"]).wait_recv()
 
 
-def backward_reduce(dim, x, cot, full, vecs, norms, saved):
-    seq, width = x.shape
+def backward_reduce(dim, tokens, cots, full, norms, saved):
+    seq, width = tokens.shape[1:]
     wide = width // 4
     block, half = wide // 2, wide // 4
     bf, f32, dma, v = jnp.bfloat16, jnp.float32, pltpu.SemaphoreType.DMA, pltpu.VMEM
@@ -1192,7 +1311,7 @@
     return pl.pallas_call(
         functools.partial(backward_reduce_kernel, dim),
         out_shape=(S((12, 2, block, width), bf), S((2, seq, width), bf), S((2, 16, width), f32)),
-        in_specs=[hbm, hbm, hbm, vmem, vmem] + [hbm] * 5,
+        in_specs=[hbm, hbm, hbm, vmem] + [hbm] * 5,
         out_specs=[hbm, hbm, vmem],
         scratch_shapes=[
             v((48, seq, wide), bf), v((4, seq, width), bf), v((seq, width), f32), v((seq, width), bf),
@@ -1206,14 +1325,68 @@
             v((2, block, width), f32),
             v((2, block, width), f32), v((2, block, width), bf), v((4, block, width), bf),
             v((2, block, width), bf), v((4, block, width), bf), v((6, block, width), bf), v((6, block, width), bf),
-            dma((2, 4)), dma((2, 2)), dma((2,)), dma((2,)), dma((16,)), dma((4,)), dma((4,)), dma((5,)), dma((5,)),
+            dma((2, 4)), dma((2, 2)), dma((2,)), dma((2,)), dma((16,)), dma((4,)), dma((4,)), dma((1,)), dma((1,)), dma((5,)), dma((5,)),
         ] + [dma((n,)) for n in (2, 4) * 7] + [dma((6,)), dma((6,))] + [dma((6,)), dma((12,))],
         compiler_params=pltpu.CompilerParams(collective_id=1, has_side_effects=True, vmem_limit_bytes=63 * 2**20),
-    )(x, cot, full, vecs, norms, *saved)
-
-
-def swap_core(value):
-    return lax.ppermute(value, "section", [(0, 1), (1, 0)])
+    )(tokens, cots, full, norms, *saved)
+
+
+def finish_kernel(parts, acts_in, grads_in, acts, grads, g_qkv, g_out, g_up, g_down,
+                  pb, ab, gb, qb, ob, ub, db, psem, asem, osem):
+    def load(k):
+        return pltpu.make_async_copy(parts.at[k], pb.at[k], psem.at[k])
+
+    others = [(acts_in, ab, acts, 0), (grads_in, gb, grads, 1)]
+    for k in range(12):
+        load(k).start()
+    for source, buffer, place, n in others:
+        pltpu.make_async_copy(source, buffer, asem.at[n]).start()
+    stores = []
+    rows = pb.shape[1]
+
+    def store(source, place):
+        copy = pltpu.make_async_copy(source, place, osem.at[len(stores)])
+        copy.start()
+        stores.append(copy)
+
+    for k in range(12):
+        load(k).wait()
+        if k < 4:
+            span = pl.ds(k * rows, rows)
+            db[span] = high(pb[k])
+            store(db.at[span], g_down.at[span])
+        elif k < 8:
+            ub[:, pl.ds((k - 4) * rows, rows)] = high(pb[k]).T
+            if k == 7:
+                store(ub, g_up)
+        elif k == 8:
+            ob[...] = high(pb[k])
+            store(ob, g_out)
+        else:
+            qb[k - 9] = high(pb[k]).T
+            store(qb.at[k - 9], g_qkv.at[k - 9])
+    for source, buffer, place, n in others:
+        pltpu.make_async_copy(source, buffer, asem.at[n]).wait()
+        store(buffer, place)
+    for copy in stores:
+        copy.wait()
+
+
+def finish(parts, acts, grads):
+    count, rows, width = parts.shape
+    bf, f32, dma, v = jnp.bfloat16, jnp.float32, pltpu.SemaphoreType.DMA, pltpu.VMEM
+    S = jax.ShapeDtypeStruct
+    shapes = [(3, width, rows), (rows, width), (width, width), (width, width)]
+    hbm = pl.BlockSpec(memory_space=pl.ANY)
+    return pl.pallas_call(
+        finish_kernel,
+        out_shape=[S(acts.shape, bf), S(grads.shape, bf)] + [S(shape, f32) for shape in shapes],
+        in_specs=[hbm] * 3,
+        out_specs=[hbm] * 6,
+        scratch_shapes=[v(parts.shape, bf), v(acts.shape, bf), v(grads.shape, bf)] + [v(shape, f32) for shape in shapes]
+        + [dma((12,)), dma((2,)), dma((11,))],
+        compiler_params=pltpu.CompilerParams(vmem_limit_bytes=40 * 2**20),
+    )(parts, acts, grads)
 
 
 def by_page(
@@ -1230,44 +1403,32 @@
     norm_shifts,
 ):
     core, place = lax.axis_index("section"), lax.axis_index("mp")
-    is_first = core == 0
     width = token_in.shape[2]
     quarter = width // 4
-    x = lax.dynamic_index_in_dim(token_in, core, 0, keepdims=False)
-    cot = lax.dynamic_index_in_dim(cotangent, core, 0, keepdims=False)
-    ffn_in_t = w_ffn_in[0].T.reshape(4, 1, quarter, width)
-    ffn = jnp.concatenate([ffn_in_t, w_ffn_out[0].reshape(4, 1, quarter, width)], axis=1)
-    shard = jnp.concatenate(
-        [w_qkv[0].transpose(0, 2, 1), w_attn_out, ffn.reshape(8, quarter, width)], axis=0
-    )
     vec = high(jnp.concatenate([qv_bias[0], ffn_in_bias[0].reshape(4, quarter)], axis=0))
     vec = jnp.pad(vec, ((0, 2), (0, 0)))
     norms = jnp.concatenate([out_biases[0], norm_gains[0], norm_shifts[0]], axis=0)
     norms = jnp.pad(norms, ((0, 2), (0, 0)))
-    full, vecs, all_norms, *saved = gather_forward(HEAD_DIM, x, shard, vec, norms)
-    parts, grads, totals = backward_reduce(HEAD_DIM, x, cot, full, vecs, all_norms, saved)
-    outs = saved[4]
-
-    def trade(both):
-        own = lax.dynamic_index_in_dim(both, core, 0)
-        received = swap_core(lax.dynamic_index_in_dim(both, 1 - core, 0))
-        return jnp.where(is_first, jnp.concatenate([own, received]), jnp.concatenate([received, own]))
-
+    full, vecs, norms, *saved, acts = gather_forward(
+        HEAD_DIM, token_in, w_qkv[0], w_attn_out[0], w_ffn_in[0], w_ffn_out[0], vec, norms
+    )
+    parts, grads, totals = backward_reduce(HEAD_DIM, token_in, cotangent, full, norms, saved)
+    parts = parts.reshape(12, quarter, width)
+    acts, grads, grad_qkv, grad_out, grad_up, grad_down = finish(parts, acts, grads)
     totals = lax.dynamic_index_in_dim(totals, core, 0, keepdims=False)
     own = lax.dynamic_slice_in_dim(totals[8:], place * quarter, quarter, 1)
     piece = width // (lax.axis_size("mp") * lax.axis_size("dp"))
     begin = (place * lax.axis_size("dp") + lax.axis_index("dp")) * piece
     rows = lax.dynamic_slice_in_dim(totals[:8], begin, piece, 1)
-    parts = parts.reshape(12, quarter, width)
     return (
-        trade(outs)[None],
-        trade(grads)[None],
-        high(parts[9:12].transpose(0, 2, 1))[None],
+        acts[None],
+        grads[None],
+        grad_qkv[None],
         own[0:2][None],
-        high(parts[8])[None],
-        high(parts[4:8].reshape(width, width).T)[None],
+        grad_out[None],
+        grad_up[None],
         own[2:6].reshape(1, width),
-        high(parts[0:4].reshape(width, width))[None],
+        grad_down[None],
         rows[0:2][None],
         rows[2:4][None],
         rows[4:6][None],

time: 558 us -> 472 us (0.85)
  Pallas kernels: 498 us -> 457 us
  other arithmetic: 27.3 us -> 3.35 us
  local copies, waits for them, and re-layouts: 29.6 us -> 9.95 us
    pallas_call x1, Pallas kernels: 292 us -> 268 us  [backward_reduce(): pl.pallas_call(functools.partial(backward_reduce_kernel, dim), out_shape=...]
    pallas_call x1, Pallas kernels: 206 us -> 182 us  [gather_forward(): pl.pallas_call(functools.partial(gather_forward_kernel, dim), out_shape=(...]
    concatenate x2 -> x0, other arithmetic: 10.2 us -> none  [the longest x1 6.11 us: by_page(): jnp.concatenate([w_qkv[0].transpose(0, 2, 1), w_attn_out, ffn.reshape(8,...]
    broadcast_in_dim x2 -> x0, local copies, waits for them, and re-layouts: 7.69 us -> none  [the longest x1 5.34 us: by_page(): high(parts[4:8].reshape(width, width).T)[None]]
    pallas_call x0 -> x1, Pallas kernels: none -> 6.85 us  [finish(): pl.pallas_call(finish_kernel, out_shape=[S(acts.shape, bf), S(grads.shape...]
    select_n x2 -> x0, other arithmetic: 6.55 us -> none  [trade(): jnp.where(is_first, jnp.concatenate([own, received]), jnp.concatenate([re...]
    convert_element_type x2 -> x0, other arithmetic: 6.19 us -> none  [high(): return value.astype(jnp.float32)]
  transfers between devices with their start and end apart: 2 -> 0, of which waited for: 0 -> 0; matrix products, arithmetic and copies ran while one was open for 5% -> 0% of each run, Pallas kernels for 0% -> 0%
where the time goes in v4:
time: 472 us; the launch traced here: 471 us
  Pallas kernels  457 us (97%)
  local copies, waits for them, and re-layouts  9.95 us (2%)
    pallas_call x1, Pallas kernels, backward_reduce(): pl.pallas_call(functools.partial(backward_reduce_kernel, dim), out_shape=...  268 us
    pallas_call x1, Pallas kernels, gather_forward(): pl.pallas_call(functools.partial(gather_forward_kernel, dim), out_shape=(...  182 us

profile of v4, /device:TPU:0, one launch (start us, length us, event | category | flops | bytes accessed | tf_op | source)
XLA Modules:
  0.0 470.5 jit_solution(1213916235956459532)
XLA Ops:
  0.6 1.4 select_maximum_fusion.norm_in
  2.0 0.7 reduce
  2.7 1.3 fusion.3.vec
  4.0 181.5 %shard_map.194 = (bf16[2,12288,1024]{2,1,0:T(8,128)(2,1)}, f32[2,4,8,256]{3,2,1,0:T(8,128)}, f32[2,8,1024]{2,1,0:T(8,128)}, bf16[2,4,4,512,256]{4,3,2,1,0:T(8,12...) custom-call(bf16[2,512,1024]{2,1,0:T(8,128)(2,1)} %tokens.3, ...), custom_call_target="tpu_custom_call" | custom-call | tf_op jit(solution)/shard_map/pallas_call | solution.py:918
  185.6 268.2 %shard_map.195 = (bf16[12,2,128,1024]{3,2,1,0:T(8,128)(2,1)}, bf16[2,512,1024]{2,1,0:T(8,128)(2,1)}, f32[2,16,1024]{2,1,0:T(8,128)}) custom-call(bf16[2,512,1024]{2,1,0:T(8,128)(2,1)} %tokens.3, bf16[2,512,1024]{2,1,0:T(8,128)(2,1)} %cots.1, bf16[2,12288,1024]{2,1,0:T(8,128)(2,1)} %get-tuple-element.28.full, f32[2,8,1024]{2,1,0:T(8,128)} %get-tuple-element.29.norms, ...), custom_call_target="tpu_custom_call" | custom-call | tf_op jit(solution)/shard_map/pallas_call | solution.py:1311
  453.7 0.0 copy-start
  453.7 2.8 copy-done
  456.5 0.0 copy-start.1
  456.5 1.6 copy-done.1
  458.1 0.0 copy-start.2
  458.1 1.6 copy-done.2
  459.7 6.8 %shard_map.196 = (bf16[2,512,1024]{2,1,0:T(8,128)(2,1)}, bf16[2,512,1024]{2,1,0:T(8,128)(2,1)}, f32[3,1024,256]{2,1,0:T(8,128)}, f32[256,1024]{1,0:T(8,128)}, f3...) custom-call(bf16[12,256,1024]{2,1,0:T(8,128)(2,1)S(1)} %bitcast.18, bf16[2,512,1024]{2,1,0:T(8,128)(2,1)S(1)} %copy-done.1, ...), custom_call_target="tpu_custom_call" | custom-call | tf_op jit(solution)/shard_map/pallas_call | solution.py:1381
  466.6 0.8 constant_dynamic-slice_fusion
  467.3 0.6 fusion.4
  467.9 0.8 dynamic-slice_bitcast_fusion
  468.7 0.6 copy.22
  469.3 1.3 dynamic-slice.4
  (1 shorter events, 0.0 us)
Async XLA Ops:
  453.7 2.8 copy-start
  456.5 1.6 copy-start.1
  458.1 1.6 copy-start.2

commit v5 on v4

--- a/solution.py
+++ b/solution.py
@@ -979,16 +979,20 @@
         a, b = lax.rem(s, 2), lax.rem(s, 4)
         return remote(src.at[a], dst.at[b], ss.at[a], rs.at[b], near[name])
 
-    x1 = lambda s: link_copy(s, x1s, x1r, x1ss, x1rs, "x")
-    y1 = lambda s: link_copy(s, y1s, y1r, y1ss, y1rs, "y")
+    def first_copy(s, n, src, dst, ss, rs, name):
+        a, b = lax.rem(s, 2), lax.rem(s, 4)
+        return remote(src.at[a, n], dst.at[b, n], ss.at[a, n], rs.at[b, n], near[name])
+
+    x1 = lambda s, n: first_copy(s, n, x1s, x1r, x1ss, x1rs, "x")
+    y1 = lambda s, n: first_copy(s, n, y1s, y1r, y1ss, y1rs, "y")
     x2 = lambda s: link_copy(s, x2s, x2r, x2ss, x2rs, "x")
     y2 = lambda s: link_copy(s, y2s, y2r, y2ss, y2rs, "y")
-    z1 = lambda s: link_copy(s, zs1, zr1, z1ss, z1rs, "inner")
-    z2 = lambda s: link_copy(s, zs2, zr2, z2ss, z2rs, "across")
-
-    def z3(s):
+    z1 = lambda s, n: first_copy(s, n, zs1, zr1, z1ss, z1rs, "inner")
+    z2 = lambda s, n: first_copy(s, n, zs2, zr2, z2ss, z2rs, "across")
+
+    def z3(s, n):
         b = lax.rem(s, 6)
-        return remote(zs3.at[b], zr3.at[b], z3ss.at[b], z3rs.at[b], near["outer"])
+        return remote(zs3.at[b, n], zr3.at[b, n], z3ss.at[b, n], z3rs.at[b, n], near["outer"])
 
     def stage0(s):
         k, slot = lax.rem(s, 12), lax.rem(s, 2)
@@ -1007,68 +1011,70 @@
         far = keep[a, 3] + high(recvc[b, 3])
         x1s[a, 0] = low(far[:half])
         y1s[a, 0] = low(far[half:])
+        x1(s, 0).start()
+        y1(s, 0).start()
         by_x = keep[a, 1] + high(recvc[b, 1])
         x1s[a, 1] = low(by_x[:half])
         part[a, 0] = by_x[half:]
         by_y = keep[a, 2] + high(recvc[b, 2])
         y1s[a, 1] = low(by_y[half:])
         part[a, 1] = by_y[:half]
-        x1(s).start()
-        y1(s).start()
+        x1(s, 1).start()
+        y1(s, 1).start()
         base[a] = keep[a, 0] + high(recvc[b, 0])
 
     def stage2(s):
         a, b = lax.rem(s, 2), lax.rem(s, 4)
-        x1(s).wait()
-        y1(s).wait()
+        x1(s, 0).wait()
         y2s[a] = low(part[a, 1] + high(x1r[b, 0]))
+        y2(s).start()
+        y1(s, 0).wait()
         x2s[a] = low(part[a, 0] + high(y1r[b, 0]))
+        x2(s).start()
+        x1(s, 1).wait()
+        y1(s, 1).wait()
         own = base[a]
-        mid[a, pl.ds(0, half)] = own[:half] + high(x1r[b, 1])
-        mid[a, pl.ds(half, half)] = own[half:] + high(y1r[b, 1])
-        x2(s).start()
-        y2(s).start()
+        mid[a, 0] = own[:half] + high(x1r[b, 1])
+        mid[a, 1] = own[half:] + high(y1r[b, 1])
 
     def stage3(s):
         a, b = lax.rem(s, 2), lax.rem(s, 4)
-        x2(s).wait()
-        y2(s).wait()
-        own = mid[a]
-        top = own[:half] + high(y2r[b])
-        end = own[half:] + high(x2r[b])
-
-        @pl.when(is_end)
-        def _():
-            zs1[a, pl.ds(0, half)] = low(top)
-            zs1[a, pl.ds(half, half)] = low(end)
-            z1(s).start()
-
-        @pl.when(is_mid)
-        def _():
-            zk[a, pl.ds(0, half)] = top
-            zk[a, pl.ds(half, half)] = end
+        for n, copy, got in ((0, y2, y2r), (1, x2, x2r)):
+            copy(s).wait()
+            total = mid[a, n] + high(got[b])
+
+            @pl.when(is_end)
+            def _():
+                zs1[a, n] = low(total)
+                z1(s, n).start()
+
+            @pl.when(is_mid)
+            def _():
+                zk[a, n] = total
 
     def stage4(s):
         a, b = lax.rem(s, 2), lax.rem(s, 4)
-
-        @pl.when(is_end)
-        def _():
-            z1(s).wait_send()
+        for n in range(2):
+
+            @pl.when(is_end)
+            def _():
+                z1(s, n).wait_send()
+
+            @pl.when(is_mid)
+            def _():
+                z1(s, n).wait_recv()
+                zs2[a, n] = low(zk[a, n] + high(zr1[b, n]))
+                z2(s, n).start()
+
+    def stage5(s):
+        a, b, to = lax.rem(s, 2), lax.rem(s, 4), lax.rem(s, 6)
 
         @pl.when(is_mid)
         def _():
-            z1(s).wait_recv()
-            zs2[a] = low(zk[a] + high(zr1[b]))
-            z2(s).start()
-
-    def stage5(s):
-        a, b = lax.rem(s, 2), lax.rem(s, 4)
-
-        @pl.when(is_mid)
-        def _():
-            z2(s).wait()
-            zs3[lax.rem(s, 6)] = low(high(zs2[a]) + high(zr2[b]))
-            z3(s).start()
+            for n in range(2):
+                z2(s, n).wait()
+                zs3[to, n] = low(high(zs2[a, n]) + high(zr2[b, n]))
+                z3(s, n).start()
 
     def stage6(s, begin):
         layer, k, b = 1 - s // 12, lax.rem(s, 12), lax.rem(s, 6)
@@ -1087,13 +1093,15 @@
         @pl.when(is_end)
         def _():
             if begin:
-                z3(s).wait_recv()
+                for n in range(2):
+                    z3(s, n).wait_recv()
             finish(zr3)
 
         @pl.when(is_mid)
         def _():
             if begin:
-                z3(s).wait_send()
+                for n in range(2):
+                    z3(s, n).wait_send()
             finish(zs3)
 
     def load_g(l, n):
@@ -1207,28 +1215,29 @@
     def end_segment(l):
         by_rows(acc.shape[0], 64, lambda r: g.__setitem__(r, low(acc[r])))
         store_dx(l, True)
-
-        @pl.when(l == 1)
-        def _():
+        if l == 1:
             ahead(0)
 
     def segment(i):
-        l, j = 1 - i // 9, lax.rem(i, 9)
-
-        @pl.when(i == 9)
-        def _():
+        l = jnp.where(i < 8, 1, 0)
+        j = jnp.where(i < 8, i, i - 9)
+
+        @pl.when(i == 8)
+        def _():
+            end_segment(1)
             operands(0)
+            load_x(between).wait()
             store_dx(1, False)
 
-        @pl.when(j == 0)
+        @pl.when(j == -1)
         def _():
             top_segment(l)
 
-        @pl.when(j < 4)
+        @pl.when((j >= 0) & (j < 4))
         def _():
             ffn_segment(l, j)
 
-        @pl.when(j == 4)
+        @pl.when(j == 3)
         def _():
             middle_segment(l)
 
@@ -1236,17 +1245,16 @@
         def _():
             attention_segment(l, j - 4)
 
-        @pl.when(j == 8)
-        def _():
-            end_segment(l)
-
-        @pl.when(i == 8)
-        def _():
-            load_x(between).wait()
+        @pl.when(i == 17)
+        def _():
+            end_segment(0)
+
+        @pl.when(i == 11)
+        def _():
+            operands_there(0)
 
         @pl.when(i == 12)
         def _():
-            operands_there(0)
             load_x(tokens.at[c]).start()
 
         @pl.when(i == 16)
@@ -1278,7 +1286,7 @@
         run(stage6, 7, False)
         for k in range(6):
 
-            @pl.when(i == 18 + k)
+            @pl.when(i == 19 + k)
             def _():
                 if k:
                     trade(k - 1).wait()
@@ -1288,9 +1296,9 @@
 
         run(stage0, 0)
 
-        @pl.when(i < 17)
-        def _():
-            segment(i + 1)
+        @pl.when(i < 18)
+        def _():
+            segment(i)
 
         return carry
 
@@ -1310,7 +1318,7 @@
     S = jax.ShapeDtypeStruct
     return pl.pallas_call(
         functools.partial(backward_reduce_kernel, dim),
-        out_shape=(S((12, 2, block, width), bf), S((2, seq, width), bf), S((2, 16, width), f32)),
+        out_shape=(S((12, 2, 2, half, width), bf), S((2, seq, width), bf), S((2, 16, width), f32)),
         in_specs=[hbm, hbm, hbm, vmem] + [hbm] * 5,
         out_specs=[hbm, hbm, vmem],
         scratch_shapes=[
@@ -1322,11 +1330,12 @@
             v((2, 2, half, width), bf), v((4, 2, half, width), bf), v((2, 2, half, width), bf), v((4, 2, half, width), bf),
             v((2, 2, half, width), f32), v((2, block, width), f32),
             v((2, half, width), bf), v((4, half, width), bf), v((2, half, width), bf), v((4, half, width), bf),
-            v((2, block, width), f32),
-            v((2, block, width), f32), v((2, block, width), bf), v((4, block, width), bf),
-            v((2, block, width), bf), v((4, block, width), bf), v((6, block, width), bf), v((6, block, width), bf),
+            v((2, 2, half, width), f32),
+            v((2, 2, half, width), f32), v((2, 2, half, width), bf), v((4, 2, half, width), bf),
+            v((2, 2, half, width), bf), v((4, 2, half, width), bf), v((6, 2, half, width), bf), v((6, 2, half, width), bf),
             dma((2, 4)), dma((2, 2)), dma((2,)), dma((2,)), dma((16,)), dma((4,)), dma((4,)), dma((1,)), dma((1,)), dma((5,)), dma((5,)),
-        ] + [dma((n,)) for n in (2, 4) * 7] + [dma((6,)), dma((6,))] + [dma((6,)), dma((12,))],
+        ] + [dma((n,)) for n in (2, 4)] + [dma((n, 2)) for n in (2, 4) * 2] + [dma((n,)) for n in (2, 4) * 2]
+        + [dma((n, 2)) for n in (2, 4, 2, 4, 6, 6)] + [dma((6,)), dma((12,))],
         compiler_params=pltpu.CompilerParams(collective_id=1, has_side_effects=True, vmem_limit_bytes=63 * 2**20),
     )(tokens, cots, full, norms, *saved)
 
@@ -1385,7 +1394,7 @@
         out_specs=[hbm] * 6,
         scratch_shapes=[v(parts.shape, bf), v(acts.shape, bf), v(grads.shape, bf)] + [v(shape, f32) for shape in shapes]
         + [dma((12,)), dma((2,)), dma((11,))],
-        compiler_params=pltpu.CompilerParams(vmem_limit_bytes=40 * 2**20),
+        compiler_params=pltpu.CompilerParams(vmem_limit_bytes=63 * 2**20),
     )(parts, acts, grads)
 
 

time: 472 us -> 454 us (0.962)
  Pallas kernels: 457 us -> 445 us
  local copies, waits for them, and re-layouts: 9.95 us -> 3.99 us
    pallas_call x1, Pallas kernels: 268 us -> 253 us  [backward_reduce(): pl.pallas_call(functools.partial(backward_reduce_kernel, dim), out_shape=...]
    unnamed x8 -> x2, local copies, waits for them, and re-layouts: 7.33 us -> 1.37 us
where the time goes in v5:
time: 454 us; the launch traced here: 453 us
  Pallas kernels  445 us (98%)
    pallas_call x1, Pallas kernels, backward_reduce(): pl.pallas_call(functools.partial(backward_reduce_kernel, dim), out_shape=...  253 us
    pallas_call x1, Pallas kernels, gather_forward(): pl.pallas_call(functools.partial(gather_forward_kernel, dim), out_shape=(...  181 us
    pallas_call x1, Pallas kernels, finish(): pl.pallas_call(finish_kernel, out_shape=[S(acts.shape, bf), S(grads.shape...  10.1 us

profile of v5, /device:TPU:0, one launch (start us, length us, event | category | flops | bytes accessed | tf_op | source)
XLA Modules:
  0.0 453.0 jit_solution(15593746254123882719)
XLA Ops:
  0.6 1.4 select_maximum_fusion.norm_in
  2.0 0.7 reduce
  2.7 1.3 fusion.3.vec
  4.0 181.5 %shard_map.194 = (bf16[2,12288,1024]{2,1,0:T(8,128)(2,1)}, f32[2,4,8,256]{3,2,1,0:T(8,128)}, f32[2,8,1024]{2,1,0:T(8,128)}, bf16[2,4,4,512,256]{4,3,2,1,0:T(8,12...) custom-call(bf16[2,512,1024]{2,1,0:T(8,128)(2,1)} %tokens.3, ...), custom_call_target="tpu_custom_call" | custom-call | tf_op jit(solution)/shard_map/pallas_call | solution.py:918
  185.5 253.4 %shard_map.195 = (bf16[12,2,2,64,1024]{4,3,2,1,0:T(8,128)(2,1)}, bf16[2,512,1024]{2,1,0:T(8,128)(2,1)}, f32[2,16,1024]{2,1,0:T(8,128)}) custom-call(bf16[2,512,1024]{2,1,0:T(8,128)(2,1)} %tokens.3, bf16[2,512,1024]{2,1,0:T(8,128)(2,1)} %cots.1, bf16[2,12288,1024]{2,1,0:T(8,128)(2,1)} %get-tuple-element.28.full, f32[2,8,1024]{2,1,0:T(8,128)} %get-tuple-element.29.norms, ...), custom_call_target="tpu_custom_call" | custom-call | tf_op jit(solution)/shard_map/pallas_call | solution.py:1319
  438.9 10.1 %shard_map.196 = (bf16[2,512,1024]{2,1,0:T(8,128)(2,1)}, bf16[2,512,1024]{2,1,0:T(8,128)(2,1)}, f32[3,1024,256]{2,1,0:T(8,128)}, f32[256,1024]{1,0:T(8,128)}, f3...) custom-call(bf16[12,256,1024]{2,1,0:T(8,128)(2,1)} %bitcast.18, bf16[2,512,1024]{2,1,0:T(8,128)(2,1)} %get-tuple-element.36.acts_in, ...), custom_call_target="tpu_custom_call" | custom-call | tf_op jit(solution)/shard_map/pallas_call | solution.py:1390
  449.0 0.8 constant_dynamic-slice_fusion
  449.7 0.6 fusion.4
  450.3 0.8 dynamic-slice_bitcast_fusion
  451.1 0.6 copy.22
  451.7 1.3 dynamic-slice.4
  (1 shorter events, 0.0 us)

commit v6 on v5

--- a/solution.py
+++ b/solution.py
@@ -384,8 +384,10 @@
 
 def softmax(q, k):
     scores = dot_nt(q * jnp.asarray(SCALE, q.dtype), k)
-    exponent = jnp.exp(scores - jnp.max(scores, axis=-1, keepdims=True))
-    return exponent * (1.0 / jnp.sum(exponent, axis=-1, keepdims=True))
+    top = jnp.max(scores, axis=-1, keepdims=True)
+    exponent = jnp.exp(scores - top)
+    total = jnp.sum(exponent, axis=-1, keepdims=True)
+    return exponent * (1.0 / total), top + jnp.log(total)
 
 
 def by_rows(rows, step, body):
@@ -441,12 +443,12 @@
     return jnp.sum(high(dz), axis=0, keepdims=True)
 
 
-def attention_back_block(dab, w, qkv, dq_out, dk_out, dv_out, acc, dim):
+def attention_back_block(dab, w, qkv, logs, dq_out, dk_out, dv_out, acc, dim):
     dob = low(dot_nt(dab[...], w[3]))
     for j in range(dob.shape[1] // dim):
         cols = slice(j * dim, (j + 1) * dim)
         q, k, v, do = qkv[0, :, cols], qkv[1, :, cols], qkv[2, :, cols], dob[:, cols]
-        a = softmax(q, k)
+        a = jnp.exp(dot_nt(q * jnp.asarray(SCALE, q.dtype), k) - logs[:, j : j + 1])
         da = dot_nt(do, v)
         ds = low(a * (da - jnp.sum(a * da, axis=-1, keepdims=True)))
         dv_out[:, cols] = low(dot_tn(low(a), do))
@@ -467,7 +469,7 @@
     ]
 
 
-def project_block(x, w, vec, save, dim):
+def project_block(x, w, vec, save, logs, dim):
     rows = x[...]
     q = low(dot_nt(rows, w[0]) + vec[0:1])
     k = low(dot_nt(rows, w[1]))
@@ -475,7 +477,8 @@
     save[0], save[1], save[2] = q, k, v
     for j in range(q.shape[1] // dim):
         cols = slice(j * dim, (j + 1) * dim)
-        save[3, :, cols] = low(dot(low(softmax(q[:, cols], k[:, cols])), v[:, cols]))
+        soft, logs[:, j : j + 1] = softmax(q[:, cols], k[:, cols])
+        save[3, :, cols] = low(dot(low(soft), v[:, cols]))
 
 
 def unit_values(hb, w, bias):
@@ -486,8 +489,8 @@
 
 
 def gather_forward_kernel(
-    dim, tokens, w_qkv, w_out, w_up, w_down, vec, norm_in, full, vecs, norms, qkvo, gd, us, hbs, between, acts,
-    turned, x, acc, u, hb, wa, wf, sa, gb, sd, wasem, wfsem, sasem, gbsem, sdsem, usem,
+    dim, tokens, w_qkv, w_out, w_up, w_down, qv, up_bias, biases, gains, shifts, full, vecs, norms, qkvo, logs, gd, us, hbs, between, acts,
+    turned, x, acc, u, hb, wa, wf, sa, gb, sd, wasem, wfsem, sasem, gbsem, sdsem, usem, vec, norm_in, lb, lbsem,
     ini_s, ini_r, loc, x1ss, x1rs, y1ss, y1rs, x2ss, x2rs, y2ss, y2rs, zs, zr, cs, cr, vs, vr, vloc, as_, ar,
 ):
     c, p, d = lax.axis_index("section"), lax.axis_index("mp"), lax.axis_index("dp")
@@ -499,11 +502,6 @@
     odd = lax.rem(d, 2)
     others = [(cc, spots[r], d) for r in range(4) for cc in (c, 1 - c)][1:]
 
-    barrier = pltpu.get_barrier_semaphore()
-    for device in others + [near["pair"]]:
-        pl.semaphore_signal(barrier, inc=1, device_id=device, device_id_type=MESH)
-    pl.semaphore_wait(barrier, 8)
-
     def place_of(s, spot, h):
         k = lax.rem(s, 12)
         row = jnp.where(k < 4, k * 8 + spot * 2, 32 + (k // 4 - 1) * 32 + spot * 8 + lax.rem(k, 4) * 2)
@@ -531,7 +529,8 @@
         return w_down.at[pl.ds(2 * rows * (k - 8), 2 * rows)]
 
     def init_start(k):
-        turn(k)
+        if k > 2:
+            turn(k)
         pltpu.make_async_copy(chunk(k), init_place(k, c), loc.at[k]).start()
         remote(chunk(k), init_place(k, c), ini_s.at[k], ini_r.at[k], near["core"]).start()
 
@@ -675,8 +674,14 @@
     def load_down(l, b, q, slot):
         return load(l, 32 + 4 * q + b, slot)
 
+    def load_last(l, q):
+        return weights(l, 32 + 4 * q + 3, wa.at[q, 0], wasem.at[q, 0])
+
     def save_attn(l, q):
         return pltpu.make_async_copy(sa.at[q], qkvo.at[l, q], sasem.at[q])
+
+    def save_logs(l, q):
+        return pltpu.make_async_copy(lb.at[q], logs.at[l, q], lbsem.at[q])
 
     def save_g(l, n):
         return pltpu.make_async_copy(gb.at[n], gd.at[l, n, 0], gbsem.at[n])
@@ -719,8 +724,9 @@
     def attention_segment(l, q):
         for copy in load_qkv(l, q):
             copy.wait()
-        project_block(x, wa.at[q], vecs[l, q], sa.at[q], dim)
+        project_block(x, wa.at[q], vecs[l, q], sa.at[q], lb.at[q], dim)
         save_attn(l, q).start()
+        save_logs(l, q).start()
 
     def out_segment(l):
         @pl.when(l == 1)
@@ -740,35 +746,31 @@
         keep(l, 2).start()
 
     def up_segment(l, b, slot):
-        def run(q):
+        for q in range(4):
             load_in(l, b, q, slot + q).wait()
-            n, two = 4 * q + b, lax.rem(q, 2)
-
-            @pl.when(q >= 2)
-            def _():
-                save_d(l, n - 8, two).wait()
-
+        for q in range(4):
             g, slope = unit_values(hb, wf[slot + q], vecs[l, q, pl.ds(2 + b, 1)])
-            gb[n] = g
-            sd[two] = slope
-            save_g(l, n).start()
-            save_d(l, n, two).start()
-
-        each(4, run)
-        for q in (2, 3):
-            save_d(l, 4 * q + b, q % 2).wait()
+            gb[4 * q + b] = g
+            sd[q] = slope
+        for q in range(4):
+            save_g(l, 4 * q + b).start()
+            save_d(l, 4 * q + b, q).start()
+
+    def up_saved(l, b):
+        for q in range(4):
+            save_d(l, 4 * q + b, q).wait()
 
     def down_segment(l, b, slot):
-        def run(q):
+        for q in range(4):
             load_down(l, b, q, slot + q).wait()
-            acc[...] += dot(gb[4 * q + b], wf[slot + q])
-
-        each(4, run)
+        first_two = dot(gb[b], wf[slot]) + dot(gb[4 + b], wf[slot + 1])
+        acc[...] += first_two + dot(gb[8 + b], wf[slot + 2]) + dot(gb[12 + b], wf[slot + 3])
 
     def end_segment(l):
         keep(l, 0).wait()
         keep(l, 2).wait()
         each(4, lambda q: save_attn(l, q).wait())
+        each(4, lambda q: save_logs(l, q).wait())
         each(16, lambda n: save_g(l, n).wait())
 
         @pl.when(l == 1)
@@ -825,11 +827,13 @@
                 load_in(l, 2, q, q).start()
             for q in range(4):
                 load_in(l, 3, q, 4 + q).start()
+            up_saved(l, 1)
             up_segment(l, 2, 0)
             for q in range(4):
                 load_down(l, 0, q, q).start()
 
         def turn_part():
+            up_saved(l, 2)
             up_segment(l, 3, 4)
             down_segment(l, 0, 0)
 
@@ -837,13 +841,17 @@
             for b in (1, 2):
                 for q in range(4):
                     load_down(l, b, q, 4 * (b - 1) + q).start()
+            for q in range(4):
+                load_last(l, q).start()
+            up_saved(l, 3)
             down_segment(l, 1, 0)
+            down_segment(l, 2, 4)
+
+        def end_part():
             for q in range(4):
-                load_down(l, 3, q, q).start()
-            down_segment(l, 2, 4)
-
-        def end_part():
-            down_segment(l, 3, 0)
+                load_last(l, q).wait()
+            first_two = dot(gb[3], wa[0, 0]) + dot(gb[7], wa[1, 0])
+            acc[...] += first_two + dot(gb[11], wa[2, 0]) + dot(gb[15], wa[3, 0])
             end_segment(l)
 
         at(0, attention_first)
@@ -857,6 +865,11 @@
         @pl.when((part == 2) | (part == 3))
         def _():
             b = part - 2
+
+            @pl.when(b == 1)
+            def _():
+                up_saved(l, 0)
+
             up_segment(l, b, 4 - 4 * b)
 
         at(4, up_part)
@@ -866,6 +879,18 @@
 
     first_rows = pltpu.make_async_copy(tokens.at[c], x, usem.at[4])
     first_rows.start()
+    vec[...] = jnp.zeros_like(vec)
+    vec[0:2] = high(qv[...])
+    for b in range(4):
+        vec[2 + b : 3 + b] = high(up_bias[:, 2 * rows * b : 2 * rows * (b + 1)])
+    norm_in[...] = jnp.zeros_like(norm_in)
+    norm_in[0:2], norm_in[2:4], norm_in[4:6] = biases[...], gains[...], shifts[...]
+    barrier = pltpu.get_barrier_semaphore()
+    for device in others + [near["pair"]]:
+        pl.semaphore_signal(barrier, inc=1, device_id=device, device_id_type=MESH)
+    for k in range(3):
+        turn(k)
+    pl.semaphore_wait(barrier, 8)
     for k in range(3):
         init_start(k)
     for copy in small_local() + small():
@@ -887,8 +912,7 @@
         run(stage_a, -1)
         run(stage_b, 1)
         run(stage_c, 2)
-        run_late(stage_d, 4)
-        run_late(stage_e, 5)
+        run_late(stage_e, 4)
         run_late(stage_f, 6)
         for t in range(3):
 
@@ -897,7 +921,8 @@
                 for k in range(3 * t + 3, 3 * t + 6):
                     init_start(k)
 
-        run(compute, 5)
+        run(compute, 4)
+        run_late(stage_d, 3)
         return carry
 
     lax.fori_loop(0, 2 * TRIPLES + 6, step, 0)
@@ -909,7 +934,7 @@
     remote(x, acts.at[1 - c], as_.at[0], ar.at[0], near["core"]).wait_recv()
 
 
-def gather_forward(dim, tokens, w_qkv, w_out, w_up, w_down, vec, norms):
+def gather_forward(dim, tokens, w_qkv, w_out, w_up, w_down, qv, up_bias, biases, gains, shifts):
     rows, width = w_out.shape
     seq = tokens.shape[1]
     bf, f32, dma, v = jnp.bfloat16, jnp.float32, pltpu.SemaphoreType.DMA, pltpu.VMEM
@@ -918,26 +943,27 @@
     return pl.pallas_call(
         functools.partial(gather_forward_kernel, dim),
         out_shape=(
-            S((2, 48 * rows, width), bf), S((2, 4) + vec.shape, f32), S((2,) + norms.shape, f32),
-            S((2, 4, 4, seq, rows), bf), S((2, 16, 2, seq, rows), bf), S((2, 2, seq, width), f32),
+            S((2, 48 * rows, width), bf), S((2, 4, 8, rows), f32), S((2, 8, width), f32),
+            S((2, 4, 4, seq, rows), bf), S((2, 4, seq, 128), f32), S((2, 16, 2, seq, rows), bf), S((2, 2, seq, width), f32),
             S((2, seq, width), bf), S((seq, width), bf), S((2, seq, width), bf),
         ),
-        in_specs=[hbm] + [vmem] * 6,
-        out_specs=[hbm, vmem, vmem] + [hbm] * 6,
+        in_specs=[hbm] + [vmem] * 9,
+        out_specs=[hbm, vmem, vmem] + [hbm] * 7,
         scratch_shapes=[
             v((7, rows, width), bf),
             v((seq, width), bf), v((seq, width), f32), v((seq, width), f32), v((seq, width), bf),
             v((4, 3, rows, width), bf), v((8, rows, width), bf), v((4, 4, seq, rows), bf), v((16, seq, rows), bf),
-            v((2, seq, rows), bf), dma((4, 3)), dma((8,)), dma((4,)), dma((16,)), dma((2,)), dma((5,)),
+            v((4, seq, rows), bf), dma((4, 3)), dma((8,)), dma((4,)), dma((16,)), dma((4,)), dma((5,)),
+            v((8, rows), f32), v((8, width), f32), v((4, seq, 128), f32), dma((4,)),
         ] + [dma((12,))] * 3 + [dma((24,))] * 8 + [dma((24, 3))] * 4
         + [dma((8,)), dma((2, 5)), dma((2,)), dma((1,)), dma((1,))],
         compiler_params=pltpu.CompilerParams(collective_id=0, has_side_effects=True, vmem_limit_bytes=60 * 2**20),
-    )(tokens, w_qkv, w_out, w_up, w_down, vec, norms)
+    )(tokens, w_qkv, w_out, w_up, w_down, qv, up_bias, biases, gains, shifts)
 
 
 def backward_reduce_kernel(
-    dim, tokens, cots, full, norms, qkvo, gd, us, hbs, between, out, grads, totals,
-    left, right, acc, g, u, wa, wf, da, df, trades,
+    dim, tokens, cots, full, norms, qkvo, logs, gd, us, hbs, between, out, grads, totals,
+    left, right, acc, g, u, wa, wf, da, df, dl, dlsem, trades,
     sendc, recvc, keep, x1s, x1r, y1s, y1r, part, base, x2s, x2r, y2s, y2r, mid,
     zk, zs1, zr1, zs2, zr2, zs3, zr3,
     wasem, wfsem, dasem, dfsem, gsem, osem4, bsem, gds, gdr, tss, trs,
@@ -953,23 +979,6 @@
     rows = sendc.shape[2]
     half = rows // 2
     wide = 2 * rows
-
-    barrier = pltpu.get_barrier_semaphore()
-
-    def signal(device):
-        pl.semaphore_signal(barrier, inc=1, device_id=device, device_id_type=MESH)
-
-    for name in ("core", "x", "y", "pair", "far"):
-        signal(near[name])
-
-    @pl.when(is_end)
-    def _():
-        pl.semaphore_wait(barrier, 5)
-
-    @pl.when(is_mid)
-    def _():
-        signal(near["across"])
-        pl.semaphore_wait(barrier, 6)
 
     def core_copy(s):
         a, b = lax.rem(s, 2), lax.rem(s, 4)
@@ -1126,7 +1135,8 @@
 
     def attn(l, q, slot):
         return weight_copies(full, l, 0, q, 0, wa.at[slot], wasem.at[slot], wide) + [
-            pltpu.make_async_copy(qkvo.at[l, q], da.at[slot], dasem.at[slot])
+            pltpu.make_async_copy(qkvo.at[l, q], da.at[slot], dasem.at[slot]),
+            pltpu.make_async_copy(logs.at[l, q], dl.at[slot], dlsem.at[slot]),
         ]
 
     def store_dx(l, begin):
@@ -1207,7 +1217,7 @@
                 copy.start()
 
         dq, dk, dv = left.at[36 + q], left.at[40 + q], left.at[44 + q]
-        attention_back_block(right.at[2], wa.at[slot], da.at[slot], dq, dk, dv, acc, dim)
+        attention_back_block(right.at[2], wa.at[slot], da.at[slot], dl[slot], dq, dk, dv, acc, dim)
         cols = pl.ds(pl.multiple_of(q * wide, wide), wide)
         totals[l, 8:9, cols] = jnp.sum(high(dq[...]), axis=0, keepdims=True)
         totals[l, 9:10, cols] = jnp.sum(high(dv[...]), axis=0, keepdims=True)
@@ -1226,8 +1236,11 @@
         def _():
             end_segment(1)
             operands(0)
+            store_dx(1, False)
+
+        @pl.when(i == 7)
+        def _():
             load_x(between).wait()
-            store_dx(1, False)
 
         @pl.when(j == -1)
         def _():
@@ -1249,7 +1262,7 @@
         def _():
             end_segment(0)
 
-        @pl.when(i == 11)
+        @pl.when(i == 10)
         def _():
             operands_there(0)
 
@@ -1270,6 +1283,23 @@
     operands(1)
     load_x(between).start()
     totals[...] = jnp.zeros_like(totals)
+    barrier = pltpu.get_barrier_semaphore()
+
+    def signal(device):
+        pl.semaphore_signal(barrier, inc=1, device_id=device, device_id_type=MESH)
+
+    for name in ("core", "x", "y", "pair", "far"):
+        signal(near[name])
+
+    @pl.when(is_end)
+    def _():
+        pl.semaphore_wait(barrier, 5)
+
+    @pl.when(is_mid)
+    def _():
+        signal(near["across"])
+        pl.semaphore_wait(barrier, 6)
+
     first_rows.wait()
 
     def step(count, carry):
@@ -1296,9 +1326,9 @@
 
         run(stage0, 0)
 
-        @pl.when(i < 18)
-        def _():
-            segment(i)
+        @pl.when((i < 19) & (i != 0))
+        def _():
+            segment(jnp.where(i < 0, i, i - 1))
 
         return carry
 
@@ -1319,13 +1349,13 @@
     return pl.pallas_call(
         functools.partial(backward_reduce_kernel, dim),
         out_shape=(S((12, 2, 2, half, width), bf), S((2, seq, width), bf), S((2, 16, width), f32)),
-        in_specs=[hbm, hbm, hbm, vmem] + [hbm] * 5,
+        in_specs=[hbm, hbm, hbm, vmem] + [hbm] * 6,
         out_specs=[hbm, hbm, vmem],
         scratch_shapes=[
             v((48, seq, wide), bf), v((4, seq, width), bf), v((seq, width), f32), v((seq, width), bf),
             v((seq, width), f32),
             v((2, 4, wide, width), bf), v((2, 2, wide, width), bf), v((2, 4, seq, wide), bf), v((2, seq, wide), bf),
-            v((5, 2, 16, width), f32),
+            v((2, seq, 128), f32), dma((2,)), v((5, 2, 16, width), f32),
             v((2, 4, block, width), bf), v((4, 4, block, width), bf), v((2, 4, block, width), f32),
             v((2, 2, half, width), bf), v((4, 2, half, width), bf), v((2, 2, half, width), bf), v((4, 2, half, width), bf),
             v((2, 2, half, width), f32), v((2, block, width), f32),
@@ -1340,8 +1370,8 @@
     )(tokens, cots, full, norms, *saved)
 
 
-def finish_kernel(parts, acts_in, grads_in, acts, grads, g_qkv, g_out, g_up, g_down,
-                  pb, ab, gb, qb, ob, ub, db, psem, asem, osem):
+def finish_kernel(parts, acts_in, grads_in, totals, acts, grads, g_qkv, g_out, g_up, g_down, g_qv, g_bias,
+                  g_biases, g_gains, g_shifts, pb, ab, gb, qb, ob, ub, db, psem, asem, osem):
     def load(k):
         return pltpu.make_async_copy(parts.at[k], pb.at[k], psem.at[k])
 
@@ -1352,6 +1382,16 @@
         pltpu.make_async_copy(source, buffer, asem.at[n]).start()
     stores = []
     rows = pb.shape[1]
+    c, p, d = lax.axis_index("section"), lax.axis_index("mp"), lax.axis_index("dp")
+    mine = totals.at[c]
+    own = mine[8:16, pl.ds(pl.multiple_of(p * rows, rows), rows)]
+    g_qv[...] = own[0:2]
+    for b in range(4):
+        g_bias[:, b * rows : (b + 1) * rows] = own[2 + b : 3 + b]
+    piece = g_gains.shape[1]
+    both = mine[0:8, pl.ds(pl.multiple_of(p * rows + d // 2 * 2 * piece, 2 * piece), 2 * piece)]
+    both = jnp.where(lax.rem(d, 2) == 0, both[:, :piece], both[:, piece:])
+    g_biases[...], g_gains[...], g_shifts[...] = both[0:2], both[2:4], both[4:6]
 
     def store(source, place):
         copy = pltpu.make_async_copy(source, place, osem.at[len(stores)])
@@ -1381,21 +1421,23 @@
         copy.wait()
 
 
-def finish(parts, acts, grads):
+def finish(parts, acts, grads, totals):
     count, rows, width = parts.shape
     bf, f32, dma, v = jnp.bfloat16, jnp.float32, pltpu.SemaphoreType.DMA, pltpu.VMEM
     S = jax.ShapeDtypeStruct
     shapes = [(3, width, rows), (rows, width), (width, width), (width, width)]
-    hbm = pl.BlockSpec(memory_space=pl.ANY)
+    piece = width // (lax.axis_size("mp") * lax.axis_size("dp"))
+    hbm, vmem = pl.BlockSpec(memory_space=pl.ANY), pl.BlockSpec(memory_space=pltpu.VMEM)
+    vectors = [(2, rows), (1, 4 * rows)] + [(2, piece)] * 3
     return pl.pallas_call(
         finish_kernel,
-        out_shape=[S(acts.shape, bf), S(grads.shape, bf)] + [S(shape, f32) for shape in shapes],
-        in_specs=[hbm] * 3,
-        out_specs=[hbm] * 6,
+        out_shape=[S(acts.shape, bf), S(grads.shape, bf)] + [S(shape, f32) for shape in shapes + vectors],
+        in_specs=[hbm] * 3 + [vmem],
+        out_specs=[hbm] * 6 + [vmem] * 5,
         scratch_shapes=[v(parts.shape, bf), v(acts.shape, bf), v(grads.shape, bf)] + [v(shape, f32) for shape in shapes]
         + [dma((12,)), dma((2,)), dma((11,))],
         compiler_params=pltpu.CompilerParams(vmem_limit_bytes=63 * 2**20),
-    )(parts, acts, grads)
+    )(parts, acts, grads, totals)
 
 
 def by_page(
@@ -1411,37 +1453,33 @@
     norm_gains,
     norm_shifts,
 ):
-    core, place = lax.axis_index("section"), lax.axis_index("mp")
     width = token_in.shape[2]
-    quarter = width // 4
-    vec = high(jnp.concatenate([qv_bias[0], ffn_in_bias[0].reshape(4, quarter)], axis=0))
-    vec = jnp.pad(vec, ((0, 2), (0, 0)))
-    norms = jnp.concatenate([out_biases[0], norm_gains[0], norm_shifts[0]], axis=0)
-    norms = jnp.pad(norms, ((0, 2), (0, 0)))
     full, vecs, norms, *saved, acts = gather_forward(
-        HEAD_DIM, token_in, w_qkv[0], w_attn_out[0], w_ffn_in[0], w_ffn_out[0], vec, norms
+        HEAD_DIM,
+        token_in,
+        w_qkv[0],
+        w_attn_out[0],
+        w_ffn_in[0],
+        w_ffn_out[0],
+        qv_bias[0],
+        ffn_in_bias,
+        out_biases[0],
+        norm_gains[0],
+        norm_shifts[0],
     )
     parts, grads, totals = backward_reduce(HEAD_DIM, token_in, cotangent, full, norms, saved)
-    parts = parts.reshape(12, quarter, width)
-    acts, grads, grad_qkv, grad_out, grad_up, grad_down = finish(parts, acts, grads)
-    totals = lax.dynamic_index_in_dim(totals, core, 0, keepdims=False)
-    own = lax.dynamic_slice_in_dim(totals[8:], place * quarter, quarter, 1)
-    piece = width // (lax.axis_size("mp") * lax.axis_size("dp"))
-    begin = (place * lax.axis_size("dp") + lax.axis_index("dp")) * piece
-    rows = lax.dynamic_slice_in_dim(totals[:8], begin, piece, 1)
+    results = finish(parts.reshape(12, width // 4, width), acts, grads, totals)
+    acts, grads, grad_qkv, grad_out, grad_up, grad_down, grad_qv, grad_bias, *rows = results
     return (
         acts[None],
         grads[None],
         grad_qkv[None],
-        own[0:2][None],
+        grad_qv[None],
         grad_out[None],
         grad_up[None],
-        own[2:6].reshape(1, width),
+        grad_bias,
         grad_down[None],
-        rows[0:2][None],
-        rows[2:4][None],
-        rows[4:6][None],
-    )
+    ) + tuple(row[None] for row in rows)
 
 
 def on_device(*args):

time: 454 us -> 441 us (0.971)
  Pallas kernels: 445 us -> 439 us
    pallas_call x1, Pallas kernels: 253 us -> 249 us  [backward_reduce(): pl.pallas_call(functools.partial(backward_reduce_kernel, dim), out_shape=...]
where the time goes in v6:
time: 441 us; the launch traced here: 440 us
  Pallas kernels  439 us (100%)
    pallas_call x1, Pallas kernels, backward_reduce(): pl.pallas_call(functools.partial(backward_reduce_kernel, dim), out_shape=...  249 us
    pallas_call x1, Pallas kernels, gather_forward(): pl.pallas_call(functools.partial(gather_forward_kernel, dim), out_shape=(...  179 us
    pallas_call x1, Pallas kernels, finish(): pl.pallas_call(finish_kernel, out_shape=[S(acts.shape, bf), S(grads.shape...  11.6 us

profile of v6, /device:TPU:0, one launch (start us, length us, event | category | flops | bytes accessed | tf_op | source)
XLA Modules:
  0.0 439.9 jit_solution(10625417359077378464)
XLA Ops:
  0.6 179.0 %shard_map.194 = (bf16[2,12288,1024]{2,1,0:T(8,128)(2,1)}, f32[2,4,8,256]{3,2,1,0:T(8,128)}, f32[2,8,1024]{2,1,0:T(8,128)}, bf16[2,4,4,512,256]{4,3,2,1,0:T(8,12...) custom-call(bf16[2,512,1024]{2,1,0:T(8,128)(2,1)} %tokens.3, ...), custom_call_target="tpu_custom_call" | custom-call | tf_op jit(solution)/shard_map/pallas_call | solution.py:943
  179.6 248.6 %shard_map.195 = (bf16[12,2,2,64,1024]{4,3,2,1,0:T(8,128)(2,1)}, bf16[2,512,1024]{2,1,0:T(8,128)(2,1)}, f32[2,16,1024]{2,1,0:T(8,128)}) custom-call(bf16[2,512,1024]{2,1,0:T(8,128)(2,1)} %tokens.3, bf16[2,512,1024]{2,1,0:T(8,128)(2,1)} %cots.1, bf16[2,12288,1024]{2,1,0:T(8,128)(2,1)} %get-tuple-element.34.full, f32[2,8,1024]{2,1,0:T(8,128)} %get-tuple-element.35.norms, ...), custom_call_target="tpu_custom_call" | custom-call | tf_op jit(solution)/shard_map/pallas_call | solution.py:1349
  428.2 11.6 %shard_map.196 = (bf16[2,512,1024]{2,1,0:T(8,128)(2,1)}, bf16[2,512,1024]{2,1,0:T(8,128)(2,1)}, f32[3,1024,256]{2,1,0:T(8,128)}, f32[256,1024]{1,0:T(8,128)}, f3...) custom-call(bf16[12,256,1024]{2,1,0:T(8,128)(2,1)} %bitcast.19, ...), custom_call_target="tpu_custom_call" | custom-call | tf_op jit(solution)/shard_map/pallas_call | solution.py:1432

commit v7 on v6

--- a/solution.py
+++ b/solution.py
@@ -489,8 +489,9 @@
 
 
 def gather_forward_kernel(
-    dim, tokens, w_qkv, w_out, w_up, w_down, qv, up_bias, biases, gains, shifts, full, vecs, norms, qkvo, logs, gd, us, hbs, between, acts,
+    dim, tokens, qkv_in, out_in, up_in, down_in, qv, up_bias, biases, gains, shifts, full, vecs, norms, qkvo, logs, gd, us, hbs, between, acts,
     turned, x, acc, u, hb, wa, wf, sa, gb, sd, wasem, wfsem, sasem, gbsem, sdsem, usem, vec, norm_in, lb, lbsem,
+    w_qkv, w_out, w_up, w_down, rawsem,
     ini_s, ini_r, loc, x1ss, x1rs, y1ss, y1rs, x2ss, x2rs, y2ss, y2rs, zs, zr, cs, cr, vs, vr, vloc, as_, ar,
 ):
     c, p, d = lax.axis_index("section"), lax.axis_index("mp"), lax.axis_index("dp")
@@ -696,23 +697,19 @@
             return pltpu.make_async_copy(x, between, usem.at[3])
         return pltpu.make_async_copy(u, us.at[l, which], usem.at[which])
 
-    def give(l, begin):
-        @pl.when(l == c)
-        def _():
-            copy = pltpu.make_async_copy(x, acts.at[c], as_.at[0])
+    def give(begin):
+        @pl.when(c == 0)
+        def _():
+            copy = pltpu.make_async_copy(x, acts.at[0], as_.at[0])
             copy.start() if begin else copy.wait()
 
-        @pl.when(l != c)
-        def _():
-            copy = remote(x, acts.at[c], as_.at[0], ar.at[0], near["core"])
+        @pl.when(c == 1)
+        def _():
+            copy = remote(x, acts.at[1], as_.at[0], ar.at[0], near["core"])
             copy.start() if begin else copy.wait_send()
 
-    def kept(l):
-        @pl.when(l == 0)
-        def _():
-            keep(0, 3).wait()
-
-        give(l, False)
+    def last_sum():
+        return pltpu.make_async_copy(acc, us.at[1, 1], usem.at[1])
 
     def each(count, body):
         def run(q, carry):
@@ -773,17 +770,16 @@
         each(4, lambda q: save_logs(l, q).wait())
         each(16, lambda n: save_g(l, n).wait())
 
+        @pl.when(l == 0)
+        def _():
+            second_norm(norms.at[0], acc, u, x)
+            keep(0, 1).start()
+            give(True)
+            keep(0, 3).start()
+
         @pl.when(l == 1)
         def _():
-            kept(0)
-
-        second_norm(norms.at[l], acc, u, x)
-        keep(l, 1).start()
-        give(l, True)
-
-        @pl.when(l == 0)
-        def _():
-            keep(0, 3).start()
+            last_sum().start()
 
     def small_there():
         for copy in small_local():
@@ -878,6 +874,14 @@
         at(7, end_part)
 
     first_rows = pltpu.make_async_copy(tokens.at[c], x, usem.at[4])
+    raw = [
+        pltpu.make_async_copy(source, place, rawsem.at[n])
+        for n, (source, place) in enumerate(
+            ((qkv_in, w_qkv), (out_in, w_out), (up_in, w_up), (down_in, w_down))
+        )
+    ]
+    for copy in raw:
+        copy.start()
     first_rows.start()
     vec[...] = jnp.zeros_like(vec)
     vec[0:2] = high(qv[...])
@@ -888,6 +892,7 @@
     barrier = pltpu.get_barrier_semaphore()
     for device in others + [near["pair"]]:
         pl.semaphore_signal(barrier, inc=1, device_id=device, device_id_type=MESH)
+    raw[0].wait()
     for k in range(3):
         turn(k)
     pl.semaphore_wait(barrier, 8)
@@ -918,6 +923,9 @@
 
             @pl.when(i == 2 * t)
             def _():
+                if t == 0:
+                    for copy in raw[1:]:
+                        copy.wait()
                 for k in range(3 * t + 3, 3 * t + 6):
                     init_start(k)
 
@@ -929,9 +937,13 @@
 
     for k in range(12):
         remote(chunk(k), init_place(k, c), ini_s.at[k], ini_r.at[k], near["core"]).wait_send()
-    keep(1, 1).wait()
-    kept(1)
-    remote(x, acts.at[1 - c], as_.at[0], ar.at[0], near["core"]).wait_recv()
+    keep(0, 3).wait()
+    give(False)
+    last_sum().wait()
+
+    @pl.when(c == 0)
+    def _():
+        remote(x, acts.at[1], as_.at[0], ar.at[0], near["core"]).wait_recv()
 
 
 def gather_forward(dim, tokens, w_qkv, w_out, w_up, w_down, qv, up_bias, biases, gains, shifts):
@@ -947,7 +959,7 @@
             S((2, 4, 4, seq, rows), bf), S((2, 4, seq, 128), f32), S((2, 16, 2, seq, rows), bf), S((2, 2, seq, width), f32),
             S((2, seq, width), bf), S((seq, width), bf), S((2, seq, width), bf),
         ),
-        in_specs=[hbm] + [vmem] * 9,
+        in_specs=[hbm] * 5 + [vmem] * 5,
         out_specs=[hbm, vmem, vmem] + [hbm] * 7,
         scratch_shapes=[
             v((7, rows, width), bf),
@@ -955,6 +967,7 @@
             v((4, 3, rows, width), bf), v((8, rows, width), bf), v((4, 4, seq, rows), bf), v((16, seq, rows), bf),
             v((4, seq, rows), bf), dma((4, 3)), dma((8,)), dma((4,)), dma((16,)), dma((4,)), dma((5,)),
             v((8, rows), f32), v((8, width), f32), v((4, seq, 128), f32), dma((4,)),
+            v(w_qkv.shape, bf), v(w_out.shape, bf), v(w_up.shape, bf), v(w_down.shape, bf), dma((4,)),
         ] + [dma((12,))] * 3 + [dma((24,))] * 8 + [dma((24, 3))] * 4
         + [dma((8,)), dma((2, 5)), dma((2,)), dma((1,)), dma((1,))],
         compiler_params=pltpu.CompilerParams(collective_id=0, has_side_effects=True, vmem_limit_bytes=60 * 2**20),
@@ -962,11 +975,11 @@
 
 
 def backward_reduce_kernel(
-    dim, tokens, cots, full, norms, qkvo, logs, gd, us, hbs, between, out, grads, totals,
+    dim, tokens, cots, full, norms, qkvo, logs, gd, us, hbs, between, out, grads, acts, totals,
     left, right, acc, g, u, wa, wf, da, df, dl, dlsem, trades,
     sendc, recvc, keep, x1s, x1r, y1s, y1r, part, base, x2s, x2r, y2s, y2r, mid,
     zk, zs1, zr1, zs2, zr2, zs3, zr3,
-    wasem, wfsem, dasem, dfsem, gsem, osem4, bsem, gds, gdr, tss, trs,
+    wasem, wfsem, dasem, dfsem, gsem, osem4, bsem, gds, gdr, as_, ar, tss, trs,
     cs, cr, x1ss, x1rs, y1ss, y1rs, x2ss, x2rs, y2ss, y2rs, z1ss, z1rs, z2ss, z2rs, z3ss, z3rs, os, orr,
 ):
     c, p, d = lax.axis_index("section"), lax.axis_index("mp"), lax.axis_index("dp")
@@ -1150,6 +1163,27 @@
             copy = remote(g, grads.at[c], gds.at[0], gdr.at[0], near["core"])
             copy.start() if begin else copy.wait_send()
 
+    def give(begin):
+        @pl.when(c == 1)
+        def _():
+            copy = pltpu.make_async_copy(g, acts.at[1], as_.at[0])
+            copy.start() if begin else copy.wait()
+
+        @pl.when(c == 0)
+        def _():
+            copy = remote(g, acts.at[0], as_.at[0], ar.at[0], near["core"])
+            copy.start() if begin else copy.wait_send()
+
+    def output():
+        load_u(1, 1).wait()
+        store_dx(0, False)
+
+        def run(r):
+            g[r] = low(standard(u[r])[0] * norms[1, 3:4] + norms[1, 5:6])
+
+        by_rows(u.shape[0], 64, run)
+        give(True)
+
     def ahead(l):
         load_u(l, 1).start()
         for copy in ffn(l, 0, 0) + attn(l, 0, 0):
@@ -1231,6 +1265,7 @@
     def segment(i):
         l = jnp.where(i < 8, 1, 0)
         j = jnp.where(i < 8, i, i - 9)
+        q = jnp.where(i < 8, i - 4, i - 14)
 
         @pl.when(i == 8)
         def _():
@@ -1250,15 +1285,15 @@
         def _():
             ffn_segment(l, j)
 
-        @pl.when(j == 3)
+        @pl.when((i == 3) | (i == 13))
         def _():
             middle_segment(l)
 
-        @pl.when((j >= 4) & (j < 8))
-        def _():
-            attention_segment(l, j - 4)
-
-        @pl.when(i == 17)
+        @pl.when((q >= 0) & (q < 4))
+        def _():
+            attention_segment(l, q)
+
+        @pl.when(i == 18)
         def _():
             end_segment(0)
 
@@ -1316,7 +1351,7 @@
         run(stage6, 7, False)
         for k in range(6):
 
-            @pl.when(i == 19 + k)
+            @pl.when(i == 20 + k)
             def _():
                 if k:
                     trade(k - 1).wait()
@@ -1326,14 +1361,28 @@
 
         run(stage0, 0)
 
-        @pl.when((i < 19) & (i != 0))
+        @pl.when((i < 20) & (i != 0))
         def _():
             segment(jnp.where(i < 0, i, i - 1))
 
+        @pl.when(i == 20)
+        def _():
+            load_u(1, 1).start()
+
+        @pl.when(i == 22)
+        def _():
+            output()
+
+
         return carry
 
     lax.fori_loop(0, CHUNKS + 9, step, 0)
-    store_dx(0, False)
+    give(False)
+
+    @pl.when(c == 1)
+    def _():
+        remote(g, acts.at[0], as_.at[0], ar.at[0], near["core"]).wait_recv()
+
     remote(g, grads.at[1 - c], gds.at[0], gdr.at[0], near["core"]).wait_recv()
     for k in range(12):
         remote(zs3.at[0], out.at[k, 1 - c], os.at[0], orr.at[k], near["core"]).wait_recv()
@@ -1348,9 +1397,10 @@
     S = jax.ShapeDtypeStruct
     return pl.pallas_call(
         functools.partial(backward_reduce_kernel, dim),
-        out_shape=(S((12, 2, 2, half, width), bf), S((2, seq, width), bf), S((2, 16, width), f32)),
+        out_shape=(S((12, 2, 2, half, width), bf), S((2, seq, width), bf), S((2, seq, width), bf),
+                   S((2, 16, width), f32)),
         in_specs=[hbm, hbm, hbm, vmem] + [hbm] * 6,
-        out_specs=[hbm, hbm, vmem],
+        out_specs=[hbm, hbm, hbm, vmem],
         scratch_shapes=[
             v((48, seq, wide), bf), v((4, seq, width), bf), v((seq, width), f32), v((seq, width), bf),
             v((seq, width), f32),
@@ -1363,26 +1413,36 @@
             v((2, 2, half, width), f32),
             v((2, 2, half, width), f32), v((2, 2, half, width), bf), v((4, 2, half, width), bf),
             v((2, 2, half, width), bf), v((4, 2, half, width), bf), v((6, 2, half, width), bf), v((6, 2, half, width), bf),
-            dma((2, 4)), dma((2, 2)), dma((2,)), dma((2,)), dma((16,)), dma((4,)), dma((4,)), dma((1,)), dma((1,)), dma((5,)), dma((5,)),
+            dma((2, 4)), dma((2, 2)), dma((2,)), dma((2,)), dma((16,)), dma((4,)), dma((4,)), dma((1,)), dma((1,)), dma((1,)), dma((1,)),
+            dma((5,)), dma((5,)),
         ] + [dma((n,)) for n in (2, 4)] + [dma((n, 2)) for n in (2, 4) * 2] + [dma((n,)) for n in (2, 4) * 2]
         + [dma((n, 2)) for n in (2, 4, 2, 4, 6, 6)] + [dma((6,)), dma((12,))],
         compiler_params=pltpu.CompilerParams(collective_id=1, has_side_effects=True, vmem_limit_bytes=63 * 2**20),
     )(tokens, cots, full, norms, *saved)
 
 
-def finish_kernel(parts, acts_in, grads_in, totals, acts, grads, g_qkv, g_out, g_up, g_down, g_qv, g_bias,
+def finish_kernel(parts, acts_zero, acts_one, grads_in, totals, acts, grads, g_qkv, g_out, g_up, g_down, g_qv, g_bias,
                   g_biases, g_gains, g_shifts, pb, ab, gb, qb, ob, ub, db, psem, asem, osem):
     def load(k):
         return pltpu.make_async_copy(parts.at[k], pb.at[k], psem.at[k])
 
-    others = [(acts_in, ab, acts, 0), (grads_in, gb, grads, 1)]
-    for k in range(12):
+    c, p, d = lax.axis_index("section"), lax.axis_index("mp"), lax.axis_index("dp")
+    order = (4, 5, 6, 7, 9, 10, 11, 0, 1, 2, 3, 8)
+    for k in order:
         load(k).start()
-    for source, buffer, place, n in others:
-        pltpu.make_async_copy(source, buffer, asem.at[n]).start()
+
+    @pl.when(c == 0)
+    def _():
+        pltpu.make_async_copy(acts_zero, ab, asem.at[0]).start()
+
+    @pl.when(c == 1)
+    def _():
+        pltpu.make_async_copy(acts_one, ab, asem.at[0]).start()
+
+    pltpu.make_async_copy(grads_in, gb, asem.at[1]).start()
+    others = [(acts_zero, ab, acts, 0), (grads_in, gb, grads, 1)]
     stores = []
     rows = pb.shape[1]
-    c, p, d = lax.axis_index("section"), lax.axis_index("mp"), lax.axis_index("dp")
     mine = totals.at[c]
     own = mine[8:16, pl.ds(pl.multiple_of(p * rows, rows), rows)]
     g_qv[...] = own[0:2]
@@ -1398,30 +1458,31 @@
         copy.start()
         stores.append(copy)
 
-    for k in range(12):
+    for k in order:
         load(k).wait()
         if k < 4:
             span = pl.ds(k * rows, rows)
             db[span] = high(pb[k])
             store(db.at[span], g_down.at[span])
         elif k < 8:
-            ub[:, pl.ds((k - 4) * rows, rows)] = high(pb[k]).T
+            ub[:, pl.ds((k - 4) * rows, rows)] = high(pb[k].T)
             if k == 7:
                 store(ub, g_up)
         elif k == 8:
             ob[...] = high(pb[k])
             store(ob, g_out)
         else:
-            qb[k - 9] = high(pb[k]).T
+            qb[k - 9] = high(pb[k].T)
             store(qb.at[k - 9], g_qkv.at[k - 9])
-    for source, buffer, place, n in others:
-        pltpu.make_async_copy(source, buffer, asem.at[n]).wait()
-        store(buffer, place)
+        if k == 7:
+            for source, buffer, place, n in others:
+                pltpu.make_async_copy(source, buffer, asem.at[n]).wait()
+                store(buffer, place)
     for copy in stores:
         copy.wait()
 
 
-def finish(parts, acts, grads, totals):
+def finish(parts, acts, acts_one, grads, totals):
     count, rows, width = parts.shape
     bf, f32, dma, v = jnp.bfloat16, jnp.float32, pltpu.SemaphoreType.DMA, pltpu.VMEM
     S = jax.ShapeDtypeStruct
@@ -1432,12 +1493,12 @@
     return pl.pallas_call(
         finish_kernel,
         out_shape=[S(acts.shape, bf), S(grads.shape, bf)] + [S(shape, f32) for shape in shapes + vectors],
-        in_specs=[hbm] * 3 + [vmem],
+        in_specs=[hbm] * 4 + [vmem],
         out_specs=[hbm] * 6 + [vmem] * 5,
         scratch_shapes=[v(parts.shape, bf), v(acts.shape, bf), v(grads.shape, bf)] + [v(shape, f32) for shape in shapes]
         + [dma((12,)), dma((2,)), dma((11,))],
         compiler_params=pltpu.CompilerParams(vmem_limit_bytes=63 * 2**20),
-    )(parts, acts, grads, totals)
+    )(parts, acts, acts_one, grads, totals)
 
 
 def by_page(
@@ -1467,8 +1528,8 @@
         norm_gains[0],
         norm_shifts[0],
     )
-    parts, grads, totals = backward_reduce(HEAD_DIM, token_in, cotangent, full, norms, saved)
-    results = finish(parts.reshape(12, width // 4, width), acts, grads, totals)
+    parts, grads, acts_one, totals = backward_reduce(HEAD_DIM, token_in, cotangent, full, norms, saved)
+    results = finish(parts.reshape(12, width // 4, width), acts, acts_one, grads, totals)
     acts, grads, grad_qkv, grad_out, grad_up, grad_down, grad_qv, grad_bias, *rows = results
     return (
         acts[None],

time: 441 us -> 438 us (level)
    pallas_call x1, Pallas kernels: 179 us -> 174 us  [gather_forward(): pl.pallas_call(functools.partial(gather_forward_kernel, dim), out_shape=(...]
where the time goes in v7:
time: 438 us; the launch traced here: 437 us
  Pallas kernels  436 us (100%)
    pallas_call x1, Pallas kernels, backward_reduce(): pl.pallas_call(functools.partial(backward_reduce_kernel, dim), out_shape=...  250 us
    pallas_call x1, Pallas kernels, gather_forward(): pl.pallas_call(functools.partial(gather_forward_kernel, dim), out_shape=(...  174 us
    pallas_call x1, Pallas kernels, finish(): pl.pallas_call(finish_kernel, out_shape=[S(acts.shape, bf), S(grads.shape...  12 us

profile of v7, /device:TPU:0, one launch (start us, length us, event | category | flops | bytes accessed | tf_op | source)
XLA Modules:
  0.0 437.0 jit_solution(15805282020481751194)
XLA Ops:
  0.6 174.5 %shard_map.194 = (bf16[2,12288,1024]{2,1,0:T(8,128)(2,1)}, f32[2,4,8,256]{3,2,1,0:T(8,128)}, f32[2,8,1024]{2,1,0:T(8,128)}, bf16[2,4,4,512,256]{4,3,2,1,0:T(8,12...) custom-call(bf16[2,512,1024]{2,1,0:T(8,128)(2,1)} %tokens.3, ...), custom_call_target="tpu_custom_call" | custom-call | tf_op jit(solution)/shard_map/pallas_call | solution.py:955
  175.1 249.7 %shard_map.195 = (bf16[12,2,2,64,1024]{4,3,2,1,0:T(8,128)(2,1)}, bf16[2,512,1024]{2,1,0:T(8,128)(2,1)}, bf16[2,512,1024]{2,1,0:T(8,128)(2,1)}, f32[2,16,1024]{2,1,0:T(8,128)}) custom-call(bf16[2,512,1024]{2,1,0:T(8,128)(2,1)} %tokens.3, bf16[2,512,1024]{2,1,0:T(8,128)(2,1)} %cots.1, bf16[2,12288,1024]{2,1,0:T(8,128)(2,1)} %get-tuple-element.35.full, ...), custom_call_target="tpu_custom_call" | custom-call | tf_op jit(solution)/shard_map/pallas_call | solution.py:1398
  424.9 12.0 %shard_map.196 = (bf16[2,512,1024]{2,1,0:T(8,128)(2,1)}, bf16[2,512,1024]{2,1,0:T(8,128)(2,1)}, f32[3,1024,256]{2,1,0:T(8,128)}, f32[256,1024]{1,0:T(8,128)}, f3...) custom-call(bf16[12,256,1024]{2,1,0:T(8,128)(2,1)} %bitcast.19, ...), custom_call_target="tpu_custom_call" | custom-call | tf_op jit(solution)/shard_map/pallas_call | solution.py:1493

commit v8 on v7

--- a/solution.py
+++ b/solution.py
@@ -914,8 +914,8 @@
             def _():
                 stage((i - lag) // 2)
 
+        run(stage_b, 1)
         run(stage_a, -1)
-        run(stage_b, 1)
         run(stage_c, 2)
         run_late(stage_e, 4)
         run_late(stage_f, 6)

time: 438 us -> 429 us (0.979)
  Pallas kernels: 436 us -> 427 us
    pallas_call x1, Pallas kernels: 174 us -> 167 us  [gather_forward(): pl.pallas_call(functools.partial(gather_forward_kernel, dim), out_shape=(...]
where the time goes in v8:
time: 429 us; the launch traced here: 428 us
  Pallas kernels  427 us (100%)
    pallas_call x1, Pallas kernels, backward_reduce(): pl.pallas_call(functools.partial(backward_reduce_kernel, dim), out_shape=...  248 us
    pallas_call x1, Pallas kernels, gather_forward(): pl.pallas_call(functools.partial(gather_forward_kernel, dim), out_shape=(...  167 us
    pallas_call x1, Pallas kernels, finish(): pl.pallas_call(finish_kernel, out_shape=[S(acts.shape, bf), S(grads.shape...  12 us

profile of v8, /device:TPU:0, one launch (start us, length us, event | category | flops | bytes accessed | tf_op | source)
XLA Modules:
  0.0 427.7 jit_solution(1525101782090581535)
XLA Ops:
  0.6 166.6 %shard_map.194 = (bf16[2,12288,1024]{2,1,0:T(8,128)(2,1)}, f32[2,4,8,256]{3,2,1,0:T(8,128)}, f32[2,8,1024]{2,1,0:T(8,128)}, bf16[2,4,4,512,256]{4,3,2,1,0:T(8,12...) custom-call(bf16[2,512,1024]{2,1,0:T(8,128)(2,1)} %tokens.3, ...), custom_call_target="tpu_custom_call" | custom-call | tf_op jit(solution)/shard_map/pallas_call | solution.py:955
  167.3 248.3 %shard_map.195 = (bf16[12,2,2,64,1024]{4,3,2,1,0:T(8,128)(2,1)}, bf16[2,512,1024]{2,1,0:T(8,128)(2,1)}, bf16[2,512,1024]{2,1,0:T(8,128)(2,1)}, f32[2,16,1024]{2,1,0:T(8,128)}) custom-call(bf16[2,512,1024]{2,1,0:T(8,128)(2,1)} %tokens.3, bf16[2,512,1024]{2,1,0:T(8,128)(2,1)} %cots.1, bf16[2,12288,1024]{2,1,0:T(8,128)(2,1)} %get-tuple-element.35.full, ...), custom_call_target="tpu_custom_call" | custom-call | tf_op jit(solution)/shard_map/pallas_call | solution.py:1398
  415.6 12.0 %shard_map.196 = (bf16[2,512,1024]{2,1,0:T(8,128)(2,1)}, bf16[2,512,1024]{2,1,0:T(8,128)(2,1)}, f32[3,1024,256]{2,1,0:T(8,128)}, f32[256,1024]{1,0:T(8,128)}, f3...) custom-call(bf16[12,256,1024]{2,1,0:T(8,128)(2,1)} %bitcast.19, ...), custom_call_target="tpu_custom_call" | custom-call | tf_op jit(solution)/shard_map/pallas_call | solution.py:1493

commit v9 on v8

--- a/solution.py
+++ b/solution.py
@@ -929,8 +929,8 @@
                 for k in range(3 * t + 3, 3 * t + 6):
                     init_start(k)
 
+        run_late(stage_d, 3)
         run(compute, 4)
-        run_late(stage_d, 3)
         return carry
 
     lax.fori_loop(0, 2 * TRIPLES + 6, step, 0)

time: 429 us -> 428 us (level)
  no operation moved by 1% of the time
where the time goes in v9:
time: 428 us; the launch traced here: 427 us
  Pallas kernels  427 us (100%)
    pallas_call x1, Pallas kernels, backward_reduce(): pl.pallas_call(functools.partial(backward_reduce_kernel, dim), out_shape=...  249 us
    pallas_call x1, Pallas kernels, gather_forward(): pl.pallas_call(functools.partial(gather_forward_kernel, dim), out_shape=(...  166 us
    pallas_call x1, Pallas kernels, finish(): pl.pallas_call(finish_kernel, out_shape=[S(acts.shape, bf), S(grads.shape...  12 us

profile of v9, /device:TPU:0, one launch (start us, length us, event | category | flops | bytes accessed | tf_op | source)
XLA Modules:
  0.0 427.4 jit_solution(9695421777027689332)
XLA Ops:
  0.6 165.8 %shard_map.194 = (bf16[2,12288,1024]{2,1,0:T(8,128)(2,1)}, f32[2,4,8,256]{3,2,1,0:T(8,128)}, f32[2,8,1024]{2,1,0:T(8,128)}, bf16[2,4,4,512,256]{4,3,2,1,0:T(8,12...) custom-call(bf16[2,512,1024]{2,1,0:T(8,128)(2,1)} %tokens.3, ...), custom_call_target="tpu_custom_call" | custom-call | tf_op jit(solution)/shard_map/pallas_call | solution.py:955
  166.5 248.8 %shard_map.195 = (bf16[12,2,2,64,1024]{4,3,2,1,0:T(8,128)(2,1)}, bf16[2,512,1024]{2,1,0:T(8,128)(2,1)}, bf16[2,512,1024]{2,1,0:T(8,128)(2,1)}, f32[2,16,1024]{2,1,0:T(8,128)}) custom-call(bf16[2,512,1024]{2,1,0:T(8,128)(2,1)} %tokens.3, bf16[2,512,1024]{2,1,0:T(8,128)(2,1)} %cots.1, bf16[2,12288,1024]{2,1,0:T(8,128)(2,1)} %get-tuple-element.35.full, ...), custom_call_target="tpu_custom_call" | custom-call | tf_op jit(solution)/shard_map/pallas_call | solution.py:1398
  415.3 12.0 %shard_map.196 = (bf16[2,512,1024]{2,1,0:T(8,128)(2,1)}, bf16[2,512,1024]{2,1,0:T(8,128)(2,1)}, f32[3,1024,256]{2,1,0:T(8,128)}, f32[256,1024]{1,0:T(8,128)}, f3...) custom-call(bf16[12,256,1024]{2,1,0:T(8,128)(2,1)} %bitcast.19, ...), custom_call_target="tpu_custom_call" | custom-call | tf_op jit(solution)/shard_map/pallas_call | solution.py:1493
